TPU v7x, 32 devices: a whole 2x2x4 slice. The times are simulated.
32 devices in a mesh: row: 4 (over x, core), col: 8 (over z, y).
Axes of the slice: x: 2, y: 2, z: 4, core: 2. Of those that a mesh axis runs over, the one named last changes fastest.
Arguments:
- features: bfloat16 [8192, 512], P('col', 'row'), may hold values from -6 to 6
- weight: bfloat16 [512, 512], replicated, may hold values from -0.25 to 0.25
- bias: float32 [512], replicated, may hold values from -3 to 3
- edge_src: int32 [64, 4096], P('row', 'col'), may hold values from 0 to 1023
- edge_dst: int32 [64, 4096], P('row', 'col'), may hold values from 0 to 127
- tile_count: int32 [64, 8], P('row', 'col'), may hold values from 0 to 512, as said below
Outputs:
- layer_out: bfloat16 [8192, 512], P(('row', 'col'))
Inputs may be any that keep to these rules, and one draw needn't show every extreme that they name: `tile_count`: entries of a tile past its count are padding and carry no edge. Some tile holds exactly 512 live edges from one sending block in every draw.
All inputs are finite; a program needn't handle non-finite values.
Results may differ from a plain program's by a relative error of at most 0.0034.
Values may be sent and summed in bfloat16 or wider, within the bound.
No kernel may reach another device: no remote copies, remote signals or barrier semaphores. Data moves between devices by JAX's collectives and lax.ppermute only.
A program may use at most 128 MiB of HBM per device.

v0:
```python
import math

import jax
import jax.numpy as jnp
from jax import lax
from jax.sharding import PartitionSpec as P

TILE = 128


def live_mask_of(counts, slot_cap):
    slot_index = lax.broadcasted_iota(jnp.int32, (counts.shape[0], slot_cap), 1)
    return (slot_index < counts).astype(jnp.float32)


def tile_sums(source, target, weights, table):
    picked = jnp.take(table, source.reshape(-1), axis=0)
    picked = picked.reshape(source.shape[0], source.shape[1], table.shape[1])
    places = lax.broadcasted_iota(jnp.int32, (1, TILE, 1), 1)
    onehot = ((target[:, None, :] == places) * weights[:, None, :]).astype(jnp.bfloat16)
    sums = jnp.einsum("gts,gsf->gtf", onehot, picked, preferred_element_type=jnp.float32)
    counts = jnp.sum(onehot, axis=2, dtype=jnp.float32)
    return (sums, counts)


def source_counts(edge_src, live_mask, source_rows):
    tiles_dev, slot_cap = edge_src.shape
    group_size = math.gcd(tiles_dev, 4)
    group_shape = (tiles_dev // group_size, group_size * slot_cap)
    node_ids = lax.broadcasted_iota(jnp.int32, (1, source_rows), 1)

    def group_count(packed):
        sources, weights = packed
        onehot = (sources[:, None] == node_ids).astype(jnp.bfloat16)
        return jnp.dot(
            weights[None, :].astype(jnp.bfloat16), onehot, preferred_element_type=jnp.float32
        )[0]

    partial_counts = lax.map(
        group_count, (edge_src.reshape(group_shape), live_mask.reshape(group_shape))
    )
    return jnp.sum(partial_counts, axis=0)


def body(features, weight, bias, edge_src, edge_dst, tile_count):
    tiles_dev, slot_cap = edge_src.shape
    source_rows = features.shape[0]
    live_mask = live_mask_of(tile_count, slot_cap)
    out_local = source_counts(edge_src, live_mask, source_rows)
    out_degree = lax.psum(out_local, "row")
    scaled = (features.astype(jnp.float32) * lax.rsqrt(1.0 + out_degree)[:, None]).astype(
        jnp.bfloat16
    )
    panel_rows = lax.all_gather(scaled, "row", axis=1, tiled=True)
    group_size = math.gcd(tiles_dev, 4)

    def group_step(packed):
        return tile_sums(packed[0], packed[1], packed[2], panel_rows)

    group_shape = (tiles_dev // group_size, group_size, slot_cap)
    partial_rows, in_local = lax.map(
        group_step,
        (
            edge_src.reshape(group_shape),
            edge_dst.reshape(group_shape),
            live_mask.reshape(group_shape),
        ),
    )
    partial_rows = partial_rows.reshape(tiles_dev * TILE, panel_rows.shape[1])
    in_local = in_local.reshape(tiles_dev * TILE)
    aggregate, in_degree = (
        lax.psum_scatter(partial_rows, "col", scatter_dimension=0, tiled=True),
        lax.psum_scatter(in_local, "col", scatter_dimension=0, tiled=True),
    )
    normed = (aggregate * lax.rsqrt(1.0 + in_degree)[:, None]).astype(jnp.bfloat16)
    projected = jnp.dot(normed, weight, preferred_element_type=jnp.float32) + bias
    return jax.nn.relu(projected).astype(jnp.bfloat16)


def solution(mesh):
    in_specs = (P("col", "row"), P(), P(), P("row", "col"), P("row", "col"), P("row", "col"))
    out_specs = P(("row", "col"), None)
    return jax.shard_map(body, mesh=mesh, in_specs=in_specs, out_specs=out_specs, check_vma=False)
```

profile of v0, /device:TPU:0, one launch (start us, length us, event | category | flops | bytes accessed | tf_op | source)
XLA Modules:
  0.0 184.0 jit_solution(14358103083494257773)
XLA Ops:
  6.5 0.0 copy-start
  6.5 0.0 all-gather.2.cloned.1.call-start
  6.5 0.5 broadcast.55
  7.1 1.3 reduce.3
  8.4 0.1 lt.44
  8.5 0.1 broadcast_bitcast_fusion
  8.6 0.8 reshape.89
  9.4 0.0 copy-start.1
  9.4 0.0 copy-start.2
  9.4 0.0 copy-start.3
  9.4 6.6 %while.24 = (s32[]{:T(128)}, f32[4,1024]{1,0:T(4,128)S(1)}, bf16[4,2048]{1,0:T(4,128)(2,1)S(1)}, s32[4,2048]{1,0:T(4,128)S(1)}, s32[]{:T(128)}, /*index=5*/s32[]{:T(128)}) while((s32[]{:T(128)}, f32[4,1024]{1,0:T(4,128)S(1)}, bf16[4,2048]{1,0:T(4,128)(2,1)S(1)}, s32[4,2048]{1,0:T(4,128)S(1)}, s32[]{:T(128)}, ...), condition=%wide.region_1.2_spmd.clone, body=%wide.region_0.1_spmd.clone.sunk | while | flops 6291458 | bytes 45137 | solution.py:39
  9.4 1.6 fusion.36
  11.0 0.1 dynamic_update_slice.20
  11.1 1.6 fusion.36
  12.7 0.1 dynamic_update_slice.20
  12.8 1.6 fusion.36
  14.3 0.1 dynamic_update_slice.20
  14.4 1.6 fusion.36
  16.0 0.1 dynamic_update_slice.20
  16.1 8.3 %psum.7 = f32[1024]{0:T(1024)S(1)} all-reduce(f32[1024]{0:T(1024)S(1)} %reduce_sum.18), channel_id=1, replica_groups=mesh['row'=4,'col'=8] {'row'}, use_global_device_ids=true, to_apply=%region_3.4 | all-reduce | flops 1024 | bytes 8192 | tf_op jit(solution)/shard_map/psum | solution.py:50
  24.4 0.9 multiply_convert_fusion.1
  25.3 0.0 all-gather.2.cloned.1.call-update
  25.4 0.0 reduce-scatter.2.cloned.1.call-start
  25.5 0.1 fusion.26
  25.6 17.1 %all-gather.2.cloned.1.call-done = bf16[1024,512]{1,0:T(8,128)(2,1)} async-done(((bf16[1024,128]{1,0:T(8,128)(2,1)}), bf16[1024,512]{1,0:T(8,128)(2,1)}) %all-gather.2.cloned.1.call-update) | async-done | bytes 1048592 | tf_op jit(solution)/shard_map/all_gather | solution.py:54
  42.7 43.7 %while.23 = (s32[]{:T(128)}, f32[4,4,128,512]{3,2,1,0:T(8,128)}, f32[4,4,128]{2,1,0:T(4,128)S(1)}, s32[4,4,512]{2,1,0:T(4,128)S(1)}, bf16[4,4,512]{2,1,0:T(4,128...) while((s32[]{:T(128)}, f32[4,4,128,512]{3,2,1,0:T(8,128)}, ...), condition=%wide.region_6.7_spmd, body=%wide.region_4.6_spmd.sunk | while | flops 271076864 | bytes 7481961 | solution.py:61
  42.7 9.0 %gather_fusion = bf16[2048,512]{1,0:T(8,128)(2,1)S(1)} fusion(bf16[1024,512]{1,0:T(8,128)(2,1)} %get-tuple-element.213, s32[2048]{0:T(1024)S(1)} %broadcast_clamp_fusion.2), kind=kCustom, calls=%fused_computation.clone.1 | custom fusion | bytes 4202496 | tf_op jit(solution)/shard_map/while/body/eval_jaxpr/jit(_take)/gather | solution.py:17
  51.7 1.6 fusion.34
  53.4 0.2 convert_reduce_fusion.2
  53.7 9.0 %gather_fusion = bf16[2048,512]{1,0:T(8,128)(2,1)S(1)} fusion(bf16[1024,512]{1,0:T(8,128)(2,1)} %get-tuple-element.213, s32[2048]{0:T(1024)S(1)} %broadcast_clamp_fusion.2), kind=kCustom, calls=%fused_computation.clone.1 | custom fusion | bytes 4202496 | tf_op jit(solution)/shard_map/while/body/eval_jaxpr/jit(_take)/gather | solution.py:17
  62.7 1.6 fusion.34
  64.3 0.2 convert_reduce_fusion.2
  64.6 9.0 %gather_fusion = bf16[2048,512]{1,0:T(8,128)(2,1)S(1)} fusion(bf16[1024,512]{1,0:T(8,128)(2,1)} %get-tuple-element.213, s32[2048]{0:T(1024)S(1)} %broadcast_clamp_fusion.2), kind=kCustom, calls=%fused_computation.clone.1 | custom fusion | bytes 4202496 | tf_op jit(solution)/shard_map/while/body/eval_jaxpr/jit(_take)/gather | solution.py:17
  73.6 1.6 fusion.34
  75.2 0.2 convert_reduce_fusion.2
  75.5 9.0 %gather_fusion = bf16[2048,512]{1,0:T(8,128)(2,1)S(1)} fusion(bf16[1024,512]{1,0:T(8,128)(2,1)} %get-tuple-element.213, s32[2048]{0:T(1024)S(1)} %broadcast_clamp_fusion.2), kind=kCustom, calls=%fused_computation.clone.1 | custom fusion | bytes 4202496 | tf_op jit(solution)/shard_map/while/body/eval_jaxpr/jit(_take)/gather | solution.py:17
  84.5 1.6 fusion.34
  86.2 0.2 convert_reduce_fusion.2
  86.4 0.0 copy-start.5
  86.4 0.0 copy-start.4
  86.4 0.0 reduce-scatter.2.cloned.1.call-update
  86.4 0.6 copy-done.5
  87.0 0.6 dynamic-slice
  88.3 22.6 %all-reduce = f32[2048]{0:T(1024)S(1)} all-reduce(f32[2048]{0:T(1024)S(1)} %bitcast.65), channel_id=3, replica_groups=mesh['row'=4,'col'=8] {'col'}, use_global_device_ids=true, to_apply=%region_8.9.clone | all-reduce | flops 2048 | bytes 16384
  110.9 0.1 fusion.27
  111.0 64.1 %reduce-scatter.2.cloned.1.call-done = f32[256,512]{1,0:T(8,128)} async-done(((f32[2048,512]{1,0:T(8,128)}), f32[256,512]{1,0:T(8,128)}) %reduce-scatter.2.cloned.1.call-update) | async-done | bytes 524304 | tf_op jit(solution)/shard_map/reduce_scatter | solution.py:72
  175.0 0.0 copy-done
  175.0 2.1 %fusion.24 = bf16[256,512]{1,0:T(8,128)(2,1)} fusion(bf16[512,512]{1,0:T(8,128)(2,1)S(1)} %copy-done, f32[256,512]{1,0:T(8,128)} %reduce-scatter.2.cloned.1.call-done, f32[512]{0:T(512)S(1)} %copy-done.4, f32[256]{0:T(256)S(1)} %fusion.27), kind=kOutput, calls=%fused_computation.34 | convolution fusion | flops 134873088 | bytes 1313792 | tf_op jit(solution)/shard_map/dot_general | solution.py:76
  (51 shorter events, 0.5 us)
Async XLA Ops:
  6.5 168.5 %copy-start = (bf16[512,512]{1,0:T(8,128)(2,1)S(1)}, bf16[512,512]{1,0:T(8,128)(2,1)}, u32[]{:S(2)}) copy-start(bf16[512,512]{1,0:T(8,128)(2,1)} %param.11) | copy-start | bytes 1572868
  6.5 36.1 %all-gather.2.cloned.1.call-start = ((), (), s32[]{:S(2)}) async-start(), calls=%async_computation.1 | async-start | bytes 1310720 | tf_op jit(solution)/shard_map/all_gather | solution.py:54
  9.4 15.0 %copy-start.1 = (bf16[1024,128]{1,0:T(8,128)(2,1)S(1)}, bf16[1024,128]{1,0:T(8,128)(2,1)}, u32[]{:S(2)}) copy-start(bf16[1024,128]{1,0:T(8,128)(2,1)} %param.10) | copy-start | bytes 786436
  9.4 16.0 %copy-start.2 = (s32[16,512]{1,0:T(8,128)S(1)}, s32[16,512]{1,0:T(8,128)}, u32[]{:S(2)}) copy-start(s32[16,512]{1,0:T(8,128)} %param.13) | copy-start | bytes 98308
  9.4 16.1 %copy-start.3 = (s32[16,512]{1,0:T(8,128)S(1)}, s32[16,512]{1,0:T(8,128)}, u32[]{:S(2)}) copy-start(s32[16,512]{1,0:T(8,128)} %param.14) | copy-start | bytes 98308
  25.4 149.7 %reduce-scatter.2.cloned.1.call-start = ((), (), s32[]{:S(2)}) async-start(), calls=%async_computation.2 | async-start | bytes 4718592 | tf_op jit(solution)/shard_map/reduce_scatter | solution.py:72
  86.4 0.7 copy-start.5
  86.4 88.7 %copy-start.4 = (f32[512]{0:T(512)S(1)}, f32[512]{0:T(512)}, u32[]{:S(2)}) copy-start(f32[512]{0:T(512)} %param.12) | copy-start | bytes 6148
Sparse Core Ops, SparseCore 0:
  25.5 17.1 all-gather.1
  86.5 88.4 reduce-scatter.1
where the time goes:
time: 184 us
  waiting for transfers between devices  81.2 us (44%)
  local copies, waits for them, and re-layouts  39 us (21%)
  blocking collectives  31 us (17%)
  matrix products  14.9 us (8%)
  between operations  14.2 us (8%)
  other arithmetic  3.28 us (2%)
    reduce_scatter x1, waiting for transfers between devices, body(): lax.psum_scatter(partial_rows, 'col', scatter_dimension=0, tiled=True)  64.1 us
    gather x4, local copies, waits for them, and re-layouts, tile_sums(): picked = jnp.take(table, source.reshape(-1), axis=0)  35.8 us
    unnamed x1, blocking collectives  22.6 us
    all_gather x1, waiting for transfers between devices, body(): panel_rows = lax.all_gather(scaled, 'row', axis=1, tiled=True)  17.1 us
    psum x1, blocking collectives, body(): out_degree = lax.psum(out_local, 'row')  8.35 us
    dot_general x4, matrix products, tile_sums(): jnp.einsum('gts,gsf->gtf', onehot, picked, preferred_element_type=jnp.flo...  6.54 us
    dot_general x4, matrix products, group_count(): jnp.dot(weights[None, :].astype(jnp.bfloat16), onehot, preferred_element_...  6.23 us
  transfers between devices with their start and end apart: 2, of which 2 were waited for; matrix products, arithmetic and copies ran while one was open for 0% of the time, Pallas kernels for 0%

commit v1 on v0

v1 whole, which is shorter than its diff:
```python
import functools

import jax
import jax.numpy as jnp
from jax import lax
from jax.experimental import pallas as pl
from jax.experimental.pallas import tpu as pltpu
from jax.sharding import PartitionSpec as P

TILE = 128
LANES = 128
LOW = 256
NT = (((1,), (1,)), ((), ()))
BITS8 = jnp.float8_e4m3fn


def flag(condition):
    return jnp.where(condition, 1.0, 0.0).astype(jnp.bfloat16)


def short(whole):
    return whole.astype(jnp.float32).astype(jnp.bfloat16)


def equal(ids, whole):
    return jnp.where(ids == short(whole), jnp.bfloat16(1), jnp.bfloat16(0))


def pack_kernel(src_ref, dst_ref, count_ref, out_ref, lines):
    tiles, cap = src_ref.shape
    rows, cols, depth, _ = out_ref.shape
    subs = cap // LANES
    own = tiles // cols * subs // 2
    high = 2 * (depth - own)
    src = src_ref[...]
    tile_ids = lax.broadcasted_iota(jnp.int32, (tiles, cap), 0)
    count = jnp.zeros((tiles, cap), jnp.int32)
    for t in range(tiles):
        count = jnp.where(tile_ids == t, count_ref[t], count)
    live = lax.broadcasted_iota(jnp.int32, (tiles, cap), 1) < count
    packed = src + jnp.where(live, dst_ref[...], TILE) * 65536
    for j in range(subs):
        lines[pl.ds(j, tiles, stride=subs), :] = packed[:, j * LANES : (j + 1) * LANES]
    edges = lines[...].reshape(cols, 2 * own, LANES)
    for r in range(rows):
        first = r % 2 * own
        out_ref[r, :, :own, :] = edges[:, first : first + own, :]
    src_high = jnp.where(live, src // LANES, high)
    src_low = src % LANES
    high_ids = lax.broadcasted_iota(jnp.int32, (high, cap), 0)
    low_ids = lax.broadcasted_iota(jnp.int32, (LANES, cap), 0)
    total = jnp.zeros((high, LANES), jnp.float32)
    for t in range(tiles):
        total += lax.dot_general(
            flag(high_ids == src_high[t : t + 1]),
            flag(low_ids == src_low[t : t + 1]),
            NT,
            preferred_element_type=jnp.float32,
        )
    degree = total.astype(jnp.int32)
    for r in range(rows):
        first = r % 2 * (high // 2)
        out_ref[r, :, own:, :] = jnp.broadcast_to(
            degree[first : first + high // 2], (cols, high // 2, LANES)
        )


def ring_col_of(place, cols):
    return 2 * place if place < cols // 2 else 2 * (cols - 1 - place) + 1


def ring_place(col, cols):
    return jnp.where(col % 2 == 0, col // 2, cols - 1 - col // 2)


def ring_col(place, cols):
    return jnp.where(place < cols // 2, 2 * place, 2 * (cols - 1 - place) + 1)


def sum_kernel(cols, shifts, groups, first, last, col_ref, *refs):
    row_ref, *refs = refs
    edge_refs, refs = refs[:2], refs[2:]
    xs, refs = refs[: sum(groups)], refs[sum(groups) :]
    if not first:
        old_ref, *refs = refs
    rows, _, depth, _ = edge_refs[0].shape
    out_refs, refs = refs[: rows if last else 1], refs[rows if last else 1 :]
    counts, scaled, *refs = refs
    total = refs[0] if last else out_refs[0]
    width = xs[0].shape[1]
    _, sums, src_rows = counts.shape
    highs = src_rows // LOW
    own = depth - src_rows // LANES // 2
    tiles = sums // rows // TILE // 2
    subs = own // tiles
    odd = lax.rem(row_ref[0], 2)
    place = ring_place(col_ref[0], cols)
    blocks = [ring_col(lax.rem(place + shift + cols, cols), cols) for shift in shifts]
    diagonal = lax.broadcasted_iota(jnp.int32, (LANES, LANES), 0) == lax.broadcasted_iota(
        jnp.int32, (LANES, LANES), 1
    )
    target_ids = short(lax.broadcasted_iota(jnp.int32, (TILE, LANES), 0))
    low_ids = short(lax.broadcasted_iota(jnp.int32, (LOW, LANES), 0))

    def put_scaled(g):
        halves = [
            sum(edge_ref[r, blocks[g], own:, :] for r in range(rows)).astype(jnp.float32)
            for edge_ref in edge_refs
        ]
        degree = jnp.where(odd == 0, jnp.concatenate(halves), jnp.concatenate(halves[::-1]))
        scale = lax.rsqrt(1.0 + degree)
        top = 0
        for x_ref in xs[sum(groups[:g]) : sum(groups[: g + 1])]:
            for i in range(x_ref.shape[0] // LANES):
                row = scale[top // LANES : top // LANES + 1]
                column = jnp.sum(jnp.where(diagonal, row, 0.0), axis=1, keepdims=True)
                x = x_ref[i * LANES : (i + 1) * LANES, :].astype(jnp.float32)
                scaled[g % 2, top : top + LANES, :width] = (x * column).astype(jnp.bfloat16)
                top += LANES

    def count_block(g, edge_ref, r, t):
        lefts, rights = [], []
        for j in range(subs):
            edges = edge_ref[r, blocks[g], pl.ds(t * subs + j, 1), :]
            src = edges & 65535
            target_one = equal(target_ids, edges >> 16)
            src_high = src // LOW
            left = [target_one * flag(src_high == h) for h in range(highs)]
            lefts.append(jnp.concatenate(left, axis=0).astype(BITS8))
            rights.append(equal(low_ids, src % LOW).astype(BITS8))
        return lax.dot_general(
            jnp.concatenate(lefts, axis=1),
            jnp.concatenate(rights, axis=1),
            NT,
            preferred_element_type=jnp.float32,
        )

    def add_block(g, convert, unroll):
        def fill_tile(part, i, carry):
            r, t = i // tiles, i % tiles
            block = count_block(g, edge_refs[part], r, t)
            half = 1 - odd if part else odd
            top = pl.multiple_of(((2 * r + half) * tiles + t) * TILE, TILE)
            for h in range(highs):
                counts[g % 2, pl.ds(top, TILE), h * LOW : (h + 1) * LOW] = convert(
                    block[h * TILE : (h + 1) * TILE]
                )
            return carry

        put_scaled(g)
        for part in range(2):
            if unroll:
                for i in range(rows * tiles):
                    fill_tile(part, i, 0)
            else:
                lax.fori_loop(0, rows * tiles, functools.partial(fill_tile, part), 0)
        total[...] += jnp.dot(counts[g % 2], scaled[g % 2], preferred_element_type=jnp.float32)

    scaled[...] = jnp.ones_like(scaled)
    total[...] = jnp.zeros_like(total) if first else old_ref[...]
    for g in range(len(groups)):
        add_block(g, lambda block: block.astype(jnp.bfloat16), rows * tiles <= 4)

    @pl.when(jnp.max(total[:, LANES:]) >= 256.0)
    def _():
        for g in range(len(groups)):
            add_block(
                g,
                lambda block: (block - block.astype(jnp.bfloat16).astype(jnp.float32)).astype(jnp.bfloat16),
                False,
            )

    if last:
        for shift, out_ref in enumerate(out_refs):
            size = out_ref.shape[0]
            part = pl.ds(pl.multiple_of(lax.rem(row_ref[0] + shift, rows) * size, size), size)
            norm = lax.rsqrt(1.0 + total[part, LANES : LANES + width])
            out_ref[...] = (total[part, :width] * norm).astype(jnp.bfloat16)


def layer_kernel(row_ref, *refs):
    *x_refs, weight_ref, bias_hbm, out_ref, bias, arrived = refs
    copy = pltpu.make_async_copy(bias_hbm, bias, arrived)
    copy.start()
    rows, width = len(x_refs), x_refs[0].shape[1]
    projected = None
    for shift, x_ref in enumerate(x_refs):
        top = pl.multiple_of(lax.rem(row_ref[0] - shift + rows, rows) * width, width)
        part = jnp.dot(x_ref[...], weight_ref[pl.ds(top, width), :], preferred_element_type=jnp.float32)
        projected = part if projected is None else projected + part
    copy.wait()
    out_ref[...] = jnp.maximum(projected + bias[...], 0.0).astype(jnp.bfloat16)


def body(rows, cols, features, weight, bias, edge_src, edge_dst, tile_count):
    tiles, cap = edge_src.shape
    src_rows, width = features.shape
    hidden = weight.shape[1]
    degree_rows = src_rows // LANES
    own_rows = tiles * cap // LANES // cols
    own_nodes = tiles // cols * TILE
    sums = rows * own_nodes
    order = [ring_col_of(place, cols) for place in range(cols)]
    ahead = [(order[p], order[(p + 1) % cols]) for p in range(cols)]
    back = [(order[(p + 1) % cols], order[p]) for p in range(cols)]
    half = src_rows // 2

    depth = (own_rows + degree_rows) // 2
    packed = pl.pallas_call(
        pack_kernel,
        in_specs=[pl.BlockSpec(), pl.BlockSpec(), pl.BlockSpec(memory_space=pltpu.SMEM)],
        out_shape=jax.ShapeDtypeStruct((rows, cols, depth, LANES), jnp.int32),
        scratch_shapes=[pltpu.VMEM((cols * own_rows, LANES), jnp.int32)],
    )(edge_src, edge_dst, tile_count.reshape(tiles))
    edges = lax.all_to_all(
        packed.reshape(rows * cols, depth, LANES),
        ("row", "col"),
        split_axis=0,
        concat_axis=0,
        tiled=True,
    )
    other = lax.ppermute(edges, "row", [(r, r + 1 - 2 * (r % 2)) for r in range(rows)])
    edges = [half.reshape(rows, cols, depth, LANES) for half in (edges, other)]
    col = lax.axis_index("col").astype(jnp.int32).reshape(1)
    row = lax.axis_index("row").astype(jnp.int32).reshape(1)

    def add_blocks(total, blocks, last, flops):
        first = total is None
        shifts = [shift for shift, _ in blocks]
        groups = [len(pieces) for _, pieces in blocks]
        pieces = [piece for _, listed in blocks for piece in listed]

        whole = lambda array: pl.BlockSpec(array.shape, lambda i, c, r: (0,) * array.ndim)
        operands = pieces + ([] if first else [total])
        out_shape = (
            [jax.ShapeDtypeStruct((own_nodes, width), jnp.bfloat16)] * rows
            if last
            else [jax.ShapeDtypeStruct((sums, 2 * LANES), jnp.float32)]
        )
        scratch = [
            pltpu.VMEM((2, sums, src_rows), jnp.bfloat16),
            pltpu.VMEM((2, src_rows, 2 * LANES), jnp.bfloat16),
        ]
        if last:
            scratch.append(pltpu.VMEM((sums, 2 * LANES), jnp.float32))
        return pl.pallas_call(
            functools.partial(sum_kernel, cols, shifts, groups, first, last),
            grid_spec=pltpu.PrefetchScalarGridSpec(
                num_scalar_prefetch=2,
                grid=(1,),
                in_specs=[whole(operand) for operand in edges + operands],
                out_specs=[whole(array) for array in out_shape],
                scratch_shapes=scratch,
            ),
            out_shape=out_shape,
            compiler_params=pltpu.CompilerParams(vmem_limit_bytes=48 * 1024 * 1024),
            cost_estimate=pl.CostEstimate(flops=flops, bytes_accessed=2**22, transcendentals=0),
        )(col, row, *edges, *operands)

    block_flops = 2 * sums * src_rows * (2 * LANES + cap)
    ups = downs = features
    total, waiting = None, [(0, [features])]
    for hop in range(1, cols // 2):
        ups = lax.ppermute(ups, "col", ahead)
        downs = lax.ppermute(downs, "col", back)
        waiting += [(-hop, [ups]), (hop, [downs])]
        if hop > 1:
            (total,) = add_blocks(total, waiting, False, 2 * len(waiting) * block_flops)
            waiting = []
    ups = lax.ppermute(ups[:half], "col", ahead)
    downs = lax.ppermute(downs[half:], "col", back)
    waiting.append((cols // 2, [ups, downs]))
    normed = list(add_blocks(total, waiting, True, block_flops))
    for shift in range(1, rows):
        pairs = [(r, (r + shift) % rows) for r in range(rows)]
        normed[shift] = lax.ppermute(normed[shift], "row", pairs)
    operands = [*normed, weight]
    return pl.pallas_call(
        layer_kernel,
        grid_spec=pltpu.PrefetchScalarGridSpec(
            num_scalar_prefetch=1,
            grid=(1,),
            in_specs=[pl.BlockSpec(array.shape, lambda i, r: (0, 0)) for array in operands]
            + [pl.BlockSpec(memory_space=pl.ANY)],
            out_specs=pl.BlockSpec((own_nodes, hidden), lambda i, r: (0, 0)),
            scratch_shapes=[pltpu.VMEM((1, hidden), jnp.float32), pltpu.SemaphoreType.DMA],
        ),
        out_shape=jax.ShapeDtypeStruct((own_nodes, hidden), jnp.bfloat16),
        compiler_params=pltpu.CompilerParams(vmem_limit_bytes=8 * 1024 * 1024),
    )(row, *operands, bias.reshape(1, hidden))


def solution(mesh):
    rows, cols = mesh.shape["row"], mesh.shape["col"]
    in_specs = (P("col", "row"), P(), P(), P("row", "col"), P("row", "col"), P("row", "col"))
    out_specs = P(("row", "col"), None)
    return jax.shard_map(
        functools.partial(body, rows, cols),
        mesh=mesh,
        in_specs=in_specs,
        out_specs=out_specs,
        check_vma=False,
    )
```

time: 184 us -> 48.5 us (0.26)
  waiting for transfers between devices: 81.2 us -> 11.6 us
  local copies, waits for them, and re-layouts: 39 us -> 0.03 us
  blocking collectives: 31 us -> 0 us
  Pallas kernels: 0 us -> 18.6 us
  starting transfers between devices: 0.04 us -> 17.9 us
  matrix products: 14.9 us -> 0 us
  between operations: 14.2 us -> 0.28 us
  other arithmetic: 3.28 us -> 0 us
    reduce_scatter x1 -> x0, waiting for transfers between devices: 64.1 us -> none  [body(): lax.psum_scatter(partial_rows, 'col', scatter_dimension=0, tiled=True)]
    gather x4 -> x0, local copies, waits for them, and re-layouts: 35.8 us -> none  [tile_sums(): picked = jnp.take(table, source.reshape(-1), axis=0)]
    unnamed x1 -> x0, blocking collectives: 22.6 us -> none
    pallas_call x0 -> x5, Pallas kernels: none -> 18.6 us  [the longest x3 15.3 us: add_blocks(): pl.pallas_call(functools.partial(sum_kernel, cols, shifts, groups, first,...]
    all_gather x1 -> x0, waiting for transfers between devices: 17.1 us -> none  [body(): panel_rows = lax.all_gather(scaled, 'row', axis=1, tiled=True)]
    dot_general x9 -> x0, matrix products: 14.9 us -> none  [the longest x4 6.54 us: tile_sums(): jnp.einsum('gts,gsf->gtf', onehot, picked, preferred_element_type=jnp.flo...]
    ppermute x0 -> x12, starting transfers between devices: none -> 11.6 us  [the longest x3 5.87 us: body(): ups = lax.ppermute(ups, 'col', ahead)]
    psum x1 -> x0, blocking collectives: 8.35 us -> none  [body(): out_degree = lax.psum(out_local, 'row')]
  transfers between devices with their start and end apart: 2 -> 13, of which waited for: 2 -> 6; matrix products, arithmetic and copies ran while one was open for 0% -> 0% of each run, Pallas kernels for 0% -> 32%
where the time goes in v1:
time: 48.5 us; the launch traced here: 48.3 us
  Pallas kernels  18.6 us (38%)
  starting transfers between devices  17.9 us (37%)
  waiting for transfers between devices  11.6 us (24%)
    pallas_call x3, Pallas kernels, add_blocks(): pl.pallas_call(functools.partial(sum_kernel, cols, shifts, groups, first,...  15.3 us
    all_to_all x1, starting transfers between devices, body(): lax.all_to_all(packed.reshape(rows * cols, depth, LANES), ('row', 'col'),...  6.3 us
    ppermute x3, starting transfers between devices, body(): ups = lax.ppermute(ups, 'col', ahead)  5.87 us
    all_to_all x1, waiting for transfers between devices, body(): lax.all_to_all(packed.reshape(rows * cols, depth, LANES), ('row', 'col'),...  5.65 us
    ppermute x3, waiting for transfers between devices, body(): normed[shift] = lax.ppermute(normed[shift], 'row', pairs)  3.68 us
    pallas_call x1, Pallas kernels, body(): pl.pallas_call(pack_kernel, in_specs=[pl.BlockSpec(), pl.BlockSpec(), pl....  2.14 us
    ppermute x3, waiting for transfers between devices, body(): ups = lax.ppermute(ups, 'col', ahead)  2.07 us
    ppermute x3, starting transfers between devices, body(): normed[shift] = lax.ppermute(normed[shift], 'row', pairs)  2.05 us
  transfers between devices with their start and end apart: 13, of which 6 were waited for; matrix products, arithmetic and copies ran while one was open for 0% of the time, Pallas kernels for 32%

profile of v1, /device:TPU:0, one launch (start us, length us, event | category | flops | bytes accessed | tf_op | source)
XLA Modules:
  0.0 48.3 jit_solution(11230686807301064778)
XLA Ops:
  0.0 0.0 copy-start.2
  0.0 3.0 %collective-permute-start.1 = (bf16[1024,128]{1,0:T(8,128)(2,1)}, bf16[1024,128]{1,0:T(8,128)(2,1)S(1)}, u32[]{:S(2)}, u32[]{:S(2)}) collective-permute-start(bf16[1024,128]{1,0:T(8,128)(2,1)} %refs_3_.1), channel_id=1, source_target_pairs={{0,2},{2,4},{4,6},{6,7},{7,5},{5,3},{3,1},{1,0},{8,10},{10,12},{12... | collective-permute-start | bytes 786440 | tf_op jit(solution)/shard_map/ppermute | solution.py:264
  3.0 0.0 collective-permute-start.5
  3.0 2.1 %shard_map.64 = s32[4,8,8,128]{3,2,1,0:T(8,128)} custom-call(s32[16,512]{1,0:T(8,128)} %src_ref.1, s32[16,512]{1,0:T(8,128)} %dst_ref.1, s32[16]{0:T(128)} %bitcast.15), custom_call_target="tpu_custom_call" | custom-call | tf_op jit(solution)/shard_map/pallas_call | solution.py:209
  5.2 6.3 %all-to-all-start = ((s32[32,8,128]{2,1,0:T(8,128)}), s32[32,8,128]{2,1,0:T(8,128)S(1)}, u32[]{:S(2)}, u32[]{:S(2)}) async-start(s32[32,8,128]{2,1,0:T(8,128)} %bitcast.14), calls=%async_computation | async-start | bytes 262144 | tf_op jit(solution)/shard_map/all_to_all | solution.py:215
  11.5 0.0 collective-permute-done.1.refs_4_
  11.5 1.8 %collective-permute-start.2 = (bf16[1024,128]{1,0:T(8,128)(2,1)S(1)}, bf16[1024,128]{1,0:T(8,128)(2,1)S(1)}, u32[]{:S(2)}, u32[]{:S(2)}) collective-permute-start(bf16[1024,128]{1,0:T(8,128)(2,1)S(1)} %collective-permute-done.1.refs_4_), channel_id=1, source_target_pairs={{0,2},{2,4},{4,6},{6,7},{7,5},{5,3},{3,1},{1,0},{8,10},{10,12},{12... | collective-permute-start | bytes 786440 | tf_op jit(solution)/shard_map/ppermute | solution.py:264
  13.3 0.0 collective-permute-done.5.refs_5_
  13.3 0.3 collective-permute-start.6
  13.6 5.7 %all-to-all-done = s32[32,8,128]{2,1,0:T(8,128)S(1)} async-done(((s32[32,8,128]{2,1,0:T(8,128)}), s32[32,8,128]{2,1,0:T(8,128)S(1)}, u32[]{:S(2)}, u32[]{:S(2)}) %all-to-all-start) | async-done | bytes 131104 | tf_op jit(solution)/shard_map/all_to_all | solution.py:215
  19.2 0.1 collective-permute-start
  19.3 2.1 %collective-permute-done.2.refs_6_ = bf16[1024,128]{1,0:T(8,128)(2,1)S(1)} collective-permute-done((bf16[1024,128]{1,0:T(8,128)(2,1)S(1)}, bf16[1024,128]{1,0:T(8,128)(2,1)S(1)}, u32[]{:S(2)}, u32[]{:S(2)}) %collective-permute-start.2) | collective-permute-done | bytes 262176 | tf_op jit(solution)/shard_map/ppermute | solution.py:264
  21.4 1.0 %collective-permute-start.3 = (bf16[1024,128]{1,0:T(8,128)(2,1)S(1)}, bf16[1024,128]{1,0:T(8,128)(2,1)S(1)}, u32[]{:S(2)}, u32[]{:S(2)}) collective-permute-start(bf16[1024,128]{1,0:T(8,128)(2,1)S(1)} %collective-permute-done.2.refs_6_), channel_id=1, source_target_pairs={{0,2},{2,4},{4,6},{6,7},{7,5},{5,3},{3,1},{1,0},{8,10},{10,12},{12... | collective-permute-start | bytes 786440 | tf_op jit(solution)/shard_map/ppermute | solution.py:264
  22.4 0.1 collective-permute-done.6.refs_7_
  22.6 1.0 %collective-permute-start.7 = (bf16[1024,128]{1,0:T(8,128)(2,1)S(1)}, bf16[1024,128]{1,0:T(8,128)(2,1)S(1)}, u32[]{:S(2)}, u32[]{:S(2)}) collective-permute-start(bf16[1024,128]{1,0:T(8,128)(2,1)S(1)} %collective-permute-done.6.refs_7_), channel_id=1, source_target_pairs={{2,0},{4,2},{6,4},{7,6},{5,7},{3,5},{1,3},{0,1},{10,8},{12,10},{14... | collective-permute-start | bytes 786440 | tf_op jit(solution)/shard_map/ppermute | solution.py:265
  23.5 0.0 collective-permute-done
  23.5 0.0 copy-done.2
  23.5 8.9 %shard_map.65.refs_5_ = f32[1024,256]{1,0:T(8,128)S(1)} custom-call(s32[1]{0:T(128)} %bitcast.1.col_ref, s32[1]{0:T(128)} %bitcast.refs_0_.row_ref, s32[4,8,8,128]{3,2,1,0:T(8,128)S(1)} %bitcast.7, s32[4,8,8,128]{3,2,1,0:T(8,128)S(1)} %bitcast.11, bf16[1024,128]{1,0:T(8,128)(2,1)S(1)} %copy-done.2, bf16[1024,128]{1,0:T(8,128)(2,1)S(1)} %collective-permute-done.1.refs_4_, ...), custom_call_target="tpu_custom_call" | custom-call | flops 16106127360 | bytes 4194304 | tf_op jit(solution)/shard_map/pallas_call | solution.py:246
  32.5 0.0 collective-permute-done.3.refs_3_
  32.5 1.2 %collective-permute-start.4 = (bf16[512,128]{1,0:T(8,128)(2,1)S(1)}, bf16[512,128]{1,0:T(8,128)(2,1)S(1)}, u32[]{:S(2)}, u32[]{:S(2)}) collective-permute-start(bf16[512,128]{1,0:T(8,128)(2,1)S(1)} %slice.8), channel_id=1, source_target_pairs={{0,2},{2,4},{4,6},{6,7},{7,5},{5,3},{3,1},{1,0},{8,10},{10,12},{12... | collective-permute-start | bytes 393224 | tf_op jit(solution)/shard_map/ppermute | solution.py:270
  33.7 0.0 collective-permute-done.7.refs_4_
  33.7 1.1 %collective-permute-start.8 = (bf16[512,128]{1,0:T(8,128)(2,1)S(1)}, bf16[512,128]{1,0:T(8,128)(2,1)S(1)}, u32[]{:S(2)}, u32[]{:S(2)}) collective-permute-start(bf16[512,128]{1,0:T(8,128)(2,1)S(1)} %slice.9), channel_id=1, source_target_pairs={{2,0},{4,2},{6,4},{7,6},{5,7},{3,5},{1,3},{0,1},{10,8},{12,10},{14... | collective-permute-start | bytes 393224 | tf_op jit(solution)/shard_map/ppermute | solution.py:271
  34.8 4.3 %shard_map.66.refs_5_ = f32[1024,256]{1,0:T(8,128)S(1)} custom-call(s32[1]{0:T(128)} %bitcast.1.col_ref, s32[1]{0:T(128)} %bitcast.refs_0_.row_ref, s32[4,8,8,128]{3,2,1,0:T(8,128)S(1)} %bitcast.8, s32[4,8,8,128]{3,2,1,0:T(8,128)S(1)} %bitcast.12, bf16[1024,128]{1,0:T(8,128)(2,1)S(1)} %collective-permute-done.3.refs_3_, ...), custom_call_target="tpu_custom_call" | custom-call | flops 6442450944 | bytes 4194304 | tf_op jit(solution)/shard_map/pallas_call | solution.py:246
  39.2 0.0 copy-start
  39.2 0.0 collective-permute-done.4.refs_3_
  39.2 0.0 collective-permute-done.8.refs_4_
  39.2 2.0 %shard_map.67 = (bf16[256,128]{1,0:T(8,128)(2,1)S(1)}, bf16[256,128]{1,0:T(8,128)(2,1)S(1)}, bf16[256,128]{1,0:T(8,128)(2,1)S(1)}, bf16[256,128]{1,0:T(8,128)(2,1)S(1)}) custom-call(s32[1]{0:T(128)} %bitcast.1.col_ref, s32[1]{0:T(128)} %bitcast.refs_0_.row_ref, s32[4,8,8,128]{3,2,1,0:T(8,128)S(1)} %bitcast.9, s32[4,8,8,128]{3,2,1,0:T(8,128)S(1)} %bitcast.13, ...), custom_call_target="tpu_custom_call" | custom-call | flops 1610612736 | bytes 4194304 | tf_op jit(solution)/shard_map/pallas_call | solution.py:246
  41.2 1.5 %collective-permute-start.10 = (bf16[256,128]{1,0:T(8,128)(2,1)S(1)}, bf16[256,128]{1,0:T(8,128)(2,1)S(1)}, u32[]{:S(2)}, u32[]{:S(2)}) collective-permute-start(bf16[256,128]{1,0:T(8,128)(2,1)S(1)} %get-tuple-element.11), channel_id=1, source_target_pairs={{0,16},{8,24},{16,0},{24,8},{1,17},{9,25},{17,1},{25,9},{2,18},{10... | collective-permute-start | bytes 196616 | tf_op jit(solution)/shard_map/ppermute | solution.py:276
  42.7 0.0 collective-permute-start.11
  42.8 0.0 copy-start.1
  42.8 0.5 %collective-permute-start.9 = (bf16[256,128]{1,0:T(8,128)(2,1)S(1)}, bf16[256,128]{1,0:T(8,128)(2,1)S(1)}, u32[]{:S(2)}, u32[]{:S(2)}) collective-permute-start(bf16[256,128]{1,0:T(8,128)(2,1)S(1)} %get-tuple-element.10), channel_id=1, source_target_pairs={{0,8},{8,16},{16,24},{24,0},{1,9},{9,17},{17,25},{25,1},{2,10},{10... | collective-permute-start | bytes 196616 | tf_op jit(solution)/shard_map/ppermute | solution.py:276
  43.3 2.3 %collective-permute-done.10.refs_2_ = bf16[256,128]{1,0:T(8,128)(2,1)S(1)} collective-permute-done((bf16[256,128]{1,0:T(8,128)(2,1)S(1)}, bf16[256,128]{1,0:T(8,128)(2,1)S(1)}, u32[]{:S(2)}, u32[]{:S(2)}) %collective-permute-start.10) | collective-permute-done | bytes 65568 | tf_op jit(solution)/shard_map/ppermute | solution.py:276
  45.5 0.4 collective-permute-done.11.refs_3_
  45.9 1.0 %collective-permute-done.9.refs_1_ = bf16[256,128]{1,0:T(8,128)(2,1)S(1)} collective-permute-done((bf16[256,128]{1,0:T(8,128)(2,1)S(1)}, bf16[256,128]{1,0:T(8,128)(2,1)S(1)}, u32[]{:S(2)}, u32[]{:S(2)}) %collective-permute-start.9) | collective-permute-done | bytes 65568 | tf_op jit(solution)/shard_map/ppermute | solution.py:276
  46.9 0.0 copy-done
  46.9 0.0 copy-done.1
  46.9 1.2 %shard_map.68 = bf16[256,512]{1,0:T(8,128)(2,1)} custom-call(s32[1]{0:T(128)} %bitcast.refs_0_.row_ref, bf16[256,128]{1,0:T(8,128)(2,1)S(1)} %get-tuple-element.9.refs_0_, bf16[256,128]{1,0:T(8,128)(2,1)S(1)} %collective-permute-done.9.refs_1_, bf16[256,128]{1,0:T(8,128)(2,1)S(1)} %collective-permute-done.10.refs_2_, ...), custom_call_target="tpu_custom_call" | custom-call | tf_op jit(solution)/shard_map/pallas_call | solution.py:278
  (2 shorter events, 0.0 us)
Async XLA Ops:
  0.0 23.5 %copy-start.2 = (bf16[1024,128]{1,0:T(8,128)(2,1)S(1)}, bf16[1024,128]{1,0:T(8,128)(2,1)}, u32[]{:S(2)}) copy-start(bf16[1024,128]{1,0:T(8,128)(2,1)} %refs_3_.1) | copy-start | bytes 786436
  0.0 11.5 %collective-permute-start.1 = (bf16[1024,128]{1,0:T(8,128)(2,1)}, bf16[1024,128]{1,0:T(8,128)(2,1)S(1)}, u32[]{:S(2)}, u32[]{:S(2)}) collective-permute-start(bf16[1024,128]{1,0:T(8,128)(2,1)} %refs_3_.1), channel_id=1, source_target_pairs={{0,2},{2,4},{4,6},{6,7},{7,5},{5,3},{3,1},{1,0},{8,10},{10,12},{12... | collective-permute-start | bytes 786440 | tf_op jit(solution)/shard_map/ppermute | solution.py:264
  3.0 10.3 %collective-permute-start.5 = (bf16[1024,128]{1,0:T(8,128)(2,1)}, bf16[1024,128]{1,0:T(8,128)(2,1)S(1)}, u32[]{:S(2)}, u32[]{:S(2)}) collective-permute-start(bf16[1024,128]{1,0:T(8,128)(2,1)} %refs_3_.1), channel_id=1, source_target_pairs={{2,0},{4,2},{6,4},{7,6},{5,7},{3,5},{1,3},{0,1},{10,8},{12,10},{14... | collective-permute-start | bytes 786440 | tf_op jit(solution)/shard_map/ppermute | solution.py:265
  5.2 14.1 %all-to-all-start = ((s32[32,8,128]{2,1,0:T(8,128)}), s32[32,8,128]{2,1,0:T(8,128)S(1)}, u32[]{:S(2)}, u32[]{:S(2)}) async-start(s32[32,8,128]{2,1,0:T(8,128)} %bitcast.14), calls=%async_computation | async-start | bytes 262144 | tf_op jit(solution)/shard_map/all_to_all | solution.py:215
  11.5 9.9 %collective-permute-start.2 = (bf16[1024,128]{1,0:T(8,128)(2,1)S(1)}, bf16[1024,128]{1,0:T(8,128)(2,1)S(1)}, u32[]{:S(2)}, u32[]{:S(2)}) collective-permute-start(bf16[1024,128]{1,0:T(8,128)(2,1)S(1)} %collective-permute-done.1.refs_4_), channel_id=1, source_target_pairs={{0,2},{2,4},{4,6},{6,7},{7,5},{5,3},{3,1},{1,0},{8,10},{10,12},{12... | collective-permute-start | bytes 786440 | tf_op jit(solution)/shard_map/ppermute | solution.py:264
  13.3 9.3 %collective-permute-start.6 = (bf16[1024,128]{1,0:T(8,128)(2,1)S(1)}, bf16[1024,128]{1,0:T(8,128)(2,1)S(1)}, u32[]{:S(2)}, u32[]{:S(2)}) collective-permute-start(bf16[1024,128]{1,0:T(8,128)(2,1)S(1)} %collective-permute-done.5.refs_5_), channel_id=1, source_target_pairs={{2,0},{4,2},{6,4},{7,6},{5,7},{3,5},{1,3},{0,1},{10,8},{12,10},{14... | collective-permute-start | bytes 786440 | tf_op jit(solution)/shard_map/ppermute | solution.py:265
  19.2 4.3 %collective-permute-start = (s32[32,8,128]{2,1,0:T(8,128)S(1)}, s32[32,8,128]{2,1,0:T(8,128)S(1)}, u32[]{:S(2)}, u32[]{:S(2)}) collective-permute-start(s32[32,8,128]{2,1,0:T(8,128)S(1)} %all-to-all-done), channel_id=1, source_target_pairs={{0,8},{8,0},{16,24},{24,16},{1,9},{9,1},{17,25},{25,17},{2,10},{10... | collective-permute-start | bytes 393224 | tf_op jit(solution)/shard_map/ppermute | solution.py:222
  21.4 11.1 %collective-permute-start.3 = (bf16[1024,128]{1,0:T(8,128)(2,1)S(1)}, bf16[1024,128]{1,0:T(8,128)(2,1)S(1)}, u32[]{:S(2)}, u32[]{:S(2)}) collective-permute-start(bf16[1024,128]{1,0:T(8,128)(2,1)S(1)} %collective-permute-done.2.refs_6_), channel_id=1, source_target_pairs={{0,2},{2,4},{4,6},{6,7},{7,5},{5,3},{3,1},{1,0},{8,10},{10,12},{12... | collective-permute-start | bytes 786440 | tf_op jit(solution)/shard_map/ppermute | solution.py:264
  22.6 11.2 %collective-permute-start.7 = (bf16[1024,128]{1,0:T(8,128)(2,1)S(1)}, bf16[1024,128]{1,0:T(8,128)(2,1)S(1)}, u32[]{:S(2)}, u32[]{:S(2)}) collective-permute-start(bf16[1024,128]{1,0:T(8,128)(2,1)S(1)} %collective-permute-done.6.refs_7_), channel_id=1, source_target_pairs={{2,0},{4,2},{6,4},{7,6},{5,7},{3,5},{1,3},{0,1},{10,8},{12,10},{14... | collective-permute-start | bytes 786440 | tf_op jit(solution)/shard_map/ppermute | solution.py:265
  32.5 6.7 %collective-permute-start.4 = (bf16[512,128]{1,0:T(8,128)(2,1)S(1)}, bf16[512,128]{1,0:T(8,128)(2,1)S(1)}, u32[]{:S(2)}, u32[]{:S(2)}) collective-permute-start(bf16[512,128]{1,0:T(8,128)(2,1)S(1)} %slice.8), channel_id=1, source_target_pairs={{0,2},{2,4},{4,6},{6,7},{7,5},{5,3},{3,1},{1,0},{8,10},{10,12},{12... | collective-permute-start | bytes 393224 | tf_op jit(solution)/shard_map/ppermute | solution.py:270
  33.7 5.5 %collective-permute-start.8 = (bf16[512,128]{1,0:T(8,128)(2,1)S(1)}, bf16[512,128]{1,0:T(8,128)(2,1)S(1)}, u32[]{:S(2)}, u32[]{:S(2)}) collective-permute-start(bf16[512,128]{1,0:T(8,128)(2,1)S(1)} %slice.9), channel_id=1, source_target_pairs={{2,0},{4,2},{6,4},{7,6},{5,7},{3,5},{1,3},{0,1},{10,8},{12,10},{14... | collective-permute-start | bytes 393224 | tf_op jit(solution)/shard_map/ppermute | solution.py:271
  39.2 7.8 %copy-start = (bf16[512,512]{1,0:T(8,128)(2,1)S(1)}, bf16[512,512]{1,0:T(8,128)(2,1)}, u32[]{:S(2)}) copy-start(bf16[512,512]{1,0:T(8,128)(2,1)} %refs_4_.1) | copy-start | bytes 1572868
  41.2 4.3 %collective-permute-start.10 = (bf16[256,128]{1,0:T(8,128)(2,1)S(1)}, bf16[256,128]{1,0:T(8,128)(2,1)S(1)}, u32[]{:S(2)}, u32[]{:S(2)}) collective-permute-start(bf16[256,128]{1,0:T(8,128)(2,1)S(1)} %get-tuple-element.11), channel_id=1, source_target_pairs={{0,16},{8,24},{16,0},{24,8},{1,17},{9,25},{17,1},{25,9},{2,18},{10... | collective-permute-start | bytes 196616 | tf_op jit(solution)/shard_map/ppermute | solution.py:276
  42.7 3.2 %collective-permute-start.11 = (bf16[256,128]{1,0:T(8,128)(2,1)S(1)}, bf16[256,128]{1,0:T(8,128)(2,1)S(1)}, u32[]{:S(2)}, u32[]{:S(2)}) collective-permute-start(bf16[256,128]{1,0:T(8,128)(2,1)S(1)} %get-tuple-element.12), channel_id=1, source_target_pairs={{0,24},{8,0},{16,8},{24,16},{1,25},{9,1},{17,9},{25,17},{2,26},{10... | collective-permute-start | bytes 196616 | tf_op jit(solution)/shard_map/ppermute | solution.py:276
  42.8 4.2 %copy-start.1 = (f32[512]{0:T(512)S(1)}, f32[512]{0:T(512)}, u32[]{:S(2)}) copy-start(f32[512]{0:T(512)} %param.8) | copy-start | bytes 6148
  42.8 4.2 %collective-permute-start.9 = (bf16[256,128]{1,0:T(8,128)(2,1)S(1)}, bf16[256,128]{1,0:T(8,128)(2,1)S(1)}, u32[]{:S(2)}, u32[]{:S(2)}) collective-permute-start(bf16[256,128]{1,0:T(8,128)(2,1)S(1)} %get-tuple-element.10), channel_id=1, source_target_pairs={{0,8},{8,16},{16,24},{24,0},{1,9},{9,17},{17,25},{25,1},{2,10},{10... | collective-permute-start | bytes 196616 | tf_op jit(solution)/shard_map/ppermute | solution.py:276

commit v2 on v1

--- a/solution.py
+++ b/solution.py
@@ -47,13 +47,13 @@
         out_ref[r, :, :own, :] = edges[:, first : first + own, :]
     src_high = jnp.where(live, src // LANES, high)
     src_low = src % LANES
-    high_ids = lax.broadcasted_iota(jnp.int32, (high, cap), 0)
-    low_ids = lax.broadcasted_iota(jnp.int32, (LANES, cap), 0)
+    high_ids = short(lax.broadcasted_iota(jnp.int32, (high, cap), 0))
+    low_ids = short(lax.broadcasted_iota(jnp.int32, (LANES, cap), 0))
     total = jnp.zeros((high, LANES), jnp.float32)
     for t in range(tiles):
         total += lax.dot_general(
-            flag(high_ids == src_high[t : t + 1]),
-            flag(low_ids == src_low[t : t + 1]),
+            equal(high_ids, src_high[t : t + 1]).astype(BITS8),
+            equal(low_ids, src_low[t : t + 1]).astype(BITS8),
             NT,
             preferred_element_type=jnp.float32,
         )
@@ -82,11 +82,9 @@
     edge_refs, refs = refs[:2], refs[2:]
     xs, refs = refs[: sum(groups)], refs[sum(groups) :]
     if not first:
-        old_ref, *refs = refs
+        old_ref, old_degree_ref, *refs = refs
     rows, _, depth, _ = edge_refs[0].shape
-    out_refs, refs = refs[: rows if last else 1], refs[rows if last else 1 :]
-    counts, scaled, *refs = refs
-    total = refs[0] if last else out_refs[0]
+    out_refs, (counts, scaled, total) = refs[:-3], refs[-3:]
     width = xs[0].shape[1]
     _, sums, src_rows = counts.shape
     highs = src_rows // LOW
@@ -102,6 +100,9 @@
     target_ids = short(lax.broadcasted_iota(jnp.int32, (TILE, LANES), 0))
     low_ids = short(lax.broadcasted_iota(jnp.int32, (LOW, LANES), 0))
 
+    def as_column(row):
+        return jnp.sum(jnp.where(diagonal, row, 0.0), axis=1, keepdims=True)
+
     def put_scaled(g):
         halves = [
             sum(edge_ref[r, blocks[g], own:, :] for r in range(rows)).astype(jnp.float32)
@@ -112,8 +113,7 @@
         top = 0
         for x_ref in xs[sum(groups[:g]) : sum(groups[: g + 1])]:
             for i in range(x_ref.shape[0] // LANES):
-                row = scale[top // LANES : top // LANES + 1]
-                column = jnp.sum(jnp.where(diagonal, row, 0.0), axis=1, keepdims=True)
+                column = as_column(scale[top // LANES : top // LANES + 1])
                 x = x_ref[i * LANES : (i + 1) * LANES, :].astype(jnp.float32)
                 scaled[g % 2, top : top + LANES, :width] = (x * column).astype(jnp.bfloat16)
                 top += LANES
@@ -135,12 +135,11 @@
             preferred_element_type=jnp.float32,
         )
 
-    def add_block(g, convert, unroll):
+    def add_block(g, convert, unroll, start):
         def fill_tile(part, i, carry):
-            r, t = i // tiles, i % tiles
-            block = count_block(g, edge_refs[part], r, t)
-            half = 1 - odd if part else odd
-            top = pl.multiple_of(((2 * r + half) * tiles + t) * TILE, TILE)
+            block = count_block(g, edge_refs[part], i // tiles, i % tiles)
+            top = (part * rows * tiles + i) * TILE
+            top = top if unroll else pl.multiple_of(top, TILE)
             for h in range(highs):
                 counts[g % 2, pl.ds(top, TILE), h * LOW : (h + 1) * LOW] = convert(
                     block[h * TILE : (h + 1) * TILE]
@@ -154,12 +153,12 @@
                     fill_tile(part, i, 0)
             else:
                 lax.fori_loop(0, rows * tiles, functools.partial(fill_tile, part), 0)
-        total[...] += jnp.dot(counts[g % 2], scaled[g % 2], preferred_element_type=jnp.float32)
+        added = jnp.dot(counts[g % 2], scaled[g % 2], preferred_element_type=jnp.float32)
+        total[...] = added if start else total[...] + added
 
     scaled[...] = jnp.ones_like(scaled)
-    total[...] = jnp.zeros_like(total) if first else old_ref[...]
     for g in range(len(groups)):
-        add_block(g, lambda block: block.astype(jnp.bfloat16), rows * tiles <= 4)
+        add_block(g, lambda block: block.astype(jnp.bfloat16), rows * tiles <= 4, g == 0)
 
     @pl.when(jnp.max(total[:, LANES:]) >= 256.0)
     def _():
@@ -168,14 +167,31 @@
                 g,
                 lambda block: (block - block.astype(jnp.bfloat16).astype(jnp.float32)).astype(jnp.bfloat16),
                 False,
+                False,
             )
 
     if last:
-        for shift, out_ref in enumerate(out_refs):
-            size = out_ref.shape[0]
-            part = pl.ds(pl.multiple_of(lax.rem(row_ref[0] + shift, rows) * size, size), size)
-            norm = lax.rsqrt(1.0 + total[part, LANES : LANES + width])
-            out_ref[...] = (total[part, :width] * norm).astype(jnp.bfloat16)
+        for shift in range(rows):
+            r = lax.rem(row_ref[0] + shift, rows)
+            for part in range(2):
+                for t in range(tiles):
+                    i = (part * rows + r) * tiles + t
+                    at = pl.ds(pl.multiple_of(i * TILE, TILE), TILE)
+                    value, degree = total[at, :width], total[at, LANES:]
+                    if not first:
+                        value += old_ref[at, :]
+                        degree += as_column(old_degree_ref[pl.ds(i, 1), :])
+                    half = 1 - odd if part else odd
+                    place = pl.multiple_of((half * tiles + t) * TILE, TILE)
+                    norm = lax.rsqrt(1.0 + degree[:, :width])
+                    out_refs[shift][pl.ds(place, TILE), :] = (value * norm).astype(jnp.bfloat16)
+    else:
+        for i in range(sums // TILE):
+            at = slice(i * TILE, (i + 1) * TILE)
+            line = jnp.sum(jnp.where(diagonal, total[at, LANES:], 0.0), axis=0, keepdims=True)
+            value = total[at, :width]
+            out_refs[0][at, :] = value if first else value + old_ref[at, :]
+            out_refs[1][i : i + 1, :] = line if first else line + old_degree_ref[i : i + 1, :]
 
 
 def layer_kernel(row_ref, *refs):
@@ -224,34 +240,33 @@
     col = lax.axis_index("col").astype(jnp.int32).reshape(1)
     row = lax.axis_index("row").astype(jnp.int32).reshape(1)
 
+    smem, vmem = pl.BlockSpec(memory_space=pltpu.SMEM), pl.BlockSpec(memory_space=pltpu.VMEM)
+
     def add_blocks(total, blocks, last, flops):
         first = total is None
         shifts = [shift for shift, _ in blocks]
         groups = [len(pieces) for _, pieces in blocks]
         pieces = [piece for _, listed in blocks for piece in listed]
 
-        whole = lambda array: pl.BlockSpec(array.shape, lambda i, c, r: (0,) * array.ndim)
-        operands = pieces + ([] if first else [total])
+        operands = pieces + ([] if first else list(total))
         out_shape = (
             [jax.ShapeDtypeStruct((own_nodes, width), jnp.bfloat16)] * rows
             if last
-            else [jax.ShapeDtypeStruct((sums, 2 * LANES), jnp.float32)]
+            else [
+                jax.ShapeDtypeStruct((sums, width), jnp.float32),
+                jax.ShapeDtypeStruct((sums // TILE, LANES), jnp.float32),
+            ]
         )
         scratch = [
             pltpu.VMEM((2, sums, src_rows), jnp.bfloat16),
             pltpu.VMEM((2, src_rows, 2 * LANES), jnp.bfloat16),
+            pltpu.VMEM((sums, 2 * LANES), jnp.float32),
         ]
-        if last:
-            scratch.append(pltpu.VMEM((sums, 2 * LANES), jnp.float32))
         return pl.pallas_call(
             functools.partial(sum_kernel, cols, shifts, groups, first, last),
-            grid_spec=pltpu.PrefetchScalarGridSpec(
-                num_scalar_prefetch=2,
-                grid=(1,),
-                in_specs=[whole(operand) for operand in edges + operands],
-                out_specs=[whole(array) for array in out_shape],
-                scratch_shapes=scratch,
-            ),
+            in_specs=[smem] * 2 + [vmem] * (2 + len(operands)),
+            out_specs=[vmem] * len(out_shape),
+            scratch_shapes=scratch,
             out_shape=out_shape,
             compiler_params=pltpu.CompilerParams(vmem_limit_bytes=48 * 1024 * 1024),
             cost_estimate=pl.CostEstimate(flops=flops, bytes_accessed=2**22, transcendentals=0),
@@ -265,15 +280,16 @@
         downs = lax.ppermute(downs, "col", back)
         waiting += [(-hop, [ups]), (hop, [downs])]
         if hop > 1:
-            (total,) = add_blocks(total, waiting, False, 2 * len(waiting) * block_flops)
+            total = add_blocks(total, waiting, False, 2 * len(waiting) * block_flops)
             waiting = []
     ups = lax.ppermute(ups[:half], "col", ahead)
     downs = lax.ppermute(downs[half:], "col", back)
     waiting.append((cols // 2, [ups, downs]))
-    normed = list(add_blocks(total, waiting, True, block_flops))
-    for shift in range(1, rows):
-        pairs = [(r, (r + shift) % rows) for r in range(rows)]
-        normed[shift] = lax.ppermute(normed[shift], "row", pairs)
+    normed = add_blocks(total, waiting, True, block_flops)
+    normed = [normed[0]] + [
+        lax.ppermute(normed[shift], "row", [(r, (r + shift) % rows) for r in range(rows)])
+        for shift in range(1, rows)
+    ]
     operands = [*normed, weight]
     return pl.pallas_call(
         layer_kernel,

time: 48.5 us -> 46.4 us (0.957)
  Pallas kernels: 18.6 us -> 16.5 us
    pallas_call x3, Pallas kernels: 15.3 us -> 13.4 us  [add_blocks(): pl.pallas_call(functools.partial(sum_kernel, cols, shifts, groups, first,...]
  transfers between devices with their start and end apart: 13 -> 13, of which waited for: 6 -> 6; matrix products, arithmetic and copies ran while one was open for 0% -> 0% of each run, Pallas kernels for 32% -> 29%
where the time goes in v2:
time: 46.4 us; the launch traced here: 46.2 us
  starting transfers between devices  17.9 us (39%)
  Pallas kernels  16.5 us (36%)
  waiting for transfers between devices  11.5 us (25%)
    pallas_call x3, Pallas kernels, add_blocks(): pl.pallas_call(functools.partial(sum_kernel, cols, shifts, groups, first,...  13.4 us
    all_to_all x1, starting transfers between devices, body(): lax.all_to_all(packed.reshape(rows * cols, depth, LANES), ('row', 'col'),...  6.3 us
    ppermute x3, starting transfers between devices, body(): ups = lax.ppermute(ups, 'col', ahead)  5.87 us
    all_to_all x1, waiting for transfers between devices, body(): lax.all_to_all(packed.reshape(rows * cols, depth, LANES), ('row', 'col'),...  5.65 us
    ppermute x3, waiting for transfers between devices, body(): lax.ppermute(normed[shift], 'row', [(r, (r + shift) % rows) for r in rang...  3.6 us
    ppermute x3, starting transfers between devices, body(): lax.ppermute(normed[shift], 'row', [(r, (r + shift) % rows) for r in rang...  2.13 us
    ppermute x3, waiting for transfers between devices, body(): ups = lax.ppermute(ups, 'col', ahead)  2.07 us
    pallas_call x1, Pallas kernels, body(): pl.pallas_call(pack_kernel, in_specs=[pl.BlockSpec(), pl.BlockSpec(), pl....  1.89 us
  transfers between devices with their start and end apart: 13, of which 6 were waited for; matrix products, arithmetic and copies ran while one was open for 0% of the time, Pallas kernels for 29%

profile of v2, /device:TPU:0, one launch (start us, length us, event | category | flops | bytes accessed | tf_op | source)
XLA Modules:
  0.0 46.2 jit_solution(2621699508681904627)
XLA Ops:
  0.0 0.0 copy-start.2
  0.0 3.0 %collective-permute-start.1 = (bf16[1024,128]{1,0:T(8,128)(2,1)}, bf16[1024,128]{1,0:T(8,128)(2,1)S(1)}, u32[]{:S(2)}, u32[]{:S(2)}) collective-permute-start(bf16[1024,128]{1,0:T(8,128)(2,1)} %refs_3_.1), channel_id=1, source_target_pairs={{0,2},{2,4},{4,6},{6,7},{7,5},{5,3},{3,1},{1,0},{8,10},{10,12},{12... | collective-permute-start | bytes 786440 | tf_op jit(solution)/shard_map/ppermute | solution.py:279
  3.0 0.0 collective-permute-start.5
  3.0 1.9 %shard_map.64 = s32[4,8,8,128]{3,2,1,0:T(8,128)} custom-call(s32[16,512]{1,0:T(8,128)} %src_ref.1, s32[16,512]{1,0:T(8,128)} %dst_ref.1, s32[16]{0:T(128)} %bitcast.15), custom_call_target="tpu_custom_call" | custom-call | tf_op jit(solution)/shard_map/pallas_call | solution.py:225
  4.9 6.3 %all-to-all-start = ((s32[32,8,128]{2,1,0:T(8,128)}), s32[32,8,128]{2,1,0:T(8,128)S(1)}, u32[]{:S(2)}, u32[]{:S(2)}) async-start(s32[32,8,128]{2,1,0:T(8,128)} %bitcast.14), calls=%async_computation | async-start | bytes 262144 | tf_op jit(solution)/shard_map/all_to_all | solution.py:231
  11.2 0.0 collective-permute-done.1.refs_4_
  11.2 1.8 %collective-permute-start.2 = (bf16[1024,128]{1,0:T(8,128)(2,1)S(1)}, bf16[1024,128]{1,0:T(8,128)(2,1)S(1)}, u32[]{:S(2)}, u32[]{:S(2)}) collective-permute-start(bf16[1024,128]{1,0:T(8,128)(2,1)S(1)} %collective-permute-done.1.refs_4_), channel_id=1, source_target_pairs={{0,2},{2,4},{4,6},{6,7},{7,5},{5,3},{3,1},{1,0},{8,10},{10,12},{12... | collective-permute-start | bytes 786440 | tf_op jit(solution)/shard_map/ppermute | solution.py:279
  13.1 0.0 collective-permute-done.5.refs_5_
  13.1 0.3 collective-permute-start.6
  13.3 5.7 %all-to-all-done = s32[32,8,128]{2,1,0:T(8,128)S(1)} async-done(((s32[32,8,128]{2,1,0:T(8,128)}), s32[32,8,128]{2,1,0:T(8,128)S(1)}, u32[]{:S(2)}, u32[]{:S(2)}) %all-to-all-start) | async-done | bytes 131104 | tf_op jit(solution)/shard_map/all_to_all | solution.py:231
  19.0 0.1 collective-permute-start
  19.1 2.1 %collective-permute-done.2.refs_6_ = bf16[1024,128]{1,0:T(8,128)(2,1)S(1)} collective-permute-done((bf16[1024,128]{1,0:T(8,128)(2,1)S(1)}, bf16[1024,128]{1,0:T(8,128)(2,1)S(1)}, u32[]{:S(2)}, u32[]{:S(2)}) %collective-permute-start.2) | collective-permute-done | bytes 262176 | tf_op jit(solution)/shard_map/ppermute | solution.py:279
  21.1 1.0 %collective-permute-start.3 = (bf16[1024,128]{1,0:T(8,128)(2,1)S(1)}, bf16[1024,128]{1,0:T(8,128)(2,1)S(1)}, u32[]{:S(2)}, u32[]{:S(2)}) collective-permute-start(bf16[1024,128]{1,0:T(8,128)(2,1)S(1)} %collective-permute-done.2.refs_6_), channel_id=1, source_target_pairs={{0,2},{2,4},{4,6},{6,7},{7,5},{5,3},{3,1},{1,0},{8,10},{10,12},{12... | collective-permute-start | bytes 786440 | tf_op jit(solution)/shard_map/ppermute | solution.py:279
  22.2 0.1 collective-permute-done.6.refs_7_
  22.3 1.0 %collective-permute-start.7 = (bf16[1024,128]{1,0:T(8,128)(2,1)S(1)}, bf16[1024,128]{1,0:T(8,128)(2,1)S(1)}, u32[]{:S(2)}, u32[]{:S(2)}) collective-permute-start(bf16[1024,128]{1,0:T(8,128)(2,1)S(1)} %collective-permute-done.6.refs_7_), channel_id=1, source_target_pairs={{2,0},{4,2},{6,4},{7,6},{5,7},{3,5},{1,3},{0,1},{10,8},{12,10},{14... | collective-permute-start | bytes 786440 | tf_op jit(solution)/shard_map/ppermute | solution.py:280
  23.3 0.0 collective-permute-done
  23.3 0.0 copy-done.2
  23.3 7.5 %shard_map.65 = (f32[1024,128]{1,0:T(8,128)S(1)}, f32[8,128]{1,0:T(8,128)S(1)}) custom-call(s32[1]{0:T(128)} %bitcast.1.col_ref, s32[1]{0:T(128)} %bitcast.refs_0_.row_ref, s32[4,8,8,128]{3,2,1,0:T(8,128)S(1)} %bitcast.7, s32[4,8,8,128]{3,2,1,0:T(8,128)S(1)} %bitcast.11, bf16[1024,128]{1,0:T(8,128)(2,1)S(1)} %copy-done.2, ...), custom_call_target="tpu_custom_call" | custom-call | flops 16106127360 | bytes 4194304 | tf_op jit(solution)/shard_map/pallas_call | solution.py:265
  30.8 0.0 collective-permute-done.3.refs_3_
  30.8 1.2 %collective-permute-start.4 = (bf16[512,128]{1,0:T(8,128)(2,1)S(1)}, bf16[512,128]{1,0:T(8,128)(2,1)S(1)}, u32[]{:S(2)}, u32[]{:S(2)}) collective-permute-start(bf16[512,128]{1,0:T(8,128)(2,1)S(1)} %slice.8), channel_id=1, source_target_pairs={{0,2},{2,4},{4,6},{6,7},{7,5},{5,3},{3,1},{1,0},{8,10},{10,12},{12... | collective-permute-start | bytes 393224 | tf_op jit(solution)/shard_map/ppermute | solution.py:285
  32.0 0.0 collective-permute-done.7.refs_4_
  32.1 1.1 %collective-permute-start.8 = (bf16[512,128]{1,0:T(8,128)(2,1)S(1)}, bf16[512,128]{1,0:T(8,128)(2,1)S(1)}, u32[]{:S(2)}, u32[]{:S(2)}) collective-permute-start(bf16[512,128]{1,0:T(8,128)(2,1)S(1)} %slice.9), channel_id=1, source_target_pairs={{2,0},{4,2},{6,4},{7,6},{5,7},{3,5},{1,3},{0,1},{10,8},{12,10},{14... | collective-permute-start | bytes 393224 | tf_op jit(solution)/shard_map/ppermute | solution.py:286
  33.2 3.9 %shard_map.66 = (f32[1024,128]{1,0:T(8,128)S(1)}, f32[8,128]{1,0:T(8,128)S(1)}) custom-call(s32[1]{0:T(128)} %bitcast.1.col_ref, s32[1]{0:T(128)} %bitcast.refs_0_.row_ref, s32[4,8,8,128]{3,2,1,0:T(8,128)S(1)} %bitcast.8, s32[4,8,8,128]{3,2,1,0:T(8,128)S(1)} %bitcast.12, bf16[1024,128]{1,0:T(8,128)(2,1)S(1)} %collective-permute-done.3.refs_3_, ...), custom_call_target="tpu_custom_call" | custom-call | flops 6442450944 | bytes 4194304 | tf_op jit(solution)/shard_map/pallas_call | solution.py:265
  37.1 0.0 collective-permute-done.4.refs_3_
  37.1 0.0 collective-permute-done.8.refs_4_
  37.1 0.0 copy-start
  37.1 2.0 %shard_map.67 = (bf16[256,128]{1,0:T(8,128)(2,1)S(1)}, bf16[256,128]{1,0:T(8,128)(2,1)S(1)}, bf16[256,128]{1,0:T(8,128)(2,1)S(1)}, bf16[256,128]{1,0:T(8,128)(2,1)S(1)}) custom-call(s32[1]{0:T(128)} %bitcast.1.col_ref, s32[1]{0:T(128)} %bitcast.refs_0_.row_ref, s32[4,8,8,128]{3,2,1,0:T(8,128)S(1)} %bitcast.9, s32[4,8,8,128]{3,2,1,0:T(8,128)S(1)} %bitcast.13, ...), custom_call_target="tpu_custom_call" | custom-call | flops 1610612736 | bytes 4194304 | tf_op jit(solution)/shard_map/pallas_call | solution.py:265
  39.1 1.6 %collective-permute-start.10 = (bf16[256,128]{1,0:T(8,128)(2,1)S(1)}, bf16[256,128]{1,0:T(8,128)(2,1)S(1)}, u32[]{:S(2)}, u32[]{:S(2)}) collective-permute-start(bf16[256,128]{1,0:T(8,128)(2,1)S(1)} %get-tuple-element.19), channel_id=1, source_target_pairs={{0,16},{8,24},{16,0},{24,8},{1,17},{9,25},{17,1},{25,9},{2,18},{10... | collective-permute-start | bytes 196616 | tf_op jit(solution)/shard_map/ppermute | solution.py:290
  40.7 0.0 collective-permute-start.11
  40.7 0.0 copy-start.1
  40.7 0.5 %collective-permute-start.9 = (bf16[256,128]{1,0:T(8,128)(2,1)S(1)}, bf16[256,128]{1,0:T(8,128)(2,1)S(1)}, u32[]{:S(2)}, u32[]{:S(2)}) collective-permute-start(bf16[256,128]{1,0:T(8,128)(2,1)S(1)} %get-tuple-element.18), channel_id=1, source_target_pairs={{0,8},{8,16},{16,24},{24,0},{1,9},{9,17},{17,25},{25,1},{2,10},{10... | collective-permute-start | bytes 196616 | tf_op jit(solution)/shard_map/ppermute | solution.py:290
  41.2 2.2 %collective-permute-done.10.refs_2_ = bf16[256,128]{1,0:T(8,128)(2,1)S(1)} collective-permute-done((bf16[256,128]{1,0:T(8,128)(2,1)S(1)}, bf16[256,128]{1,0:T(8,128)(2,1)S(1)}, u32[]{:S(2)}, u32[]{:S(2)}) %collective-permute-start.10) | collective-permute-done | bytes 65568 | tf_op jit(solution)/shard_map/ppermute | solution.py:290
  43.4 0.4 collective-permute-done.11.refs_3_
  43.8 1.0 %collective-permute-done.9.refs_1_ = bf16[256,128]{1,0:T(8,128)(2,1)S(1)} collective-permute-done((bf16[256,128]{1,0:T(8,128)(2,1)S(1)}, bf16[256,128]{1,0:T(8,128)(2,1)S(1)}, u32[]{:S(2)}, u32[]{:S(2)}) %collective-permute-start.9) | collective-permute-done | bytes 65568 | tf_op jit(solution)/shard_map/ppermute | solution.py:290
  44.8 0.0 copy-done
  44.8 0.0 copy-done.1
  44.8 1.2 %shard_map.68 = bf16[256,512]{1,0:T(8,128)(2,1)} custom-call(s32[1]{0:T(128)} %bitcast.refs_0_.row_ref, bf16[256,128]{1,0:T(8,128)(2,1)S(1)} %get-tuple-element.17.refs_0_, bf16[256,128]{1,0:T(8,128)(2,1)S(1)} %collective-permute-done.9.refs_1_, bf16[256,128]{1,0:T(8,128)(2,1)S(1)} %collective-permute-done.10.refs_2_, ...), custom_call_target="tpu_custom_call" | custom-call | tf_op jit(solution)/shard_map/pallas_call | solution.py:294
  (2 shorter events, 0.0 us)
Async XLA Ops:
  0.0 23.3 %copy-start.2 = (bf16[1024,128]{1,0:T(8,128)(2,1)S(1)}, bf16[1024,128]{1,0:T(8,128)(2,1)}, u32[]{:S(2)}) copy-start(bf16[1024,128]{1,0:T(8,128)(2,1)} %refs_3_.1) | copy-start | bytes 786436
  0.0 11.2 %collective-permute-start.1 = (bf16[1024,128]{1,0:T(8,128)(2,1)}, bf16[1024,128]{1,0:T(8,128)(2,1)S(1)}, u32[]{:S(2)}, u32[]{:S(2)}) collective-permute-start(bf16[1024,128]{1,0:T(8,128)(2,1)} %refs_3_.1), channel_id=1, source_target_pairs={{0,2},{2,4},{4,6},{6,7},{7,5},{5,3},{3,1},{1,0},{8,10},{10,12},{12... | collective-permute-start | bytes 786440 | tf_op jit(solution)/shard_map/ppermute | solution.py:279
  3.0 10.0 %collective-permute-start.5 = (bf16[1024,128]{1,0:T(8,128)(2,1)}, bf16[1024,128]{1,0:T(8,128)(2,1)S(1)}, u32[]{:S(2)}, u32[]{:S(2)}) collective-permute-start(bf16[1024,128]{1,0:T(8,128)(2,1)} %refs_3_.1), channel_id=1, source_target_pairs={{2,0},{4,2},{6,4},{7,6},{5,7},{3,5},{1,3},{0,1},{10,8},{12,10},{14... | collective-permute-start | bytes 786440 | tf_op jit(solution)/shard_map/ppermute | solution.py:280
  4.9 14.1 %all-to-all-start = ((s32[32,8,128]{2,1,0:T(8,128)}), s32[32,8,128]{2,1,0:T(8,128)S(1)}, u32[]{:S(2)}, u32[]{:S(2)}) async-start(s32[32,8,128]{2,1,0:T(8,128)} %bitcast.14), calls=%async_computation | async-start | bytes 262144 | tf_op jit(solution)/shard_map/all_to_all | solution.py:231
  11.2 9.9 %collective-permute-start.2 = (bf16[1024,128]{1,0:T(8,128)(2,1)S(1)}, bf16[1024,128]{1,0:T(8,128)(2,1)S(1)}, u32[]{:S(2)}, u32[]{:S(2)}) collective-permute-start(bf16[1024,128]{1,0:T(8,128)(2,1)S(1)} %collective-permute-done.1.refs_4_), channel_id=1, source_target_pairs={{0,2},{2,4},{4,6},{6,7},{7,5},{5,3},{3,1},{1,0},{8,10},{10,12},{12... | collective-permute-start | bytes 786440 | tf_op jit(solution)/shard_map/ppermute | solution.py:279
  13.1 9.3 %collective-permute-start.6 = (bf16[1024,128]{1,0:T(8,128)(2,1)S(1)}, bf16[1024,128]{1,0:T(8,128)(2,1)S(1)}, u32[]{:S(2)}, u32[]{:S(2)}) collective-permute-start(bf16[1024,128]{1,0:T(8,128)(2,1)S(1)} %collective-permute-done.5.refs_5_), channel_id=1, source_target_pairs={{2,0},{4,2},{6,4},{7,6},{5,7},{3,5},{1,3},{0,1},{10,8},{12,10},{14... | collective-permute-start | bytes 786440 | tf_op jit(solution)/shard_map/ppermute | solution.py:280
  19.0 4.3 %collective-permute-start = (s32[32,8,128]{2,1,0:T(8,128)S(1)}, s32[32,8,128]{2,1,0:T(8,128)S(1)}, u32[]{:S(2)}, u32[]{:S(2)}) collective-permute-start(s32[32,8,128]{2,1,0:T(8,128)S(1)} %all-to-all-done), channel_id=1, source_target_pairs={{0,8},{8,0},{16,24},{24,16},{1,9},{9,1},{17,25},{25,17},{2,10},{10... | collective-permute-start | bytes 393224 | tf_op jit(solution)/shard_map/ppermute | solution.py:238
  21.1 9.7 %collective-permute-start.3 = (bf16[1024,128]{1,0:T(8,128)(2,1)S(1)}, bf16[1024,128]{1,0:T(8,128)(2,1)S(1)}, u32[]{:S(2)}, u32[]{:S(2)}) collective-permute-start(bf16[1024,128]{1,0:T(8,128)(2,1)S(1)} %collective-permute-done.2.refs_6_), channel_id=1, source_target_pairs={{0,2},{2,4},{4,6},{6,7},{7,5},{5,3},{3,1},{1,0},{8,10},{10,12},{12... | collective-permute-start | bytes 786440 | tf_op jit(solution)/shard_map/ppermute | solution.py:279
  22.3 9.7 %collective-permute-start.7 = (bf16[1024,128]{1,0:T(8,128)(2,1)S(1)}, bf16[1024,128]{1,0:T(8,128)(2,1)S(1)}, u32[]{:S(2)}, u32[]{:S(2)}) collective-permute-start(bf16[1024,128]{1,0:T(8,128)(2,1)S(1)} %collective-permute-done.6.refs_7_), channel_id=1, source_target_pairs={{2,0},{4,2},{6,4},{7,6},{5,7},{3,5},{1,3},{0,1},{10,8},{12,10},{14... | collective-permute-start | bytes 786440 | tf_op jit(solution)/shard_map/ppermute | solution.py:280
  30.8 6.2 %collective-permute-start.4 = (bf16[512,128]{1,0:T(8,128)(2,1)S(1)}, bf16[512,128]{1,0:T(8,128)(2,1)S(1)}, u32[]{:S(2)}, u32[]{:S(2)}) collective-permute-start(bf16[512,128]{1,0:T(8,128)(2,1)S(1)} %slice.8), channel_id=1, source_target_pairs={{0,2},{2,4},{4,6},{6,7},{7,5},{5,3},{3,1},{1,0},{8,10},{10,12},{12... | collective-permute-start | bytes 393224 | tf_op jit(solution)/shard_map/ppermute | solution.py:285
  32.1 5.0 %collective-permute-start.8 = (bf16[512,128]{1,0:T(8,128)(2,1)S(1)}, bf16[512,128]{1,0:T(8,128)(2,1)S(1)}, u32[]{:S(2)}, u32[]{:S(2)}) collective-permute-start(bf16[512,128]{1,0:T(8,128)(2,1)S(1)} %slice.9), channel_id=1, source_target_pairs={{2,0},{4,2},{6,4},{7,6},{5,7},{3,5},{1,3},{0,1},{10,8},{12,10},{14... | collective-permute-start | bytes 393224 | tf_op jit(solution)/shard_map/ppermute | solution.py:286
  37.1 7.7 %copy-start = (bf16[512,512]{1,0:T(8,128)(2,1)S(1)}, bf16[512,512]{1,0:T(8,128)(2,1)}, u32[]{:S(2)}) copy-start(bf16[512,512]{1,0:T(8,128)(2,1)} %refs_4_.1) | copy-start | bytes 1572868
  39.1 4.3 %collective-permute-start.10 = (bf16[256,128]{1,0:T(8,128)(2,1)S(1)}, bf16[256,128]{1,0:T(8,128)(2,1)S(1)}, u32[]{:S(2)}, u32[]{:S(2)}) collective-permute-start(bf16[256,128]{1,0:T(8,128)(2,1)S(1)} %get-tuple-element.19), channel_id=1, source_target_pairs={{0,16},{8,24},{16,0},{24,8},{1,17},{9,25},{17,1},{25,9},{2,18},{10... | collective-permute-start | bytes 196616 | tf_op jit(solution)/shard_map/ppermute | solution.py:290
  40.7 3.1 %collective-permute-start.11 = (bf16[256,128]{1,0:T(8,128)(2,1)S(1)}, bf16[256,128]{1,0:T(8,128)(2,1)S(1)}, u32[]{:S(2)}, u32[]{:S(2)}) collective-permute-start(bf16[256,128]{1,0:T(8,128)(2,1)S(1)} %get-tuple-element.20), channel_id=1, source_target_pairs={{0,24},{8,0},{16,8},{24,16},{1,25},{9,1},{17,9},{25,17},{2,26},{10... | collective-permute-start | bytes 196616 | tf_op jit(solution)/shard_map/ppermute | solution.py:290
  40.7 4.1 %copy-start.1 = (f32[512]{0:T(512)S(1)}, f32[512]{0:T(512)}, u32[]{:S(2)}) copy-start(f32[512]{0:T(512)} %param.8) | copy-start | bytes 6148
  40.7 4.1 %collective-permute-start.9 = (bf16[256,128]{1,0:T(8,128)(2,1)S(1)}, bf16[256,128]{1,0:T(8,128)(2,1)S(1)}, u32[]{:S(2)}, u32[]{:S(2)}) collective-permute-start(bf16[256,128]{1,0:T(8,128)(2,1)S(1)} %get-tuple-element.18), channel_id=1, source_target_pairs={{0,8},{8,16},{16,24},{24,0},{1,9},{9,17},{17,25},{25,1},{2,10},{10... | collective-permute-start | bytes 196616 | tf_op jit(solution)/shard_map/ppermute | solution.py:290

commit v3 on v2

--- a/solution.py
+++ b/solution.py
@@ -250,11 +250,11 @@
 
         operands = pieces + ([] if first else list(total))
         out_shape = (
-            [jax.ShapeDtypeStruct((own_nodes, width), jnp.bfloat16)] * rows
+            [pltpu.VMEM((own_nodes, width), jnp.bfloat16)] * rows
             if last
             else [
-                jax.ShapeDtypeStruct((sums, width), jnp.float32),
-                jax.ShapeDtypeStruct((sums // TILE, LANES), jnp.float32),
+                pltpu.VMEM((sums, width), jnp.float32),
+                pltpu.VMEM((sums // TILE, LANES), jnp.float32),
             ]
         )
         scratch = [
@@ -270,7 +270,7 @@
             out_shape=out_shape,
             compiler_params=pltpu.CompilerParams(vmem_limit_bytes=48 * 1024 * 1024),
             cost_estimate=pl.CostEstimate(flops=flops, bytes_accessed=2**22, transcendentals=0),
-        )(col, row, *edges, *operands)
+        )(col, row, *[pltpu.with_memory_space_constraint(array, pltpu.VMEM) for array in edges + operands])
 
     block_flops = 2 * sums * src_rows * (2 * LANES + cap)
     ups = downs = features

time: 46.4 us -> 46.4 us (level)
  no operation moved by 1% of the time
where the time goes in v3:
time: 46.4 us; the launch traced here: 46.2 us
  starting transfers between devices  17.9 us (39%)
  Pallas kernels  16.5 us (36%)
  waiting for transfers between devices  11.5 us (25%)
    pallas_call x3, Pallas kernels, add_blocks(): pl.pallas_call(functools.partial(sum_kernel, cols, shifts, groups, first,...  13.4 us
    all_to_all x1, starting transfers between devices, body(): lax.all_to_all(packed.reshape(rows * cols, depth, LANES), ('row', 'col'),...  6.3 us
    ppermute x3, starting transfers between devices, body(): ups = lax.ppermute(ups, 'col', ahead)  5.87 us
    all_to_all x1, waiting for transfers between devices, body(): lax.all_to_all(packed.reshape(rows * cols, depth, LANES), ('row', 'col'),...  5.65 us
    ppermute x3, waiting for transfers between devices, body(): lax.ppermute(normed[shift], 'row', [(r, (r + shift) % rows) for r in rang...  3.6 us
    ppermute x3, starting transfers between devices, body(): lax.ppermute(normed[shift], 'row', [(r, (r + shift) % rows) for r in rang...  2.13 us
    ppermute x3, waiting for transfers between devices, body(): ups = lax.ppermute(ups, 'col', ahead)  2.07 us
    pallas_call x1, Pallas kernels, body(): pl.pallas_call(pack_kernel, in_specs=[pl.BlockSpec(), pl.BlockSpec(), pl....  1.89 us
  transfers between devices with their start and end apart: 13, of which 6 were waited for; matrix products, arithmetic and copies ran while one was open for 0% of the time, Pallas kernels for 29%

profile of v3, /device:TPU:0, one launch (start us, length us, event | category | flops | bytes accessed | tf_op | source)
XLA Modules:
  0.0 46.2 jit_solution(2621699508681904627)
XLA Ops:
  0.0 0.0 copy-start.2
  0.0 3.0 %collective-permute-start.1 = (bf16[1024,128]{1,0:T(8,128)(2,1)}, bf16[1024,128]{1,0:T(8,128)(2,1)S(1)}, u32[]{:S(2)}, u32[]{:S(2)}) collective-permute-start(bf16[1024,128]{1,0:T(8,128)(2,1)} %refs_3_.1), channel_id=1, source_target_pairs={{0,2},{2,4},{4,6},{6,7},{7,5},{5,3},{3,1},{1,0},{8,10},{10,12},{12... | collective-permute-start | bytes 786440 | tf_op jit(solution)/shard_map/ppermute | solution.py:279
  3.0 0.0 collective-permute-start.5
  3.0 1.9 %shard_map.64 = s32[4,8,8,128]{3,2,1,0:T(8,128)} custom-call(s32[16,512]{1,0:T(8,128)} %src_ref.1, s32[16,512]{1,0:T(8,128)} %dst_ref.1, s32[16]{0:T(128)} %bitcast.15), custom_call_target="tpu_custom_call" | custom-call | tf_op jit(solution)/shard_map/pallas_call | solution.py:225
  4.9 6.3 %all-to-all-start = ((s32[32,8,128]{2,1,0:T(8,128)}), s32[32,8,128]{2,1,0:T(8,128)S(1)}, u32[]{:S(2)}, u32[]{:S(2)}) async-start(s32[32,8,128]{2,1,0:T(8,128)} %bitcast.14), calls=%async_computation | async-start | bytes 262144 | tf_op jit(solution)/shard_map/all_to_all | solution.py:231
  11.2 0.0 collective-permute-done.1.refs_4_
  11.2 1.8 %collective-permute-start.2 = (bf16[1024,128]{1,0:T(8,128)(2,1)S(1)}, bf16[1024,128]{1,0:T(8,128)(2,1)S(1)}, u32[]{:S(2)}, u32[]{:S(2)}) collective-permute-start(bf16[1024,128]{1,0:T(8,128)(2,1)S(1)} %collective-permute-done.1.refs_4_), channel_id=1, source_target_pairs={{0,2},{2,4},{4,6},{6,7},{7,5},{5,3},{3,1},{1,0},{8,10},{10,12},{12... | collective-permute-start | bytes 786440 | tf_op jit(solution)/shard_map/ppermute | solution.py:279
  13.1 0.0 collective-permute-done.5.refs_5_
  13.1 0.3 collective-permute-start.6
  13.3 5.7 %all-to-all-done = s32[32,8,128]{2,1,0:T(8,128)S(1)} async-done(((s32[32,8,128]{2,1,0:T(8,128)}), s32[32,8,128]{2,1,0:T(8,128)S(1)}, u32[]{:S(2)}, u32[]{:S(2)}) %all-to-all-start) | async-done | bytes 131104 | tf_op jit(solution)/shard_map/all_to_all | solution.py:231
  19.0 0.1 collective-permute-start
  19.1 2.1 %collective-permute-done.2.refs_6_ = bf16[1024,128]{1,0:T(8,128)(2,1)S(1)} collective-permute-done((bf16[1024,128]{1,0:T(8,128)(2,1)S(1)}, bf16[1024,128]{1,0:T(8,128)(2,1)S(1)}, u32[]{:S(2)}, u32[]{:S(2)}) %collective-permute-start.2) | collective-permute-done | bytes 262176 | tf_op jit(solution)/shard_map/ppermute | solution.py:279
  21.1 1.0 %collective-permute-start.3 = (bf16[1024,128]{1,0:T(8,128)(2,1)S(1)}, bf16[1024,128]{1,0:T(8,128)(2,1)S(1)}, u32[]{:S(2)}, u32[]{:S(2)}) collective-permute-start(bf16[1024,128]{1,0:T(8,128)(2,1)S(1)} %collective-permute-done.2.refs_6_), channel_id=1, source_target_pairs={{0,2},{2,4},{4,6},{6,7},{7,5},{5,3},{3,1},{1,0},{8,10},{10,12},{12... | collective-permute-start | bytes 786440 | tf_op jit(solution)/shard_map/ppermute | solution.py:279
  22.2 0.1 collective-permute-done.6.refs_7_
  22.3 1.0 %collective-permute-start.7 = (bf16[1024,128]{1,0:T(8,128)(2,1)S(1)}, bf16[1024,128]{1,0:T(8,128)(2,1)S(1)}, u32[]{:S(2)}, u32[]{:S(2)}) collective-permute-start(bf16[1024,128]{1,0:T(8,128)(2,1)S(1)} %collective-permute-done.6.refs_7_), channel_id=1, source_target_pairs={{2,0},{4,2},{6,4},{7,6},{5,7},{3,5},{1,3},{0,1},{10,8},{12,10},{14... | collective-permute-start | bytes 786440 | tf_op jit(solution)/shard_map/ppermute | solution.py:280
  23.3 0.0 collective-permute-done
  23.3 0.0 copy-done.2
  23.3 7.5 %shard_map.65 = (f32[1024,128]{1,0:T(8,128)S(1)}, f32[8,128]{1,0:T(8,128)S(1)}) custom-call(s32[1]{0:T(128)} %bitcast.1.col_ref, s32[1]{0:T(128)} %bitcast.refs_0_.row_ref, s32[4,8,8,128]{3,2,1,0:T(8,128)S(1)} %bitcast.7, s32[4,8,8,128]{3,2,1,0:T(8,128)S(1)} %bitcast.11, bf16[1024,128]{1,0:T(8,128)(2,1)S(1)} %copy-done.2, ...), custom_call_target="tpu_custom_call" | custom-call | flops 16106127360 | bytes 4194304 | tf_op jit(solution)/shard_map/pallas_call | solution.py:265
  30.8 0.0 collective-permute-done.3.refs_3_
  30.8 1.2 %collective-permute-start.4 = (bf16[512,128]{1,0:T(8,128)(2,1)S(1)}, bf16[512,128]{1,0:T(8,128)(2,1)S(1)}, u32[]{:S(2)}, u32[]{:S(2)}) collective-permute-start(bf16[512,128]{1,0:T(8,128)(2,1)S(1)} %slice.8), channel_id=1, source_target_pairs={{0,2},{2,4},{4,6},{6,7},{7,5},{5,3},{3,1},{1,0},{8,10},{10,12},{12... | collective-permute-start | bytes 393224 | tf_op jit(solution)/shard_map/ppermute | solution.py:285
  32.0 0.0 collective-permute-done.7.refs_4_
  32.1 1.1 %collective-permute-start.8 = (bf16[512,128]{1,0:T(8,128)(2,1)S(1)}, bf16[512,128]{1,0:T(8,128)(2,1)S(1)}, u32[]{:S(2)}, u32[]{:S(2)}) collective-permute-start(bf16[512,128]{1,0:T(8,128)(2,1)S(1)} %slice.9), channel_id=1, source_target_pairs={{2,0},{4,2},{6,4},{7,6},{5,7},{3,5},{1,3},{0,1},{10,8},{12,10},{14... | collective-permute-start | bytes 393224 | tf_op jit(solution)/shard_map/ppermute | solution.py:286
  33.2 3.9 %shard_map.66 = (f32[1024,128]{1,0:T(8,128)S(1)}, f32[8,128]{1,0:T(8,128)S(1)}) custom-call(s32[1]{0:T(128)} %bitcast.1.col_ref, s32[1]{0:T(128)} %bitcast.refs_0_.row_ref, s32[4,8,8,128]{3,2,1,0:T(8,128)S(1)} %bitcast.8, s32[4,8,8,128]{3,2,1,0:T(8,128)S(1)} %bitcast.12, bf16[1024,128]{1,0:T(8,128)(2,1)S(1)} %collective-permute-done.3.refs_3_, ...), custom_call_target="tpu_custom_call" | custom-call | flops 6442450944 | bytes 4194304 | tf_op jit(solution)/shard_map/pallas_call | solution.py:265
  37.1 0.0 collective-permute-done.4.refs_3_
  37.1 0.0 collective-permute-done.8.refs_4_
  37.1 0.0 copy-start
  37.1 2.0 %shard_map.67 = (bf16[256,128]{1,0:T(8,128)(2,1)S(1)}, bf16[256,128]{1,0:T(8,128)(2,1)S(1)}, bf16[256,128]{1,0:T(8,128)(2,1)S(1)}, bf16[256,128]{1,0:T(8,128)(2,1)S(1)}) custom-call(s32[1]{0:T(128)} %bitcast.1.col_ref, s32[1]{0:T(128)} %bitcast.refs_0_.row_ref, s32[4,8,8,128]{3,2,1,0:T(8,128)S(1)} %bitcast.9, s32[4,8,8,128]{3,2,1,0:T(8,128)S(1)} %bitcast.13, ...), custom_call_target="tpu_custom_call" | custom-call | flops 1610612736 | bytes 4194304 | tf_op jit(solution)/shard_map/pallas_call | solution.py:265
  39.1 1.6 %collective-permute-start.10 = (bf16[256,128]{1,0:T(8,128)(2,1)S(1)}, bf16[256,128]{1,0:T(8,128)(2,1)S(1)}, u32[]{:S(2)}, u32[]{:S(2)}) collective-permute-start(bf16[256,128]{1,0:T(8,128)(2,1)S(1)} %get-tuple-element.19), channel_id=1, source_target_pairs={{0,16},{8,24},{16,0},{24,8},{1,17},{9,25},{17,1},{25,9},{2,18},{10... | collective-permute-start | bytes 196616 | tf_op jit(solution)/shard_map/ppermute | solution.py:290
  40.7 0.0 collective-permute-start.11
  40.7 0.0 copy-start.1
  40.7 0.5 %collective-permute-start.9 = (bf16[256,128]{1,0:T(8,128)(2,1)S(1)}, bf16[256,128]{1,0:T(8,128)(2,1)S(1)}, u32[]{:S(2)}, u32[]{:S(2)}) collective-permute-start(bf16[256,128]{1,0:T(8,128)(2,1)S(1)} %get-tuple-element.18), channel_id=1, source_target_pairs={{0,8},{8,16},{16,24},{24,0},{1,9},{9,17},{17,25},{25,1},{2,10},{10... | collective-permute-start | bytes 196616 | tf_op jit(solution)/shard_map/ppermute | solution.py:290
  41.2 2.2 %collective-permute-done.10.refs_2_ = bf16[256,128]{1,0:T(8,128)(2,1)S(1)} collective-permute-done((bf16[256,128]{1,0:T(8,128)(2,1)S(1)}, bf16[256,128]{1,0:T(8,128)(2,1)S(1)}, u32[]{:S(2)}, u32[]{:S(2)}) %collective-permute-start.10) | collective-permute-done | bytes 65568 | tf_op jit(solution)/shard_map/ppermute | solution.py:290
  43.4 0.4 collective-permute-done.11.refs_3_
  43.8 1.0 %collective-permute-done.9.refs_1_ = bf16[256,128]{1,0:T(8,128)(2,1)S(1)} collective-permute-done((bf16[256,128]{1,0:T(8,128)(2,1)S(1)}, bf16[256,128]{1,0:T(8,128)(2,1)S(1)}, u32[]{:S(2)}, u32[]{:S(2)}) %collective-permute-start.9) | collective-permute-done | bytes 65568 | tf_op jit(solution)/shard_map/ppermute | solution.py:290
  44.8 0.0 copy-done
  44.8 0.0 copy-done.1
  44.8 1.2 %shard_map.68 = bf16[256,512]{1,0:T(8,128)(2,1)} custom-call(s32[1]{0:T(128)} %bitcast.refs_0_.row_ref, bf16[256,128]{1,0:T(8,128)(2,1)S(1)} %get-tuple-element.17.refs_0_, bf16[256,128]{1,0:T(8,128)(2,1)S(1)} %collective-permute-done.9.refs_1_, bf16[256,128]{1,0:T(8,128)(2,1)S(1)} %collective-permute-done.10.refs_2_, ...), custom_call_target="tpu_custom_call" | custom-call | tf_op jit(solution)/shard_map/pallas_call | solution.py:294
  (2 shorter events, 0.0 us)
Async XLA Ops:
  0.0 23.3 %copy-start.2 = (bf16[1024,128]{1,0:T(8,128)(2,1)S(1)}, bf16[1024,128]{1,0:T(8,128)(2,1)}, u32[]{:S(2)}) copy-start(bf16[1024,128]{1,0:T(8,128)(2,1)} %refs_3_.1) | copy-start | bytes 786436
  0.0 11.2 %collective-permute-start.1 = (bf16[1024,128]{1,0:T(8,128)(2,1)}, bf16[1024,128]{1,0:T(8,128)(2,1)S(1)}, u32[]{:S(2)}, u32[]{:S(2)}) collective-permute-start(bf16[1024,128]{1,0:T(8,128)(2,1)} %refs_3_.1), channel_id=1, source_target_pairs={{0,2},{2,4},{4,6},{6,7},{7,5},{5,3},{3,1},{1,0},{8,10},{10,12},{12... | collective-permute-start | bytes 786440 | tf_op jit(solution)/shard_map/ppermute | solution.py:279
  3.0 10.0 %collective-permute-start.5 = (bf16[1024,128]{1,0:T(8,128)(2,1)}, bf16[1024,128]{1,0:T(8,128)(2,1)S(1)}, u32[]{:S(2)}, u32[]{:S(2)}) collective-permute-start(bf16[1024,128]{1,0:T(8,128)(2,1)} %refs_3_.1), channel_id=1, source_target_pairs={{2,0},{4,2},{6,4},{7,6},{5,7},{3,5},{1,3},{0,1},{10,8},{12,10},{14... | collective-permute-start | bytes 786440 | tf_op jit(solution)/shard_map/ppermute | solution.py:280
  4.9 14.1 %all-to-all-start = ((s32[32,8,128]{2,1,0:T(8,128)}), s32[32,8,128]{2,1,0:T(8,128)S(1)}, u32[]{:S(2)}, u32[]{:S(2)}) async-start(s32[32,8,128]{2,1,0:T(8,128)} %bitcast.14), calls=%async_computation | async-start | bytes 262144 | tf_op jit(solution)/shard_map/all_to_all | solution.py:231
  11.2 9.9 %collective-permute-start.2 = (bf16[1024,128]{1,0:T(8,128)(2,1)S(1)}, bf16[1024,128]{1,0:T(8,128)(2,1)S(1)}, u32[]{:S(2)}, u32[]{:S(2)}) collective-permute-start(bf16[1024,128]{1,0:T(8,128)(2,1)S(1)} %collective-permute-done.1.refs_4_), channel_id=1, source_target_pairs={{0,2},{2,4},{4,6},{6,7},{7,5},{5,3},{3,1},{1,0},{8,10},{10,12},{12... | collective-permute-start | bytes 786440 | tf_op jit(solution)/shard_map/ppermute | solution.py:279
  13.1 9.3 %collective-permute-start.6 = (bf16[1024,128]{1,0:T(8,128)(2,1)S(1)}, bf16[1024,128]{1,0:T(8,128)(2,1)S(1)}, u32[]{:S(2)}, u32[]{:S(2)}) collective-permute-start(bf16[1024,128]{1,0:T(8,128)(2,1)S(1)} %collective-permute-done.5.refs_5_), channel_id=1, source_target_pairs={{2,0},{4,2},{6,4},{7,6},{5,7},{3,5},{1,3},{0,1},{10,8},{12,10},{14... | collective-permute-start | bytes 786440 | tf_op jit(solution)/shard_map/ppermute | solution.py:280
  19.0 4.3 %collective-permute-start = (s32[32,8,128]{2,1,0:T(8,128)S(1)}, s32[32,8,128]{2,1,0:T(8,128)S(1)}, u32[]{:S(2)}, u32[]{:S(2)}) collective-permute-start(s32[32,8,128]{2,1,0:T(8,128)S(1)} %all-to-all-done), channel_id=1, source_target_pairs={{0,8},{8,0},{16,24},{24,16},{1,9},{9,1},{17,25},{25,17},{2,10},{10... | collective-permute-start | bytes 393224 | tf_op jit(solution)/shard_map/ppermute | solution.py:238
  21.1 9.7 %collective-permute-start.3 = (bf16[1024,128]{1,0:T(8,128)(2,1)S(1)}, bf16[1024,128]{1,0:T(8,128)(2,1)S(1)}, u32[]{:S(2)}, u32[]{:S(2)}) collective-permute-start(bf16[1024,128]{1,0:T(8,128)(2,1)S(1)} %collective-permute-done.2.refs_6_), channel_id=1, source_target_pairs={{0,2},{2,4},{4,6},{6,7},{7,5},{5,3},{3,1},{1,0},{8,10},{10,12},{12... | collective-permute-start | bytes 786440 | tf_op jit(solution)/shard_map/ppermute | solution.py:279
  22.3 9.7 %collective-permute-start.7 = (bf16[1024,128]{1,0:T(8,128)(2,1)S(1)}, bf16[1024,128]{1,0:T(8,128)(2,1)S(1)}, u32[]{:S(2)}, u32[]{:S(2)}) collective-permute-start(bf16[1024,128]{1,0:T(8,128)(2,1)S(1)} %collective-permute-done.6.refs_7_), channel_id=1, source_target_pairs={{2,0},{4,2},{6,4},{7,6},{5,7},{3,5},{1,3},{0,1},{10,8},{12,10},{14... | collective-permute-start | bytes 786440 | tf_op jit(solution)/shard_map/ppermute | solution.py:280
  30.8 6.2 %collective-permute-start.4 = (bf16[512,128]{1,0:T(8,128)(2,1)S(1)}, bf16[512,128]{1,0:T(8,128)(2,1)S(1)}, u32[]{:S(2)}, u32[]{:S(2)}) collective-permute-start(bf16[512,128]{1,0:T(8,128)(2,1)S(1)} %slice.8), channel_id=1, source_target_pairs={{0,2},{2,4},{4,6},{6,7},{7,5},{5,3},{3,1},{1,0},{8,10},{10,12},{12... | collective-permute-start | bytes 393224 | tf_op jit(solution)/shard_map/ppermute | solution.py:285
  32.1 5.0 %collective-permute-start.8 = (bf16[512,128]{1,0:T(8,128)(2,1)S(1)}, bf16[512,128]{1,0:T(8,128)(2,1)S(1)}, u32[]{:S(2)}, u32[]{:S(2)}) collective-permute-start(bf16[512,128]{1,0:T(8,128)(2,1)S(1)} %slice.9), channel_id=1, source_target_pairs={{2,0},{4,2},{6,4},{7,6},{5,7},{3,5},{1,3},{0,1},{10,8},{12,10},{14... | collective-permute-start | bytes 393224 | tf_op jit(solution)/shard_map/ppermute | solution.py:286
  37.1 7.7 %copy-start = (bf16[512,512]{1,0:T(8,128)(2,1)S(1)}, bf16[512,512]{1,0:T(8,128)(2,1)}, u32[]{:S(2)}) copy-start(bf16[512,512]{1,0:T(8,128)(2,1)} %refs_4_.1) | copy-start | bytes 1572868
  39.1 4.3 %collective-permute-start.10 = (bf16[256,128]{1,0:T(8,128)(2,1)S(1)}, bf16[256,128]{1,0:T(8,128)(2,1)S(1)}, u32[]{:S(2)}, u32[]{:S(2)}) collective-permute-start(bf16[256,128]{1,0:T(8,128)(2,1)S(1)} %get-tuple-element.19), channel_id=1, source_target_pairs={{0,16},{8,24},{16,0},{24,8},{1,17},{9,25},{17,1},{25,9},{2,18},{10... | collective-permute-start | bytes 196616 | tf_op jit(solution)/shard_map/ppermute | solution.py:290
  40.7 3.1 %collective-permute-start.11 = (bf16[256,128]{1,0:T(8,128)(2,1)S(1)}, bf16[256,128]{1,0:T(8,128)(2,1)S(1)}, u32[]{:S(2)}, u32[]{:S(2)}) collective-permute-start(bf16[256,128]{1,0:T(8,128)(2,1)S(1)} %get-tuple-element.20), channel_id=1, source_target_pairs={{0,24},{8,0},{16,8},{24,16},{1,25},{9,1},{17,9},{25,17},{2,26},{10... | collective-permute-start | bytes 196616 | tf_op jit(solution)/shard_map/ppermute | solution.py:290
  40.7 4.1 %copy-start.1 = (f32[512]{0:T(512)S(1)}, f32[512]{0:T(512)}, u32[]{:S(2)}) copy-start(f32[512]{0:T(512)} %param.8) | copy-start | bytes 6148
  40.7 4.1 %collective-permute-start.9 = (bf16[256,128]{1,0:T(8,128)(2,1)S(1)}, bf16[256,128]{1,0:T(8,128)(2,1)S(1)}, u32[]{:S(2)}, u32[]{:S(2)}) collective-permute-start(bf16[256,128]{1,0:T(8,128)(2,1)S(1)} %get-tuple-element.18), channel_id=1, source_target_pairs={{0,8},{8,16},{16,24},{24,0},{1,9},{9,17},{17,25},{25,1},{2,10},{10... | collective-permute-start | bytes 196616 | tf_op jit(solution)/shard_map/ppermute | solution.py:290

commit v4 on v2

--- a/solution.py
+++ b/solution.py
@@ -86,14 +86,13 @@
     rows, _, depth, _ = edge_refs[0].shape
     out_refs, (counts, scaled, total) = refs[:-3], refs[-3:]
     width = xs[0].shape[1]
-    _, sums, src_rows = counts.shape
+    sums, src_rows = counts.shape
     highs = src_rows // LOW
     own = depth - src_rows // LANES // 2
     tiles = sums // rows // TILE // 2
     subs = own // tiles
     odd = lax.rem(row_ref[0], 2)
     place = ring_place(col_ref[0], cols)
-    blocks = [ring_col(lax.rem(place + shift + cols, cols), cols) for shift in shifts]
     diagonal = lax.broadcasted_iota(jnp.int32, (LANES, LANES), 0) == lax.broadcasted_iota(
         jnp.int32, (LANES, LANES), 1
     )
@@ -103,25 +102,25 @@
     def as_column(row):
         return jnp.sum(jnp.where(diagonal, row, 0.0), axis=1, keepdims=True)
 
-    def put_scaled(g):
+    def put_scaled(block, pieces):
         halves = [
-            sum(edge_ref[r, blocks[g], own:, :] for r in range(rows)).astype(jnp.float32)
+            sum(edge_ref[r, block, own:, :] for r in range(rows)).astype(jnp.float32)
             for edge_ref in edge_refs
         ]
         degree = jnp.where(odd == 0, jnp.concatenate(halves), jnp.concatenate(halves[::-1]))
         scale = lax.rsqrt(1.0 + degree)
         top = 0
-        for x_ref in xs[sum(groups[:g]) : sum(groups[: g + 1])]:
+        for x_ref in pieces:
             for i in range(x_ref.shape[0] // LANES):
                 column = as_column(scale[top // LANES : top // LANES + 1])
                 x = x_ref[i * LANES : (i + 1) * LANES, :].astype(jnp.float32)
-                scaled[g % 2, top : top + LANES, :width] = (x * column).astype(jnp.bfloat16)
+                scaled[top : top + LANES, :width] = (x * column).astype(jnp.bfloat16)
                 top += LANES
 
-    def count_block(g, edge_ref, r, t):
+    def count_block(block, edge_ref, r, t):
         lefts, rights = [], []
         for j in range(subs):
-            edges = edge_ref[r, blocks[g], pl.ds(t * subs + j, 1), :]
+            edges = edge_ref[r, block, pl.ds(t * subs + j, 1), :]
             src = edges & 65535
             target_one = equal(target_ids, edges >> 16)
             src_high = src // LOW
@@ -135,40 +134,47 @@
             preferred_element_type=jnp.float32,
         )
 
-    def add_block(g, convert, unroll, start):
+    def add_block(convert, unroll, g, carry):
+        ahead = shifts[0]
+        for k in range(1, len(shifts)):
+            ahead = jnp.where(g == k, shifts[k], ahead)
+        block = ring_col(lax.rem(place + ahead + cols, cols), cols)
+
         def fill_tile(part, i, carry):
-            block = count_block(g, edge_refs[part], i // tiles, i % tiles)
+            tile = count_block(block, edge_refs[part], i // tiles, i % tiles)
             top = (part * rows * tiles + i) * TILE
             top = top if unroll else pl.multiple_of(top, TILE)
             for h in range(highs):
-                counts[g % 2, pl.ds(top, TILE), h * LOW : (h + 1) * LOW] = convert(
-                    block[h * TILE : (h + 1) * TILE]
+                counts[pl.ds(top, TILE), h * LOW : (h + 1) * LOW] = convert(
+                    tile[h * TILE : (h + 1) * TILE]
                 )
             return carry
 
-        put_scaled(g)
+        for k in range(len(groups)):
+            pieces = xs[sum(groups[:k]) : sum(groups[: k + 1])]
+            pl.when(g == k)(functools.partial(put_scaled, block, pieces))
         for part in range(2):
             if unroll:
                 for i in range(rows * tiles):
                     fill_tile(part, i, 0)
             else:
                 lax.fori_loop(0, rows * tiles, functools.partial(fill_tile, part), 0)
-        added = jnp.dot(counts[g % 2], scaled[g % 2], preferred_element_type=jnp.float32)
-        total[...] = added if start else total[...] + added
+        total[...] += jnp.dot(counts[...], scaled[...], preferred_element_type=jnp.float32)
+        return carry
+
+    def rounded(tile):
+        return tile.astype(jnp.bfloat16)
+
+    def remainder(tile):
+        return (tile - tile.astype(jnp.bfloat16).astype(jnp.float32)).astype(jnp.bfloat16)
 
     scaled[...] = jnp.ones_like(scaled)
-    for g in range(len(groups)):
-        add_block(g, lambda block: block.astype(jnp.bfloat16), rows * tiles <= 4, g == 0)
+    total[...] = jnp.zeros_like(total)
+    lax.fori_loop(0, len(groups), functools.partial(add_block, rounded, rows * tiles <= 4), 0)
 
     @pl.when(jnp.max(total[:, LANES:]) >= 256.0)
     def _():
-        for g in range(len(groups)):
-            add_block(
-                g,
-                lambda block: (block - block.astype(jnp.bfloat16).astype(jnp.float32)).astype(jnp.bfloat16),
-                False,
-                False,
-            )
+        lax.fori_loop(0, len(groups), functools.partial(add_block, remainder, False), 0)
 
     if last:
         for shift in range(rows):
@@ -258,8 +264,8 @@
             ]
         )
         scratch = [
-            pltpu.VMEM((2, sums, src_rows), jnp.bfloat16),
-            pltpu.VMEM((2, src_rows, 2 * LANES), jnp.bfloat16),
+            pltpu.VMEM((sums, src_rows), jnp.bfloat16),
+            pltpu.VMEM((src_rows, 2 * LANES), jnp.bfloat16),
             pltpu.VMEM((sums, 2 * LANES), jnp.float32),
         ]
         return pl.pallas_call(

time: 46.4 us -> 48 us (1.034)
  Pallas kernels: 16.5 us -> 18.2 us
    pallas_call x3, Pallas kernels: 13.4 us -> 15.2 us  [add_blocks(): pl.pallas_call(functools.partial(sum_kernel, cols, shifts, groups, first,...]
  transfers between devices with their start and end apart: 13 -> 13, of which waited for: 6 -> 6; matrix products, arithmetic and copies ran while one was open for 0% -> 0% of each run, Pallas kernels for 29% -> 31%
where the time goes in v4:
time: 48 us; the launch traced here: 47.8 us
  Pallas kernels  18.2 us (38%)
  starting transfers between devices  17.9 us (37%)
  waiting for transfers between devices  11.5 us (24%)
    pallas_call x3, Pallas kernels, add_blocks(): pl.pallas_call(functools.partial(sum_kernel, cols, shifts, groups, first,...  15.2 us
    all_to_all x1, starting transfers between devices, body(): lax.all_to_all(packed.reshape(rows * cols, depth, LANES), ('row', 'col'),...  6.3 us
    ppermute x3, starting transfers between devices, body(): ups = lax.ppermute(ups, 'col', ahead)  5.87 us
    all_to_all x1, waiting for transfers between devices, body(): lax.all_to_all(packed.reshape(rows * cols, depth, LANES), ('row', 'col'),...  5.65 us
    ppermute x3, waiting for transfers between devices, body(): lax.ppermute(normed[shift], 'row', [(r, (r + shift) % rows) for r in rang...  3.63 us
    ppermute x3, starting transfers between devices, body(): lax.ppermute(normed[shift], 'row', [(r, (r + shift) % rows) for r in rang...  2.11 us
    ppermute x3, waiting for transfers between devices, body(): ups = lax.ppermute(ups, 'col', ahead)  2.07 us
    pallas_call x1, Pallas kernels, body(): pl.pallas_call(pack_kernel, in_specs=[pl.BlockSpec(), pl.BlockSpec(), pl....  1.89 us
  transfers between devices with their start and end apart: 13, of which 6 were waited for; matrix products, arithmetic and copies ran while one was open for 0% of the time, Pallas kernels for 31%

profile of v4, /device:TPU:0, one launch (start us, length us, event | category | flops | bytes accessed | tf_op | source)
XLA Modules:
  0.0 47.8 jit_solution(10968244456620128735)
XLA Ops:
  0.0 0.0 copy-start.2
  0.0 3.0 %collective-permute-start.1 = (bf16[1024,128]{1,0:T(8,128)(2,1)}, bf16[1024,128]{1,0:T(8,128)(2,1)S(1)}, u32[]{:S(2)}, u32[]{:S(2)}) collective-permute-start(bf16[1024,128]{1,0:T(8,128)(2,1)} %refs_3_.1), channel_id=1, source_target_pairs={{0,2},{2,4},{4,6},{6,7},{7,5},{5,3},{3,1},{1,0},{8,10},{10,12},{12... | collective-permute-start | bytes 786440 | tf_op jit(solution)/shard_map/ppermute | solution.py:285
  3.0 0.0 collective-permute-start.5
  3.0 1.9 %shard_map.64 = s32[4,8,8,128]{3,2,1,0:T(8,128)} custom-call(s32[16,512]{1,0:T(8,128)} %src_ref.1, s32[16,512]{1,0:T(8,128)} %dst_ref.1, s32[16]{0:T(128)} %bitcast.15), custom_call_target="tpu_custom_call" | custom-call | tf_op jit(solution)/shard_map/pallas_call | solution.py:231
  4.9 6.3 %all-to-all-start = ((s32[32,8,128]{2,1,0:T(8,128)}), s32[32,8,128]{2,1,0:T(8,128)S(1)}, u32[]{:S(2)}, u32[]{:S(2)}) async-start(s32[32,8,128]{2,1,0:T(8,128)} %bitcast.14), calls=%async_computation | async-start | bytes 262144 | tf_op jit(solution)/shard_map/all_to_all | solution.py:237
  11.2 0.0 collective-permute-done.1.refs_4_
  11.2 1.8 %collective-permute-start.2 = (bf16[1024,128]{1,0:T(8,128)(2,1)S(1)}, bf16[1024,128]{1,0:T(8,128)(2,1)S(1)}, u32[]{:S(2)}, u32[]{:S(2)}) collective-permute-start(bf16[1024,128]{1,0:T(8,128)(2,1)S(1)} %collective-permute-done.1.refs_4_), channel_id=1, source_target_pairs={{0,2},{2,4},{4,6},{6,7},{7,5},{5,3},{3,1},{1,0},{8,10},{10,12},{12... | collective-permute-start | bytes 786440 | tf_op jit(solution)/shard_map/ppermute | solution.py:285
  13.1 0.0 collective-permute-done.5.refs_5_
  13.1 0.3 collective-permute-start.6
  13.3 5.7 %all-to-all-done = s32[32,8,128]{2,1,0:T(8,128)S(1)} async-done(((s32[32,8,128]{2,1,0:T(8,128)}), s32[32,8,128]{2,1,0:T(8,128)S(1)}, u32[]{:S(2)}, u32[]{:S(2)}) %all-to-all-start) | async-done | bytes 131104 | tf_op jit(solution)/shard_map/all_to_all | solution.py:237
  19.0 0.1 collective-permute-start
  19.1 2.1 %collective-permute-done.2.refs_6_ = bf16[1024,128]{1,0:T(8,128)(2,1)S(1)} collective-permute-done((bf16[1024,128]{1,0:T(8,128)(2,1)S(1)}, bf16[1024,128]{1,0:T(8,128)(2,1)S(1)}, u32[]{:S(2)}, u32[]{:S(2)}) %collective-permute-start.2) | collective-permute-done | bytes 262176 | tf_op jit(solution)/shard_map/ppermute | solution.py:285
  21.1 1.0 %collective-permute-start.3 = (bf16[1024,128]{1,0:T(8,128)(2,1)S(1)}, bf16[1024,128]{1,0:T(8,128)(2,1)S(1)}, u32[]{:S(2)}, u32[]{:S(2)}) collective-permute-start(bf16[1024,128]{1,0:T(8,128)(2,1)S(1)} %collective-permute-done.2.refs_6_), channel_id=1, source_target_pairs={{0,2},{2,4},{4,6},{6,7},{7,5},{5,3},{3,1},{1,0},{8,10},{10,12},{12... | collective-permute-start | bytes 786440 | tf_op jit(solution)/shard_map/ppermute | solution.py:285
  22.2 0.1 collective-permute-done.6.refs_7_
  22.3 1.0 %collective-permute-start.7 = (bf16[1024,128]{1,0:T(8,128)(2,1)S(1)}, bf16[1024,128]{1,0:T(8,128)(2,1)S(1)}, u32[]{:S(2)}, u32[]{:S(2)}) collective-permute-start(bf16[1024,128]{1,0:T(8,128)(2,1)S(1)} %collective-permute-done.6.refs_7_), channel_id=1, source_target_pairs={{2,0},{4,2},{6,4},{7,6},{5,7},{3,5},{1,3},{0,1},{10,8},{12,10},{14... | collective-permute-start | bytes 786440 | tf_op jit(solution)/shard_map/ppermute | solution.py:286
  23.3 0.0 collective-permute-done
  23.3 0.0 copy-done.2
  23.3 9.2 %shard_map.65 = (f32[1024,128]{1,0:T(8,128)S(1)}, f32[8,128]{1,0:T(8,128)S(1)}) custom-call(s32[1]{0:T(128)} %bitcast.1.col_ref, s32[1]{0:T(128)} %bitcast.refs_0_.row_ref, s32[4,8,8,128]{3,2,1,0:T(8,128)S(1)} %bitcast.7, s32[4,8,8,128]{3,2,1,0:T(8,128)S(1)} %bitcast.11, bf16[1024,128]{1,0:T(8,128)(2,1)S(1)} %copy-done.2, ...), custom_call_target="tpu_custom_call" | custom-call | flops 16106127360 | bytes 4194304 | tf_op jit(solution)/shard_map/pallas_call | solution.py:271
  32.5 0.0 collective-permute-done.3.refs_3_
  32.5 1.2 %collective-permute-start.4 = (bf16[512,128]{1,0:T(8,128)(2,1)S(1)}, bf16[512,128]{1,0:T(8,128)(2,1)S(1)}, u32[]{:S(2)}, u32[]{:S(2)}) collective-permute-start(bf16[512,128]{1,0:T(8,128)(2,1)S(1)} %slice.8), channel_id=1, source_target_pairs={{0,2},{2,4},{4,6},{6,7},{7,5},{5,3},{3,1},{1,0},{8,10},{10,12},{12... | collective-permute-start | bytes 393224 | tf_op jit(solution)/shard_map/ppermute | solution.py:291
  33.7 0.0 collective-permute-done.7.refs_4_
  33.8 1.1 %collective-permute-start.8 = (bf16[512,128]{1,0:T(8,128)(2,1)S(1)}, bf16[512,128]{1,0:T(8,128)(2,1)S(1)}, u32[]{:S(2)}, u32[]{:S(2)}) collective-permute-start(bf16[512,128]{1,0:T(8,128)(2,1)S(1)} %slice.9), channel_id=1, source_target_pairs={{2,0},{4,2},{6,4},{7,6},{5,7},{3,5},{1,3},{0,1},{10,8},{12,10},{14... | collective-permute-start | bytes 393224 | tf_op jit(solution)/shard_map/ppermute | solution.py:292
  34.9 3.9 %shard_map.66 = (f32[1024,128]{1,0:T(8,128)S(1)}, f32[8,128]{1,0:T(8,128)S(1)}) custom-call(s32[1]{0:T(128)} %bitcast.1.col_ref, s32[1]{0:T(128)} %bitcast.refs_0_.row_ref, s32[4,8,8,128]{3,2,1,0:T(8,128)S(1)} %bitcast.8, s32[4,8,8,128]{3,2,1,0:T(8,128)S(1)} %bitcast.12, bf16[1024,128]{1,0:T(8,128)(2,1)S(1)} %collective-permute-done.3.refs_3_, ...), custom_call_target="tpu_custom_call" | custom-call | flops 6442450944 | bytes 4194304 | tf_op jit(solution)/shard_map/pallas_call | solution.py:271
  38.8 0.0 collective-permute-done.4.refs_3_
  38.8 0.0 collective-permute-done.8.refs_4_
  38.8 0.0 copy-start
  38.8 2.0 %shard_map.67 = (bf16[256,128]{1,0:T(8,128)(2,1)S(1)}, bf16[256,128]{1,0:T(8,128)(2,1)S(1)}, bf16[256,128]{1,0:T(8,128)(2,1)S(1)}, bf16[256,128]{1,0:T(8,128)(2,1)S(1)}) custom-call(s32[1]{0:T(128)} %bitcast.1.col_ref, s32[1]{0:T(128)} %bitcast.refs_0_.row_ref, s32[4,8,8,128]{3,2,1,0:T(8,128)S(1)} %bitcast.9, s32[4,8,8,128]{3,2,1,0:T(8,128)S(1)} %bitcast.13, ...), custom_call_target="tpu_custom_call" | custom-call | flops 1610612736 | bytes 4194304 | tf_op jit(solution)/shard_map/pallas_call | solution.py:271
  40.8 1.6 %collective-permute-start.10 = (bf16[256,128]{1,0:T(8,128)(2,1)S(1)}, bf16[256,128]{1,0:T(8,128)(2,1)S(1)}, u32[]{:S(2)}, u32[]{:S(2)}) collective-permute-start(bf16[256,128]{1,0:T(8,128)(2,1)S(1)} %get-tuple-element.19), channel_id=1, source_target_pairs={{0,16},{8,24},{16,0},{24,8},{1,17},{9,25},{17,1},{25,9},{2,18},{10... | collective-permute-start | bytes 196616 | tf_op jit(solution)/shard_map/ppermute | solution.py:296
  42.4 0.0 collective-permute-start.11
  42.4 0.0 copy-start.1
  42.4 0.5 %collective-permute-start.9 = (bf16[256,128]{1,0:T(8,128)(2,1)S(1)}, bf16[256,128]{1,0:T(8,128)(2,1)S(1)}, u32[]{:S(2)}, u32[]{:S(2)}) collective-permute-start(bf16[256,128]{1,0:T(8,128)(2,1)S(1)} %get-tuple-element.18), channel_id=1, source_target_pairs={{0,8},{8,16},{16,24},{24,0},{1,9},{9,17},{17,25},{25,1},{2,10},{10... | collective-permute-start | bytes 196616 | tf_op jit(solution)/shard_map/ppermute | solution.py:296
  42.9 2.2 %collective-permute-done.10.refs_2_ = bf16[256,128]{1,0:T(8,128)(2,1)S(1)} collective-permute-done((bf16[256,128]{1,0:T(8,128)(2,1)S(1)}, bf16[256,128]{1,0:T(8,128)(2,1)S(1)}, u32[]{:S(2)}, u32[]{:S(2)}) %collective-permute-start.10) | collective-permute-done | bytes 65568 | tf_op jit(solution)/shard_map/ppermute | solution.py:296
  45.2 0.4 collective-permute-done.11.refs_3_
  45.5 1.0 %collective-permute-done.9.refs_1_ = bf16[256,128]{1,0:T(8,128)(2,1)S(1)} collective-permute-done((bf16[256,128]{1,0:T(8,128)(2,1)S(1)}, bf16[256,128]{1,0:T(8,128)(2,1)S(1)}, u32[]{:S(2)}, u32[]{:S(2)}) %collective-permute-start.9) | collective-permute-done | bytes 65568 | tf_op jit(solution)/shard_map/ppermute | solution.py:296
  46.6 0.0 copy-done
  46.6 0.0 copy-done.1
  46.6 1.2 %shard_map.68 = bf16[256,512]{1,0:T(8,128)(2,1)} custom-call(s32[1]{0:T(128)} %bitcast.refs_0_.row_ref, bf16[256,128]{1,0:T(8,128)(2,1)S(1)} %get-tuple-element.17.refs_0_, bf16[256,128]{1,0:T(8,128)(2,1)S(1)} %collective-permute-done.9.refs_1_, bf16[256,128]{1,0:T(8,128)(2,1)S(1)} %collective-permute-done.10.refs_2_, ...), custom_call_target="tpu_custom_call" | custom-call | tf_op jit(solution)/shard_map/pallas_call | solution.py:300
  (2 shorter events, 0.0 us)
Async XLA Ops:
  0.0 23.3 %copy-start.2 = (bf16[1024,128]{1,0:T(8,128)(2,1)S(1)}, bf16[1024,128]{1,0:T(8,128)(2,1)}, u32[]{:S(2)}) copy-start(bf16[1024,128]{1,0:T(8,128)(2,1)} %refs_3_.1) | copy-start | bytes 786436
  0.0 11.2 %collective-permute-start.1 = (bf16[1024,128]{1,0:T(8,128)(2,1)}, bf16[1024,128]{1,0:T(8,128)(2,1)S(1)}, u32[]{:S(2)}, u32[]{:S(2)}) collective-permute-start(bf16[1024,128]{1,0:T(8,128)(2,1)} %refs_3_.1), channel_id=1, source_target_pairs={{0,2},{2,4},{4,6},{6,7},{7,5},{5,3},{3,1},{1,0},{8,10},{10,12},{12... | collective-permute-start | bytes 786440 | tf_op jit(solution)/shard_map/ppermute | solution.py:285
  3.0 10.0 %collective-permute-start.5 = (bf16[1024,128]{1,0:T(8,128)(2,1)}, bf16[1024,128]{1,0:T(8,128)(2,1)S(1)}, u32[]{:S(2)}, u32[]{:S(2)}) collective-permute-start(bf16[1024,128]{1,0:T(8,128)(2,1)} %refs_3_.1), channel_id=1, source_target_pairs={{2,0},{4,2},{6,4},{7,6},{5,7},{3,5},{1,3},{0,1},{10,8},{12,10},{14... | collective-permute-start | bytes 786440 | tf_op jit(solution)/shard_map/ppermute | solution.py:286
  4.9 14.1 %all-to-all-start = ((s32[32,8,128]{2,1,0:T(8,128)}), s32[32,8,128]{2,1,0:T(8,128)S(1)}, u32[]{:S(2)}, u32[]{:S(2)}) async-start(s32[32,8,128]{2,1,0:T(8,128)} %bitcast.14), calls=%async_computation | async-start | bytes 262144 | tf_op jit(solution)/shard_map/all_to_all | solution.py:237
  11.2 9.9 %collective-permute-start.2 = (bf16[1024,128]{1,0:T(8,128)(2,1)S(1)}, bf16[1024,128]{1,0:T(8,128)(2,1)S(1)}, u32[]{:S(2)}, u32[]{:S(2)}) collective-permute-start(bf16[1024,128]{1,0:T(8,128)(2,1)S(1)} %collective-permute-done.1.refs_4_), channel_id=1, source_target_pairs={{0,2},{2,4},{4,6},{6,7},{7,5},{5,3},{3,1},{1,0},{8,10},{10,12},{12... | collective-permute-start | bytes 786440 | tf_op jit(solution)/shard_map/ppermute | solution.py:285
  13.1 9.3 %collective-permute-start.6 = (bf16[1024,128]{1,0:T(8,128)(2,1)S(1)}, bf16[1024,128]{1,0:T(8,128)(2,1)S(1)}, u32[]{:S(2)}, u32[]{:S(2)}) collective-permute-start(bf16[1024,128]{1,0:T(8,128)(2,1)S(1)} %collective-permute-done.5.refs_5_), channel_id=1, source_target_pairs={{2,0},{4,2},{6,4},{7,6},{5,7},{3,5},{1,3},{0,1},{10,8},{12,10},{14... | collective-permute-start | bytes 786440 | tf_op jit(solution)/shard_map/ppermute | solution.py:286
  19.0 4.3 %collective-permute-start = (s32[32,8,128]{2,1,0:T(8,128)S(1)}, s32[32,8,128]{2,1,0:T(8,128)S(1)}, u32[]{:S(2)}, u32[]{:S(2)}) collective-permute-start(s32[32,8,128]{2,1,0:T(8,128)S(1)} %all-to-all-done), channel_id=1, source_target_pairs={{0,8},{8,0},{16,24},{24,16},{1,9},{9,1},{17,25},{25,17},{2,10},{10... | collective-permute-start | bytes 393224 | tf_op jit(solution)/shard_map/ppermute | solution.py:244
  21.1 11.4 %collective-permute-start.3 = (bf16[1024,128]{1,0:T(8,128)(2,1)S(1)}, bf16[1024,128]{1,0:T(8,128)(2,1)S(1)}, u32[]{:S(2)}, u32[]{:S(2)}) collective-permute-start(bf16[1024,128]{1,0:T(8,128)(2,1)S(1)} %collective-permute-done.2.refs_6_), channel_id=1, source_target_pairs={{0,2},{2,4},{4,6},{6,7},{7,5},{5,3},{3,1},{1,0},{8,10},{10,12},{12... | collective-permute-start | bytes 786440 | tf_op jit(solution)/shard_map/ppermute | solution.py:285
  22.3 11.4 %collective-permute-start.7 = (bf16[1024,128]{1,0:T(8,128)(2,1)S(1)}, bf16[1024,128]{1,0:T(8,128)(2,1)S(1)}, u32[]{:S(2)}, u32[]{:S(2)}) collective-permute-start(bf16[1024,128]{1,0:T(8,128)(2,1)S(1)} %collective-permute-done.6.refs_7_), channel_id=1, source_target_pairs={{2,0},{4,2},{6,4},{7,6},{5,7},{3,5},{1,3},{0,1},{10,8},{12,10},{14... | collective-permute-start | bytes 786440 | tf_op jit(solution)/shard_map/ppermute | solution.py:286
  32.5 6.3 %collective-permute-start.4 = (bf16[512,128]{1,0:T(8,128)(2,1)S(1)}, bf16[512,128]{1,0:T(8,128)(2,1)S(1)}, u32[]{:S(2)}, u32[]{:S(2)}) collective-permute-start(bf16[512,128]{1,0:T(8,128)(2,1)S(1)} %slice.8), channel_id=1, source_target_pairs={{0,2},{2,4},{4,6},{6,7},{7,5},{5,3},{3,1},{1,0},{8,10},{10,12},{12... | collective-permute-start | bytes 393224 | tf_op jit(solution)/shard_map/ppermute | solution.py:291
  33.8 5.0 %collective-permute-start.8 = (bf16[512,128]{1,0:T(8,128)(2,1)S(1)}, bf16[512,128]{1,0:T(8,128)(2,1)S(1)}, u32[]{:S(2)}, u32[]{:S(2)}) collective-permute-start(bf16[512,128]{1,0:T(8,128)(2,1)S(1)} %slice.9), channel_id=1, source_target_pairs={{2,0},{4,2},{6,4},{7,6},{5,7},{3,5},{1,3},{0,1},{10,8},{12,10},{14... | collective-permute-start | bytes 393224 | tf_op jit(solution)/shard_map/ppermute | solution.py:292
  38.8 7.8 %copy-start = (bf16[512,512]{1,0:T(8,128)(2,1)S(1)}, bf16[512,512]{1,0:T(8,128)(2,1)}, u32[]{:S(2)}) copy-start(bf16[512,512]{1,0:T(8,128)(2,1)} %refs_4_.1) | copy-start | bytes 1572868
  40.8 4.3 %collective-permute-start.10 = (bf16[256,128]{1,0:T(8,128)(2,1)S(1)}, bf16[256,128]{1,0:T(8,128)(2,1)S(1)}, u32[]{:S(2)}, u32[]{:S(2)}) collective-permute-start(bf16[256,128]{1,0:T(8,128)(2,1)S(1)} %get-tuple-element.19), channel_id=1, source_target_pairs={{0,16},{8,24},{16,0},{24,8},{1,17},{9,25},{17,1},{25,9},{2,18},{10... | collective-permute-start | bytes 196616 | tf_op jit(solution)/shard_map/ppermute | solution.py:296
  42.4 3.1 %collective-permute-start.11 = (bf16[256,128]{1,0:T(8,128)(2,1)S(1)}, bf16[256,128]{1,0:T(8,128)(2,1)S(1)}, u32[]{:S(2)}, u32[]{:S(2)}) collective-permute-start(bf16[256,128]{1,0:T(8,128)(2,1)S(1)} %get-tuple-element.20), channel_id=1, source_target_pairs={{0,24},{8,0},{16,8},{24,16},{1,25},{9,1},{17,9},{25,17},{2,26},{10... | collective-permute-start | bytes 196616 | tf_op jit(solution)/shard_map/ppermute | solution.py:296
  42.4 4.1 %copy-start.1 = (f32[512]{0:T(512)S(1)}, f32[512]{0:T(512)}, u32[]{:S(2)}) copy-start(f32[512]{0:T(512)} %param.8) | copy-start | bytes 6148
  42.4 4.1 %collective-permute-start.9 = (bf16[256,128]{1,0:T(8,128)(2,1)S(1)}, bf16[256,128]{1,0:T(8,128)(2,1)S(1)}, u32[]{:S(2)}, u32[]{:S(2)}) collective-permute-start(bf16[256,128]{1,0:T(8,128)(2,1)S(1)} %get-tuple-element.18), channel_id=1, source_target_pairs={{0,8},{8,16},{16,24},{24,0},{1,9},{9,17},{17,25},{25,1},{2,10},{10... | collective-permute-start | bytes 196616 | tf_op jit(solution)/shard_map/ppermute | solution.py:296

commit v5 on v2

--- a/solution.py
+++ b/solution.py
@@ -93,7 +93,8 @@
     subs = own // tiles
     odd = lax.rem(row_ref[0], 2)
     place = ring_place(col_ref[0], cols)
-    blocks = [ring_col(lax.rem(place + shift + cols, cols), cols) for shift in shifts]
+    sign = 1 - 2 * lax.rem(place, 2)
+    blocks = [ring_col(lax.rem(place + sign * shift + cols, cols), cols) for shift in shifts]
     diagonal = lax.broadcasted_iota(jnp.int32, (LANES, LANES), 0) == lax.broadcasted_iota(
         jnp.int32, (LANES, LANES), 1
     )
@@ -172,7 +173,7 @@
 
     if last:
         for shift in range(rows):
-            r = lax.rem(row_ref[0] + shift, rows)
+            r = row_ref[0] ^ shift
             for part in range(2):
                 for t in range(tiles):
                     i = (part * rows + r) * tiles + t
@@ -201,7 +202,7 @@
     rows, width = len(x_refs), x_refs[0].shape[1]
     projected = None
     for shift, x_ref in enumerate(x_refs):
-        top = pl.multiple_of(lax.rem(row_ref[0] - shift + rows, rows) * width, width)
+        top = pl.multiple_of((row_ref[0] ^ shift) * width, width)
         part = jnp.dot(x_ref[...], weight_ref[pl.ds(top, width), :], preferred_element_type=jnp.float32)
         projected = part if projected is None else projected + part
     copy.wait()
@@ -217,8 +218,8 @@
     own_nodes = tiles // cols * TILE
     sums = rows * own_nodes
     order = [ring_col_of(place, cols) for place in range(cols)]
-    ahead = [(order[p], order[(p + 1) % cols]) for p in range(cols)]
-    back = [(order[(p + 1) % cols], order[p]) for p in range(cols)]
+    near = [(order[p], order[p ^ 1]) for p in range(cols)]
+    next_near = [(order[p], order[((p + 1) % cols ^ 1) - 1]) for p in range(cols)]
     half = src_rows // 2
 
     depth = (own_rows + degree_rows) // 2
@@ -235,7 +236,7 @@
         concat_axis=0,
         tiled=True,
     )
-    other = lax.ppermute(edges, "row", [(r, r + 1 - 2 * (r % 2)) for r in range(rows)])
+    other = lax.ppermute(edges, "row", [(r, r ^ 1) for r in range(rows)])
     edges = [half.reshape(rows, cols, depth, LANES) for half in (edges, other)]
     col = lax.axis_index("col").astype(jnp.int32).reshape(1)
     row = lax.axis_index("row").astype(jnp.int32).reshape(1)
@@ -273,21 +274,20 @@
         )(col, row, *edges, *operands)
 
     block_flops = 2 * sums * src_rows * (2 * LANES + cap)
-    ups = downs = features
+    here = there = features
     total, waiting = None, [(0, [features])]
     for hop in range(1, cols // 2):
-        ups = lax.ppermute(ups, "col", ahead)
-        downs = lax.ppermute(downs, "col", back)
-        waiting += [(-hop, [ups]), (hop, [downs])]
+        here, there = lax.ppermute(there, "col", near), lax.ppermute(here, "col", next_near)
+        waiting += [(hop, [here]), (-hop, [there])]
         if hop > 1:
             total = add_blocks(total, waiting, False, 2 * len(waiting) * block_flops)
             waiting = []
-    ups = lax.ppermute(ups[:half], "col", ahead)
-    downs = lax.ppermute(downs[half:], "col", back)
-    waiting.append((cols // 2, [ups, downs]))
+    upper = lax.ppermute(there[:half], "col", near)
+    lower = lax.ppermute(here[half:], "col", next_near)
+    waiting.append((cols // 2, [upper, lower]))
     normed = add_blocks(total, waiting, True, block_flops)
     normed = [normed[0]] + [
-        lax.ppermute(normed[shift], "row", [(r, (r + shift) % rows) for r in range(rows)])
+        lax.ppermute(normed[shift], "row", [(r, r ^ shift) for r in range(rows)])
         for shift in range(1, rows)
     ]
     operands = [*normed, weight]

time: 46.4 us -> 46.4 us (level)
  starting transfers between devices: 17.9 us -> 18.7 us
  waiting for transfers between devices: 11.5 us -> 10.8 us
    ppermute x12, starting transfers between devices: 11.6 us -> 14.9 us  [the longest x3 5.9 us: body(): lax.ppermute(here, 'col', next_near)]
    all_to_all x1, starting transfers between devices: 6.3 us -> 3.82 us  [body(): lax.all_to_all(packed.reshape(rows * cols, depth, LANES), ('row', 'col'),...]
    all_to_all x1, waiting for transfers between devices: 5.65 us -> 4.43 us  [body(): lax.all_to_all(packed.reshape(rows * cols, depth, LANES), ('row', 'col'),...]
    ppermute x12, waiting for transfers between devices: 5.85 us -> 6.34 us  [the longest x3 3.53 us: body(): lax.ppermute(normed[shift], 'row', [(r, r ^ shift) for r in range(rows)])]
  transfers between devices with their start and end apart: 13 -> 13, of which waited for: 6 -> 5; matrix products, arithmetic and copies ran while one was open for 0% -> 0% of each run, Pallas kernels for 29% -> 29%
where the time goes in v5:
time: 46.4 us; the launch traced here: 46.2 us
  starting transfers between devices  18.7 us (40%)
  Pallas kernels  16.5 us (36%)
  waiting for transfers between devices  10.8 us (23%)
    pallas_call x3, Pallas kernels, add_blocks(): pl.pallas_call(functools.partial(sum_kernel, cols, shifts, groups, first,...  13.4 us
    ppermute x3, starting transfers between devices, body(): lax.ppermute(here, 'col', next_near)  5.9 us
    ppermute x3, starting transfers between devices, body(): lax.ppermute(there, 'col', near)  4.98 us
    all_to_all x1, waiting for transfers between devices, body(): lax.all_to_all(packed.reshape(rows * cols, depth, LANES), ('row', 'col'),...  4.43 us
    all_to_all x1, starting transfers between devices, body(): lax.all_to_all(packed.reshape(rows * cols, depth, LANES), ('row', 'col'),...  3.82 us
    ppermute x3, waiting for transfers between devices, body(): lax.ppermute(normed[shift], 'row', [(r, r ^ shift) for r in range(rows)])  3.53 us
    ppermute x3, waiting for transfers between devices, body(): lax.ppermute(there, 'col', near)  2.74 us
    ppermute x3, starting transfers between devices, body(): lax.ppermute(normed[shift], 'row', [(r, r ^ shift) for r in range(rows)])  2.21 us
  transfers between devices with their start and end apart: 13, of which 5 were waited for; matrix products, arithmetic and copies ran while one was open for 0% of the time, Pallas kernels for 29%

profile of v5, /device:TPU:0, one launch (start us, length us, event | category | flops | bytes accessed | tf_op | source)
XLA Modules:
  0.0 46.2 jit_solution(7945103994875135014)
XLA Ops:
  0.0 0.0 copy-start.2
  0.0 3.0 %collective-permute-start.1 = (bf16[1024,128]{1,0:T(8,128)(2,1)}, bf16[1024,128]{1,0:T(8,128)(2,1)S(1)}, u32[]{:S(2)}, u32[]{:S(2)}) collective-permute-start(bf16[1024,128]{1,0:T(8,128)(2,1)} %refs_3_.1), channel_id=1, source_target_pairs={{0,1},{2,4},{4,2},{6,7},{7,6},{5,3},{3,5},{1,0},{8,9},{10,12},{12,... | collective-permute-start | bytes 786440 | tf_op jit(solution)/shard_map/ppermute | solution.py:280
  3.0 1.6 %collective-permute-start.5 = (bf16[1024,128]{1,0:T(8,128)(2,1)}, bf16[1024,128]{1,0:T(8,128)(2,1)S(1)}, u32[]{:S(2)}, u32[]{:S(2)}) collective-permute-start(bf16[1024,128]{1,0:T(8,128)(2,1)} %refs_3_.1), channel_id=1, source_target_pairs={{0,2},{2,0},{4,6},{6,4},{7,5},{5,7},{3,1},{1,3},{8,10},{10,8},{12,... | collective-permute-start | bytes 786440 | tf_op jit(solution)/shard_map/ppermute | solution.py:280
  4.6 1.9 %shard_map.64 = s32[4,8,8,128]{3,2,1,0:T(8,128)} custom-call(s32[16,512]{1,0:T(8,128)} %src_ref.1, s32[16,512]{1,0:T(8,128)} %dst_ref.1, s32[16]{0:T(128)} %bitcast.15), custom_call_target="tpu_custom_call" | custom-call | tf_op jit(solution)/shard_map/pallas_call | solution.py:226
  6.5 3.8 %all-to-all-start = ((s32[32,8,128]{2,1,0:T(8,128)}), s32[32,8,128]{2,1,0:T(8,128)S(1)}, u32[]{:S(2)}, u32[]{:S(2)}) async-start(s32[32,8,128]{2,1,0:T(8,128)} %bitcast.14), calls=%async_computation | async-start | bytes 262144 | tf_op jit(solution)/shard_map/all_to_all | solution.py:232
  10.3 0.0 collective-permute-done.1.refs_5_
  10.3 1.8 %collective-permute-start.2 = (bf16[1024,128]{1,0:T(8,128)(2,1)S(1)}, bf16[1024,128]{1,0:T(8,128)(2,1)S(1)}, u32[]{:S(2)}, u32[]{:S(2)}) collective-permute-start(bf16[1024,128]{1,0:T(8,128)(2,1)S(1)} %collective-permute-done.1.refs_5_), channel_id=1, source_target_pairs={{0,2},{2,0},{4,6},{6,4},{7,5},{5,7},{3,1},{1,3},{8,10},{10,8},{12,... | collective-permute-start | bytes 786440 | tf_op jit(solution)/shard_map/ppermute | solution.py:280
  12.2 0.0 collective-permute-done.5.refs_4_
  12.2 1.5 %collective-permute-start.6 = (bf16[1024,128]{1,0:T(8,128)(2,1)S(1)}, bf16[1024,128]{1,0:T(8,128)(2,1)S(1)}, u32[]{:S(2)}, u32[]{:S(2)}) collective-permute-start(bf16[1024,128]{1,0:T(8,128)(2,1)S(1)} %collective-permute-done.5.refs_4_), channel_id=1, source_target_pairs={{0,1},{2,4},{4,2},{6,7},{7,6},{5,3},{3,5},{1,0},{8,9},{10,12},{12,... | collective-permute-start | bytes 786440 | tf_op jit(solution)/shard_map/ppermute | solution.py:280
  13.6 4.4 %all-to-all-done = s32[32,8,128]{2,1,0:T(8,128)S(1)} async-done(((s32[32,8,128]{2,1,0:T(8,128)}), s32[32,8,128]{2,1,0:T(8,128)S(1)}, u32[]{:S(2)}, u32[]{:S(2)}) %all-to-all-start) | async-done | bytes 131104 | tf_op jit(solution)/shard_map/all_to_all | solution.py:232
  18.1 0.1 collective-permute-start
  18.2 2.7 %collective-permute-done.2.refs_6_ = bf16[1024,128]{1,0:T(8,128)(2,1)S(1)} collective-permute-done((bf16[1024,128]{1,0:T(8,128)(2,1)S(1)}, bf16[1024,128]{1,0:T(8,128)(2,1)S(1)}, u32[]{:S(2)}, u32[]{:S(2)}) %collective-permute-start.2) | collective-permute-done | bytes 262176 | tf_op jit(solution)/shard_map/ppermute | solution.py:280
  20.9 1.5 %collective-permute-start.3 = (bf16[1024,128]{1,0:T(8,128)(2,1)S(1)}, bf16[1024,128]{1,0:T(8,128)(2,1)S(1)}, u32[]{:S(2)}, u32[]{:S(2)}) collective-permute-start(bf16[1024,128]{1,0:T(8,128)(2,1)S(1)} %collective-permute-done.2.refs_6_), channel_id=1, source_target_pairs={{0,1},{2,4},{4,2},{6,7},{7,6},{5,3},{3,5},{1,0},{8,9},{10,12},{12,... | collective-permute-start | bytes 786440 | tf_op jit(solution)/shard_map/ppermute | solution.py:280
  22.4 0.0 collective-permute-done.6.refs_7_
  22.4 1.5 %collective-permute-start.7 = (bf16[1024,128]{1,0:T(8,128)(2,1)S(1)}, bf16[1024,128]{1,0:T(8,128)(2,1)S(1)}, u32[]{:S(2)}, u32[]{:S(2)}) collective-permute-start(bf16[1024,128]{1,0:T(8,128)(2,1)S(1)} %collective-permute-done.6.refs_7_), channel_id=1, source_target_pairs={{0,2},{2,0},{4,6},{6,4},{7,5},{5,7},{3,1},{1,3},{8,10},{10,8},{12,... | collective-permute-start | bytes 786440 | tf_op jit(solution)/shard_map/ppermute | solution.py:280
  23.9 0.0 collective-permute-done
  23.9 0.0 copy-done.2
  23.9 7.5 %shard_map.65 = (f32[1024,128]{1,0:T(8,128)S(1)}, f32[8,128]{1,0:T(8,128)S(1)}) custom-call(s32[1]{0:T(128)} %bitcast.1.col_ref, s32[1]{0:T(128)} %bitcast.refs_0_.row_ref, s32[4,8,8,128]{3,2,1,0:T(8,128)S(1)} %bitcast.7, s32[4,8,8,128]{3,2,1,0:T(8,128)S(1)} %bitcast.11, bf16[1024,128]{1,0:T(8,128)(2,1)S(1)} %copy-done.2, ...), custom_call_target="tpu_custom_call" | custom-call | flops 16106127360 | bytes 4194304 | tf_op jit(solution)/shard_map/pallas_call | solution.py:266
  31.4 0.0 collective-permute-done.3.refs_4_
  31.4 0.6 %collective-permute-start.4 = (bf16[512,128]{1,0:T(8,128)(2,1)S(1)}, bf16[512,128]{1,0:T(8,128)(2,1)S(1)}, u32[]{:S(2)}, u32[]{:S(2)}) collective-permute-start(bf16[512,128]{1,0:T(8,128)(2,1)S(1)} %slice.8), channel_id=1, source_target_pairs={{0,2},{2,0},{4,6},{6,4},{7,5},{5,7},{3,1},{1,3},{8,10},{10,8},{12,... | collective-permute-start | bytes 393224 | tf_op jit(solution)/shard_map/ppermute | solution.py:285
  32.0 0.0 collective-permute-done.7.refs_3_
  32.0 1.1 %collective-permute-start.8 = (bf16[512,128]{1,0:T(8,128)(2,1)S(1)}, bf16[512,128]{1,0:T(8,128)(2,1)S(1)}, u32[]{:S(2)}, u32[]{:S(2)}) collective-permute-start(bf16[512,128]{1,0:T(8,128)(2,1)S(1)} %slice.9), channel_id=1, source_target_pairs={{0,1},{2,4},{4,2},{6,7},{7,6},{5,3},{3,5},{1,0},{8,9},{10,12},{12,... | collective-permute-start | bytes 393224 | tf_op jit(solution)/shard_map/ppermute | solution.py:286
  33.1 3.9 %shard_map.66 = (f32[1024,128]{1,0:T(8,128)S(1)}, f32[8,128]{1,0:T(8,128)S(1)}) custom-call(s32[1]{0:T(128)} %bitcast.1.col_ref, s32[1]{0:T(128)} %bitcast.refs_0_.row_ref, s32[4,8,8,128]{3,2,1,0:T(8,128)S(1)} %bitcast.8, s32[4,8,8,128]{3,2,1,0:T(8,128)S(1)} %bitcast.12, bf16[1024,128]{1,0:T(8,128)(2,1)S(1)} %collective-permute-done.7.refs_3_, ...), custom_call_target="tpu_custom_call" | custom-call | flops 6442450944 | bytes 4194304 | tf_op jit(solution)/shard_map/pallas_call | solution.py:266
  37.0 0.0 collective-permute-done.4.refs_3_
  37.0 0.1 collective-permute-done.8.refs_4_
  37.1 0.0 copy-start
  37.1 2.0 %shard_map.67 = (bf16[256,128]{1,0:T(8,128)(2,1)S(1)}, bf16[256,128]{1,0:T(8,128)(2,1)S(1)}, bf16[256,128]{1,0:T(8,128)(2,1)S(1)}, bf16[256,128]{1,0:T(8,128)(2,1)S(1)}) custom-call(s32[1]{0:T(128)} %bitcast.1.col_ref, s32[1]{0:T(128)} %bitcast.refs_0_.row_ref, s32[4,8,8,128]{3,2,1,0:T(8,128)S(1)} %bitcast.9, s32[4,8,8,128]{3,2,1,0:T(8,128)S(1)} %bitcast.13, ...), custom_call_target="tpu_custom_call" | custom-call | flops 1610612736 | bytes 4194304 | tf_op jit(solution)/shard_map/pallas_call | solution.py:266
  39.1 1.5 %collective-permute-start.10 = (bf16[256,128]{1,0:T(8,128)(2,1)S(1)}, bf16[256,128]{1,0:T(8,128)(2,1)S(1)}, u32[]{:S(2)}, u32[]{:S(2)}) collective-permute-start(bf16[256,128]{1,0:T(8,128)(2,1)S(1)} %get-tuple-element.19), channel_id=1, source_target_pairs={{0,16},{8,24},{16,0},{24,8},{1,17},{9,25},{17,1},{25,9},{2,18},{10... | collective-permute-start | bytes 196616 | tf_op jit(solution)/shard_map/ppermute | solution.py:290
  40.6 0.0 collective-permute-start.11
  40.6 0.0 copy-start.1
  40.6 0.7 %collective-permute-start.9 = (bf16[256,128]{1,0:T(8,128)(2,1)S(1)}, bf16[256,128]{1,0:T(8,128)(2,1)S(1)}, u32[]{:S(2)}, u32[]{:S(2)}) collective-permute-start(bf16[256,128]{1,0:T(8,128)(2,1)S(1)} %get-tuple-element.18), channel_id=1, source_target_pairs={{0,8},{8,0},{16,24},{24,16},{1,9},{9,1},{17,25},{25,17},{2,10},{10... | collective-permute-start | bytes 196616 | tf_op jit(solution)/shard_map/ppermute | solution.py:290
  41.3 2.1 %collective-permute-done.10.refs_2_ = bf16[256,128]{1,0:T(8,128)(2,1)S(1)} collective-permute-done((bf16[256,128]{1,0:T(8,128)(2,1)S(1)}, bf16[256,128]{1,0:T(8,128)(2,1)S(1)}, u32[]{:S(2)}, u32[]{:S(2)}) %collective-permute-start.10) | collective-permute-done | bytes 65568 | tf_op jit(solution)/shard_map/ppermute | solution.py:290
  43.4 1.4 %collective-permute-done.11.refs_3_ = bf16[256,128]{1,0:T(8,128)(2,1)S(1)} collective-permute-done((bf16[256,128]{1,0:T(8,128)(2,1)S(1)}, bf16[256,128]{1,0:T(8,128)(2,1)S(1)}, u32[]{:S(2)}, u32[]{:S(2)}) %collective-permute-start.11) | collective-permute-done | bytes 65568 | tf_op jit(solution)/shard_map/ppermute | solution.py:290
  44.8 0.0 collective-permute-done.9.refs_1_
  44.8 0.0 copy-done
  44.8 0.0 copy-done.1
  44.8 1.2 %shard_map.68 = bf16[256,512]{1,0:T(8,128)(2,1)} custom-call(s32[1]{0:T(128)} %bitcast.refs_0_.row_ref, bf16[256,128]{1,0:T(8,128)(2,1)S(1)} %get-tuple-element.17.refs_0_, bf16[256,128]{1,0:T(8,128)(2,1)S(1)} %collective-permute-done.9.refs_1_, bf16[256,128]{1,0:T(8,128)(2,1)S(1)} %collective-permute-done.10.refs_2_, ...), custom_call_target="tpu_custom_call" | custom-call | tf_op jit(solution)/shard_map/pallas_call | solution.py:294
  (2 shorter events, 0.0 us)
Async XLA Ops:
  0.0 23.9 %copy-start.2 = (bf16[1024,128]{1,0:T(8,128)(2,1)S(1)}, bf16[1024,128]{1,0:T(8,128)(2,1)}, u32[]{:S(2)}) copy-start(bf16[1024,128]{1,0:T(8,128)(2,1)} %refs_3_.1) | copy-start | bytes 786436
  0.0 10.3 %collective-permute-start.1 = (bf16[1024,128]{1,0:T(8,128)(2,1)}, bf16[1024,128]{1,0:T(8,128)(2,1)S(1)}, u32[]{:S(2)}, u32[]{:S(2)}) collective-permute-start(bf16[1024,128]{1,0:T(8,128)(2,1)} %refs_3_.1), channel_id=1, source_target_pairs={{0,1},{2,4},{4,2},{6,7},{7,6},{5,3},{3,5},{1,0},{8,9},{10,12},{12,... | collective-permute-start | bytes 786440 | tf_op jit(solution)/shard_map/ppermute | solution.py:280
  3.0 9.2 %collective-permute-start.5 = (bf16[1024,128]{1,0:T(8,128)(2,1)}, bf16[1024,128]{1,0:T(8,128)(2,1)S(1)}, u32[]{:S(2)}, u32[]{:S(2)}) collective-permute-start(bf16[1024,128]{1,0:T(8,128)(2,1)} %refs_3_.1), channel_id=1, source_target_pairs={{0,2},{2,0},{4,6},{6,4},{7,5},{5,7},{3,1},{1,3},{8,10},{10,8},{12,... | collective-permute-start | bytes 786440 | tf_op jit(solution)/shard_map/ppermute | solution.py:280
  6.5 11.6 %all-to-all-start = ((s32[32,8,128]{2,1,0:T(8,128)}), s32[32,8,128]{2,1,0:T(8,128)S(1)}, u32[]{:S(2)}, u32[]{:S(2)}) async-start(s32[32,8,128]{2,1,0:T(8,128)} %bitcast.14), calls=%async_computation | async-start | bytes 262144 | tf_op jit(solution)/shard_map/all_to_all | solution.py:232
  10.3 10.6 %collective-permute-start.2 = (bf16[1024,128]{1,0:T(8,128)(2,1)S(1)}, bf16[1024,128]{1,0:T(8,128)(2,1)S(1)}, u32[]{:S(2)}, u32[]{:S(2)}) collective-permute-start(bf16[1024,128]{1,0:T(8,128)(2,1)S(1)} %collective-permute-done.1.refs_5_), channel_id=1, source_target_pairs={{0,2},{2,0},{4,6},{6,4},{7,5},{5,7},{3,1},{1,3},{8,10},{10,8},{12,... | collective-permute-start | bytes 786440 | tf_op jit(solution)/shard_map/ppermute | solution.py:280
  12.2 10.2 %collective-permute-start.6 = (bf16[1024,128]{1,0:T(8,128)(2,1)S(1)}, bf16[1024,128]{1,0:T(8,128)(2,1)S(1)}, u32[]{:S(2)}, u32[]{:S(2)}) collective-permute-start(bf16[1024,128]{1,0:T(8,128)(2,1)S(1)} %collective-permute-done.5.refs_4_), channel_id=1, source_target_pairs={{0,1},{2,4},{4,2},{6,7},{7,6},{5,3},{3,5},{1,0},{8,9},{10,12},{12,... | collective-permute-start | bytes 786440 | tf_op jit(solution)/shard_map/ppermute | solution.py:280
  18.1 5.8 %collective-permute-start = (s32[32,8,128]{2,1,0:T(8,128)S(1)}, s32[32,8,128]{2,1,0:T(8,128)S(1)}, u32[]{:S(2)}, u32[]{:S(2)}) collective-permute-start(s32[32,8,128]{2,1,0:T(8,128)S(1)} %all-to-all-done), channel_id=1, source_target_pairs={{0,8},{8,0},{16,24},{24,16},{1,9},{9,1},{17,25},{25,17},{2,10},{10... | collective-permute-start | bytes 393224 | tf_op jit(solution)/shard_map/ppermute | solution.py:239
  20.9 10.5 %collective-permute-start.3 = (bf16[1024,128]{1,0:T(8,128)(2,1)S(1)}, bf16[1024,128]{1,0:T(8,128)(2,1)S(1)}, u32[]{:S(2)}, u32[]{:S(2)}) collective-permute-start(bf16[1024,128]{1,0:T(8,128)(2,1)S(1)} %collective-permute-done.2.refs_6_), channel_id=1, source_target_pairs={{0,1},{2,4},{4,2},{6,7},{7,6},{5,3},{3,5},{1,0},{8,9},{10,12},{12,... | collective-permute-start | bytes 786440 | tf_op jit(solution)/shard_map/ppermute | solution.py:280
  22.4 9.6 %collective-permute-start.7 = (bf16[1024,128]{1,0:T(8,128)(2,1)S(1)}, bf16[1024,128]{1,0:T(8,128)(2,1)S(1)}, u32[]{:S(2)}, u32[]{:S(2)}) collective-permute-start(bf16[1024,128]{1,0:T(8,128)(2,1)S(1)} %collective-permute-done.6.refs_7_), channel_id=1, source_target_pairs={{0,2},{2,0},{4,6},{6,4},{7,5},{5,7},{3,1},{1,3},{8,10},{10,8},{12,... | collective-permute-start | bytes 786440 | tf_op jit(solution)/shard_map/ppermute | solution.py:280
  31.4 5.6 %collective-permute-start.4 = (bf16[512,128]{1,0:T(8,128)(2,1)S(1)}, bf16[512,128]{1,0:T(8,128)(2,1)S(1)}, u32[]{:S(2)}, u32[]{:S(2)}) collective-permute-start(bf16[512,128]{1,0:T(8,128)(2,1)S(1)} %slice.8), channel_id=1, source_target_pairs={{0,2},{2,0},{4,6},{6,4},{7,5},{5,7},{3,1},{1,3},{8,10},{10,8},{12,... | collective-permute-start | bytes 393224 | tf_op jit(solution)/shard_map/ppermute | solution.py:285
  32.0 5.0 %collective-permute-start.8 = (bf16[512,128]{1,0:T(8,128)(2,1)S(1)}, bf16[512,128]{1,0:T(8,128)(2,1)S(1)}, u32[]{:S(2)}, u32[]{:S(2)}) collective-permute-start(bf16[512,128]{1,0:T(8,128)(2,1)S(1)} %slice.9), channel_id=1, source_target_pairs={{0,1},{2,4},{4,2},{6,7},{7,6},{5,3},{3,5},{1,0},{8,9},{10,12},{12,... | collective-permute-start | bytes 393224 | tf_op jit(solution)/shard_map/ppermute | solution.py:286
  37.1 7.7 %copy-start = (bf16[512,512]{1,0:T(8,128)(2,1)S(1)}, bf16[512,512]{1,0:T(8,128)(2,1)}, u32[]{:S(2)}) copy-start(bf16[512,512]{1,0:T(8,128)(2,1)} %refs_4_.1) | copy-start | bytes 1572868
  39.1 4.3 %collective-permute-start.10 = (bf16[256,128]{1,0:T(8,128)(2,1)S(1)}, bf16[256,128]{1,0:T(8,128)(2,1)S(1)}, u32[]{:S(2)}, u32[]{:S(2)}) collective-permute-start(bf16[256,128]{1,0:T(8,128)(2,1)S(1)} %get-tuple-element.19), channel_id=1, source_target_pairs={{0,16},{8,24},{16,0},{24,8},{1,17},{9,25},{17,1},{25,9},{2,18},{10... | collective-permute-start | bytes 196616 | tf_op jit(solution)/shard_map/ppermute | solution.py:290
  40.6 4.2 %collective-permute-start.11 = (bf16[256,128]{1,0:T(8,128)(2,1)S(1)}, bf16[256,128]{1,0:T(8,128)(2,1)S(1)}, u32[]{:S(2)}, u32[]{:S(2)}) collective-permute-start(bf16[256,128]{1,0:T(8,128)(2,1)S(1)} %get-tuple-element.20), channel_id=1, source_target_pairs={{0,24},{8,16},{16,8},{24,0},{1,25},{9,17},{17,9},{25,1},{2,26},{10... | collective-permute-start | bytes 196616 | tf_op jit(solution)/shard_map/ppermute | solution.py:290
  40.6 4.2 %copy-start.1 = (f32[512]{0:T(512)S(1)}, f32[512]{0:T(512)}, u32[]{:S(2)}) copy-start(f32[512]{0:T(512)} %param.8) | copy-start | bytes 6148
  40.6 4.2 %collective-permute-start.9 = (bf16[256,128]{1,0:T(8,128)(2,1)S(1)}, bf16[256,128]{1,0:T(8,128)(2,1)S(1)}, u32[]{:S(2)}, u32[]{:S(2)}) collective-permute-start(bf16[256,128]{1,0:T(8,128)(2,1)S(1)} %get-tuple-element.18), channel_id=1, source_target_pairs={{0,8},{8,0},{16,24},{24,16},{1,9},{9,1},{17,25},{25,17},{2,10},{10... | collective-permute-start | bytes 196616 | tf_op jit(solution)/shard_map/ppermute | solution.py:290

commit v6 on v5

--- a/solution.py
+++ b/solution.py
@@ -136,8 +136,8 @@
             preferred_element_type=jnp.float32,
         )
 
-    def add_block(g, convert, unroll, start):
-        def fill_tile(part, i, carry):
+    def fill_part(g, part, convert, unroll):
+        def fill_tile(i, carry):
             block = count_block(g, edge_refs[part], i // tiles, i % tiles)
             top = (part * rows * tiles + i) * TILE
             top = top if unroll else pl.multiple_of(top, TILE)
@@ -147,29 +147,44 @@
                 )
             return carry
 
-        put_scaled(g)
+        if unroll:
+            for i in range(rows * tiles):
+                fill_tile(i, 0)
+        else:
+            lax.fori_loop(0, rows * tiles, fill_tile, 0)
+
+    def add_part(g, part, start):
+        at = slice(part * (sums // 2), (part + 1) * (sums // 2))
+        added = jnp.dot(counts[g % 2, at, :], scaled[g % 2], preferred_element_type=jnp.float32)
+        total[at, :] = added if start else total[at, :] + added
+
+    def rounded(block):
+        return block.astype(jnp.bfloat16)
+
+    def remainder(block):
+        return (block - block.astype(jnp.bfloat16).astype(jnp.float32)).astype(jnp.bfloat16)
+
+    scaled[...] = jnp.ones_like(scaled)
+    unroll = rows * tiles <= 4
+    for part in range(2):
+        fill_part(0, part, rounded, unroll)
+    put_scaled(0)
+    for g in range(len(groups)):
+        more = g + 1 < len(groups)
         for part in range(2):
-            if unroll:
-                for i in range(rows * tiles):
-                    fill_tile(part, i, 0)
-            else:
-                lax.fori_loop(0, rows * tiles, functools.partial(fill_tile, part), 0)
-        added = jnp.dot(counts[g % 2], scaled[g % 2], preferred_element_type=jnp.float32)
-        total[...] = added if start else total[...] + added
-
-    scaled[...] = jnp.ones_like(scaled)
-    for g in range(len(groups)):
-        add_block(g, lambda block: block.astype(jnp.bfloat16), rows * tiles <= 4, g == 0)
+            if more:
+                fill_part(g + 1, part, rounded, unroll)
+            add_part(g, part, g == 0)
+        if more:
+            put_scaled(g + 1)
 
     @pl.when(jnp.max(total[:, LANES:]) >= 256.0)
     def _():
         for g in range(len(groups)):
-            add_block(
-                g,
-                lambda block: (block - block.astype(jnp.bfloat16).astype(jnp.float32)).astype(jnp.bfloat16),
-                False,
-                False,
-            )
+            put_scaled(g)
+            for part in range(2):
+                fill_part(g, part, remainder, False)
+                add_part(g, part, False)
 
     if last:
         for shift in range(rows):

time: 46.4 us -> 46 us (level)
  Pallas kernels: 16.5 us -> 15.7 us
    pallas_call x3, Pallas kernels: 13.4 us -> 12.6 us  [add_blocks(): pl.pallas_call(functools.partial(sum_kernel, cols, shifts, groups, first,...]
  transfers between devices with their start and end apart: 13 -> 13, of which waited for: 5 -> 5; matrix products, arithmetic and copies ran while one was open for 0% -> 0% of each run, Pallas kernels for 29% -> 27%
where the time goes in v6:
time: 46 us; the launch traced here: 45.8 us
  starting transfers between devices  18.7 us (41%)
  Pallas kernels  15.7 us (34%)
  waiting for transfers between devices  11.1 us (24%)
    pallas_call x3, Pallas kernels, add_blocks(): pl.pallas_call(functools.partial(sum_kernel, cols, shifts, groups, first,...  12.6 us
    ppermute x3, starting transfers between devices, body(): lax.ppermute(here, 'col', next_near)  5.9 us
    ppermute x3, starting transfers between devices, body(): lax.ppermute(there, 'col', near)  4.98 us
    all_to_all x1, waiting for transfers between devices, body(): lax.all_to_all(packed.reshape(rows * cols, depth, LANES), ('row', 'col'),...  4.43 us
    all_to_all x1, starting transfers between devices, body(): lax.all_to_all(packed.reshape(rows * cols, depth, LANES), ('row', 'col'),...  3.82 us
    ppermute x3, waiting for transfers between devices, body(): lax.ppermute(normed[shift], 'row', [(r, r ^ shift) for r in range(rows)])  3.53 us
    ppermute x3, waiting for transfers between devices, body(): lax.ppermute(there, 'col', near)  2.74 us
    ppermute x3, starting transfers between devices, body(): lax.ppermute(normed[shift], 'row', [(r, r ^ shift) for r in range(rows)])  2.21 us
  transfers between devices with their start and end apart: 13, of which 5 were waited for; matrix products, arithmetic and copies ran while one was open for 0% of the time, Pallas kernels for 27%

profile of v6, /device:TPU:0, one launch (start us, length us, event | category | flops | bytes accessed | tf_op | source)
XLA Modules:
  0.0 45.8 jit_solution(1309900388713234339)
XLA Ops:
  0.0 0.0 copy-start.2
  0.0 3.0 %collective-permute-start.1 = (bf16[1024,128]{1,0:T(8,128)(2,1)}, bf16[1024,128]{1,0:T(8,128)(2,1)S(1)}, u32[]{:S(2)}, u32[]{:S(2)}) collective-permute-start(bf16[1024,128]{1,0:T(8,128)(2,1)} %refs_3_.1), channel_id=1, source_target_pairs={{0,1},{2,4},{4,2},{6,7},{7,6},{5,3},{3,5},{1,0},{8,9},{10,12},{12,... | collective-permute-start | bytes 786440 | tf_op jit(solution)/shard_map/ppermute | solution.py:295
  3.0 1.6 %collective-permute-start.5 = (bf16[1024,128]{1,0:T(8,128)(2,1)}, bf16[1024,128]{1,0:T(8,128)(2,1)S(1)}, u32[]{:S(2)}, u32[]{:S(2)}) collective-permute-start(bf16[1024,128]{1,0:T(8,128)(2,1)} %refs_3_.1), channel_id=1, source_target_pairs={{0,2},{2,0},{4,6},{6,4},{7,5},{5,7},{3,1},{1,3},{8,10},{10,8},{12,... | collective-permute-start | bytes 786440 | tf_op jit(solution)/shard_map/ppermute | solution.py:295
  4.6 1.9 %shard_map.64 = s32[4,8,8,128]{3,2,1,0:T(8,128)} custom-call(s32[16,512]{1,0:T(8,128)} %src_ref.1, s32[16,512]{1,0:T(8,128)} %dst_ref.1, s32[16]{0:T(128)} %bitcast.15), custom_call_target="tpu_custom_call" | custom-call | tf_op jit(solution)/shard_map/pallas_call | solution.py:241
  6.5 3.8 %all-to-all-start = ((s32[32,8,128]{2,1,0:T(8,128)}), s32[32,8,128]{2,1,0:T(8,128)S(1)}, u32[]{:S(2)}, u32[]{:S(2)}) async-start(s32[32,8,128]{2,1,0:T(8,128)} %bitcast.14), calls=%async_computation | async-start | bytes 262144 | tf_op jit(solution)/shard_map/all_to_all | solution.py:247
  10.3 0.0 collective-permute-done.1.refs_5_
  10.3 1.8 %collective-permute-start.2 = (bf16[1024,128]{1,0:T(8,128)(2,1)S(1)}, bf16[1024,128]{1,0:T(8,128)(2,1)S(1)}, u32[]{:S(2)}, u32[]{:S(2)}) collective-permute-start(bf16[1024,128]{1,0:T(8,128)(2,1)S(1)} %collective-permute-done.1.refs_5_), channel_id=1, source_target_pairs={{0,2},{2,0},{4,6},{6,4},{7,5},{5,7},{3,1},{1,3},{8,10},{10,8},{12,... | collective-permute-start | bytes 786440 | tf_op jit(solution)/shard_map/ppermute | solution.py:295
  12.2 0.0 collective-permute-done.5.refs_4_
  12.2 1.5 %collective-permute-start.6 = (bf16[1024,128]{1,0:T(8,128)(2,1)S(1)}, bf16[1024,128]{1,0:T(8,128)(2,1)S(1)}, u32[]{:S(2)}, u32[]{:S(2)}) collective-permute-start(bf16[1024,128]{1,0:T(8,128)(2,1)S(1)} %collective-permute-done.5.refs_4_), channel_id=1, source_target_pairs={{0,1},{2,4},{4,2},{6,7},{7,6},{5,3},{3,5},{1,0},{8,9},{10,12},{12,... | collective-permute-start | bytes 786440 | tf_op jit(solution)/shard_map/ppermute | solution.py:295
  13.6 4.4 %all-to-all-done = s32[32,8,128]{2,1,0:T(8,128)S(1)} async-done(((s32[32,8,128]{2,1,0:T(8,128)}), s32[32,8,128]{2,1,0:T(8,128)S(1)}, u32[]{:S(2)}, u32[]{:S(2)}) %all-to-all-start) | async-done | bytes 131104 | tf_op jit(solution)/shard_map/all_to_all | solution.py:247
  18.1 0.1 collective-permute-start
  18.2 2.7 %collective-permute-done.2.refs_6_ = bf16[1024,128]{1,0:T(8,128)(2,1)S(1)} collective-permute-done((bf16[1024,128]{1,0:T(8,128)(2,1)S(1)}, bf16[1024,128]{1,0:T(8,128)(2,1)S(1)}, u32[]{:S(2)}, u32[]{:S(2)}) %collective-permute-start.2) | collective-permute-done | bytes 262176 | tf_op jit(solution)/shard_map/ppermute | solution.py:295
  20.9 1.5 %collective-permute-start.3 = (bf16[1024,128]{1,0:T(8,128)(2,1)S(1)}, bf16[1024,128]{1,0:T(8,128)(2,1)S(1)}, u32[]{:S(2)}, u32[]{:S(2)}) collective-permute-start(bf16[1024,128]{1,0:T(8,128)(2,1)S(1)} %collective-permute-done.2.refs_6_), channel_id=1, source_target_pairs={{0,1},{2,4},{4,2},{6,7},{7,6},{5,3},{3,5},{1,0},{8,9},{10,12},{12,... | collective-permute-start | bytes 786440 | tf_op jit(solution)/shard_map/ppermute | solution.py:295
  22.4 0.0 collective-permute-done.6.refs_7_
  22.4 1.5 %collective-permute-start.7 = (bf16[1024,128]{1,0:T(8,128)(2,1)S(1)}, bf16[1024,128]{1,0:T(8,128)(2,1)S(1)}, u32[]{:S(2)}, u32[]{:S(2)}) collective-permute-start(bf16[1024,128]{1,0:T(8,128)(2,1)S(1)} %collective-permute-done.6.refs_7_), channel_id=1, source_target_pairs={{0,2},{2,0},{4,6},{6,4},{7,5},{5,7},{3,1},{1,3},{8,10},{10,8},{12,... | collective-permute-start | bytes 786440 | tf_op jit(solution)/shard_map/ppermute | solution.py:295
  23.9 0.0 collective-permute-done
  23.9 0.0 copy-done.2
  23.9 7.1 %shard_map.65 = (f32[1024,128]{1,0:T(8,128)S(1)}, f32[8,128]{1,0:T(8,128)S(1)}) custom-call(s32[1]{0:T(128)} %bitcast.1.col_ref, s32[1]{0:T(128)} %bitcast.refs_0_.row_ref, s32[4,8,8,128]{3,2,1,0:T(8,128)S(1)} %bitcast.7, s32[4,8,8,128]{3,2,1,0:T(8,128)S(1)} %bitcast.11, bf16[1024,128]{1,0:T(8,128)(2,1)S(1)} %copy-done.2, ...), custom_call_target="tpu_custom_call" | custom-call | flops 16106127360 | bytes 4194304 | tf_op jit(solution)/shard_map/pallas_call | solution.py:281
  31.0 0.0 collective-permute-done.3.refs_4_
  31.0 0.6 %collective-permute-start.4 = (bf16[512,128]{1,0:T(8,128)(2,1)S(1)}, bf16[512,128]{1,0:T(8,128)(2,1)S(1)}, u32[]{:S(2)}, u32[]{:S(2)}) collective-permute-start(bf16[512,128]{1,0:T(8,128)(2,1)S(1)} %slice.8), channel_id=1, source_target_pairs={{0,2},{2,0},{4,6},{6,4},{7,5},{5,7},{3,1},{1,3},{8,10},{10,8},{12,... | collective-permute-start | bytes 393224 | tf_op jit(solution)/shard_map/ppermute | solution.py:300
  31.6 0.0 collective-permute-done.7.refs_3_
  31.6 1.1 %collective-permute-start.8 = (bf16[512,128]{1,0:T(8,128)(2,1)S(1)}, bf16[512,128]{1,0:T(8,128)(2,1)S(1)}, u32[]{:S(2)}, u32[]{:S(2)}) collective-permute-start(bf16[512,128]{1,0:T(8,128)(2,1)S(1)} %slice.9), channel_id=1, source_target_pairs={{0,1},{2,4},{4,2},{6,7},{7,6},{5,3},{3,5},{1,0},{8,9},{10,12},{12,... | collective-permute-start | bytes 393224 | tf_op jit(solution)/shard_map/ppermute | solution.py:301
  32.7 3.5 %shard_map.66 = (f32[1024,128]{1,0:T(8,128)S(1)}, f32[8,128]{1,0:T(8,128)S(1)}) custom-call(s32[1]{0:T(128)} %bitcast.1.col_ref, s32[1]{0:T(128)} %bitcast.refs_0_.row_ref, s32[4,8,8,128]{3,2,1,0:T(8,128)S(1)} %bitcast.8, s32[4,8,8,128]{3,2,1,0:T(8,128)S(1)} %bitcast.12, bf16[1024,128]{1,0:T(8,128)(2,1)S(1)} %collective-permute-done.7.refs_3_, ...), custom_call_target="tpu_custom_call" | custom-call | flops 6442450944 | bytes 4194304 | tf_op jit(solution)/shard_map/pallas_call | solution.py:281
  36.2 0.0 collective-permute-done.4.refs_3_
  36.3 0.4 collective-permute-done.8.refs_4_
  36.7 0.0 copy-start
  36.7 2.0 %shard_map.67 = (bf16[256,128]{1,0:T(8,128)(2,1)S(1)}, bf16[256,128]{1,0:T(8,128)(2,1)S(1)}, bf16[256,128]{1,0:T(8,128)(2,1)S(1)}, bf16[256,128]{1,0:T(8,128)(2,1)S(1)}) custom-call(s32[1]{0:T(128)} %bitcast.1.col_ref, s32[1]{0:T(128)} %bitcast.refs_0_.row_ref, s32[4,8,8,128]{3,2,1,0:T(8,128)S(1)} %bitcast.9, s32[4,8,8,128]{3,2,1,0:T(8,128)S(1)} %bitcast.13, ...), custom_call_target="tpu_custom_call" | custom-call | flops 1610612736 | bytes 4194304 | tf_op jit(solution)/shard_map/pallas_call | solution.py:281
  38.6 1.5 %collective-permute-start.10 = (bf16[256,128]{1,0:T(8,128)(2,1)S(1)}, bf16[256,128]{1,0:T(8,128)(2,1)S(1)}, u32[]{:S(2)}, u32[]{:S(2)}) collective-permute-start(bf16[256,128]{1,0:T(8,128)(2,1)S(1)} %get-tuple-element.19), channel_id=1, source_target_pairs={{0,16},{8,24},{16,0},{24,8},{1,17},{9,25},{17,1},{25,9},{2,18},{10... | collective-permute-start | bytes 196616 | tf_op jit(solution)/shard_map/ppermute | solution.py:305
  40.2 0.0 collective-permute-start.11
  40.2 0.0 copy-start.1
  40.2 0.7 %collective-permute-start.9 = (bf16[256,128]{1,0:T(8,128)(2,1)S(1)}, bf16[256,128]{1,0:T(8,128)(2,1)S(1)}, u32[]{:S(2)}, u32[]{:S(2)}) collective-permute-start(bf16[256,128]{1,0:T(8,128)(2,1)S(1)} %get-tuple-element.18), channel_id=1, source_target_pairs={{0,8},{8,0},{16,24},{24,16},{1,9},{9,1},{17,25},{25,17},{2,10},{10... | collective-permute-start | bytes 196616 | tf_op jit(solution)/shard_map/ppermute | solution.py:305
  40.9 2.1 %collective-permute-done.10.refs_2_ = bf16[256,128]{1,0:T(8,128)(2,1)S(1)} collective-permute-done((bf16[256,128]{1,0:T(8,128)(2,1)S(1)}, bf16[256,128]{1,0:T(8,128)(2,1)S(1)}, u32[]{:S(2)}, u32[]{:S(2)}) %collective-permute-start.10) | collective-permute-done | bytes 65568 | tf_op jit(solution)/shard_map/ppermute | solution.py:305
  43.0 1.4 %collective-permute-done.11.refs_3_ = bf16[256,128]{1,0:T(8,128)(2,1)S(1)} collective-permute-done((bf16[256,128]{1,0:T(8,128)(2,1)S(1)}, bf16[256,128]{1,0:T(8,128)(2,1)S(1)}, u32[]{:S(2)}, u32[]{:S(2)}) %collective-permute-start.11) | collective-permute-done | bytes 65568 | tf_op jit(solution)/shard_map/ppermute | solution.py:305
  44.4 0.0 collective-permute-done.9.refs_1_
  44.4 0.0 copy-done
  44.4 0.0 copy-done.1
  44.4 1.2 %shard_map.68 = bf16[256,512]{1,0:T(8,128)(2,1)} custom-call(s32[1]{0:T(128)} %bitcast.refs_0_.row_ref, bf16[256,128]{1,0:T(8,128)(2,1)S(1)} %get-tuple-element.17.refs_0_, bf16[256,128]{1,0:T(8,128)(2,1)S(1)} %collective-permute-done.9.refs_1_, bf16[256,128]{1,0:T(8,128)(2,1)S(1)} %collective-permute-done.10.refs_2_, ...), custom_call_target="tpu_custom_call" | custom-call | tf_op jit(solution)/shard_map/pallas_call | solution.py:309
  (2 shorter events, 0.0 us)
Async XLA Ops:
  0.0 23.9 %copy-start.2 = (bf16[1024,128]{1,0:T(8,128)(2,1)S(1)}, bf16[1024,128]{1,0:T(8,128)(2,1)}, u32[]{:S(2)}) copy-start(bf16[1024,128]{1,0:T(8,128)(2,1)} %refs_3_.1) | copy-start | bytes 786436
  0.0 10.3 %collective-permute-start.1 = (bf16[1024,128]{1,0:T(8,128)(2,1)}, bf16[1024,128]{1,0:T(8,128)(2,1)S(1)}, u32[]{:S(2)}, u32[]{:S(2)}) collective-permute-start(bf16[1024,128]{1,0:T(8,128)(2,1)} %refs_3_.1), channel_id=1, source_target_pairs={{0,1},{2,4},{4,2},{6,7},{7,6},{5,3},{3,5},{1,0},{8,9},{10,12},{12,... | collective-permute-start | bytes 786440 | tf_op jit(solution)/shard_map/ppermute | solution.py:295
  3.0 9.2 %collective-permute-start.5 = (bf16[1024,128]{1,0:T(8,128)(2,1)}, bf16[1024,128]{1,0:T(8,128)(2,1)S(1)}, u32[]{:S(2)}, u32[]{:S(2)}) collective-permute-start(bf16[1024,128]{1,0:T(8,128)(2,1)} %refs_3_.1), channel_id=1, source_target_pairs={{0,2},{2,0},{4,6},{6,4},{7,5},{5,7},{3,1},{1,3},{8,10},{10,8},{12,... | collective-permute-start | bytes 786440 | tf_op jit(solution)/shard_map/ppermute | solution.py:295
  6.5 11.6 %all-to-all-start = ((s32[32,8,128]{2,1,0:T(8,128)}), s32[32,8,128]{2,1,0:T(8,128)S(1)}, u32[]{:S(2)}, u32[]{:S(2)}) async-start(s32[32,8,128]{2,1,0:T(8,128)} %bitcast.14), calls=%async_computation | async-start | bytes 262144 | tf_op jit(solution)/shard_map/all_to_all | solution.py:247
  10.3 10.6 %collective-permute-start.2 = (bf16[1024,128]{1,0:T(8,128)(2,1)S(1)}, bf16[1024,128]{1,0:T(8,128)(2,1)S(1)}, u32[]{:S(2)}, u32[]{:S(2)}) collective-permute-start(bf16[1024,128]{1,0:T(8,128)(2,1)S(1)} %collective-permute-done.1.refs_5_), channel_id=1, source_target_pairs={{0,2},{2,0},{4,6},{6,4},{7,5},{5,7},{3,1},{1,3},{8,10},{10,8},{12,... | collective-permute-start | bytes 786440 | tf_op jit(solution)/shard_map/ppermute | solution.py:295
  12.2 10.2 %collective-permute-start.6 = (bf16[1024,128]{1,0:T(8,128)(2,1)S(1)}, bf16[1024,128]{1,0:T(8,128)(2,1)S(1)}, u32[]{:S(2)}, u32[]{:S(2)}) collective-permute-start(bf16[1024,128]{1,0:T(8,128)(2,1)S(1)} %collective-permute-done.5.refs_4_), channel_id=1, source_target_pairs={{0,1},{2,4},{4,2},{6,7},{7,6},{5,3},{3,5},{1,0},{8,9},{10,12},{12,... | collective-permute-start | bytes 786440 | tf_op jit(solution)/shard_map/ppermute | solution.py:295
  18.1 5.8 %collective-permute-start = (s32[32,8,128]{2,1,0:T(8,128)S(1)}, s32[32,8,128]{2,1,0:T(8,128)S(1)}, u32[]{:S(2)}, u32[]{:S(2)}) collective-permute-start(s32[32,8,128]{2,1,0:T(8,128)S(1)} %all-to-all-done), channel_id=1, source_target_pairs={{0,8},{8,0},{16,24},{24,16},{1,9},{9,1},{17,25},{25,17},{2,10},{10... | collective-permute-start | bytes 393224 | tf_op jit(solution)/shard_map/ppermute | solution.py:254
  20.9 10.1 %collective-permute-start.3 = (bf16[1024,128]{1,0:T(8,128)(2,1)S(1)}, bf16[1024,128]{1,0:T(8,128)(2,1)S(1)}, u32[]{:S(2)}, u32[]{:S(2)}) collective-permute-start(bf16[1024,128]{1,0:T(8,128)(2,1)S(1)} %collective-permute-done.2.refs_6_), channel_id=1, source_target_pairs={{0,1},{2,4},{4,2},{6,7},{7,6},{5,3},{3,5},{1,0},{8,9},{10,12},{12,... | collective-permute-start | bytes 786440 | tf_op jit(solution)/shard_map/ppermute | solution.py:295
  22.4 9.2 %collective-permute-start.7 = (bf16[1024,128]{1,0:T(8,128)(2,1)S(1)}, bf16[1024,128]{1,0:T(8,128)(2,1)S(1)}, u32[]{:S(2)}, u32[]{:S(2)}) collective-permute-start(bf16[1024,128]{1,0:T(8,128)(2,1)S(1)} %collective-permute-done.6.refs_7_), channel_id=1, source_target_pairs={{0,2},{2,0},{4,6},{6,4},{7,5},{5,7},{3,1},{1,3},{8,10},{10,8},{12,... | collective-permute-start | bytes 786440 | tf_op jit(solution)/shard_map/ppermute | solution.py:295
  31.0 5.2 %collective-permute-start.4 = (bf16[512,128]{1,0:T(8,128)(2,1)S(1)}, bf16[512,128]{1,0:T(8,128)(2,1)S(1)}, u32[]{:S(2)}, u32[]{:S(2)}) collective-permute-start(bf16[512,128]{1,0:T(8,128)(2,1)S(1)} %slice.8), channel_id=1, source_target_pairs={{0,2},{2,0},{4,6},{6,4},{7,5},{5,7},{3,1},{1,3},{8,10},{10,8},{12,... | collective-permute-start | bytes 393224 | tf_op jit(solution)/shard_map/ppermute | solution.py:300
  31.6 5.0 %collective-permute-start.8 = (bf16[512,128]{1,0:T(8,128)(2,1)S(1)}, bf16[512,128]{1,0:T(8,128)(2,1)S(1)}, u32[]{:S(2)}, u32[]{:S(2)}) collective-permute-start(bf16[512,128]{1,0:T(8,128)(2,1)S(1)} %slice.9), channel_id=1, source_target_pairs={{0,1},{2,4},{4,2},{6,7},{7,6},{5,3},{3,5},{1,0},{8,9},{10,12},{12,... | collective-permute-start | bytes 393224 | tf_op jit(solution)/shard_map/ppermute | solution.py:301
  36.7 7.7 %copy-start = (bf16[512,512]{1,0:T(8,128)(2,1)S(1)}, bf16[512,512]{1,0:T(8,128)(2,1)}, u32[]{:S(2)}) copy-start(bf16[512,512]{1,0:T(8,128)(2,1)} %refs_4_.1) | copy-start | bytes 1572868
  38.6 4.3 %collective-permute-start.10 = (bf16[256,128]{1,0:T(8,128)(2,1)S(1)}, bf16[256,128]{1,0:T(8,128)(2,1)S(1)}, u32[]{:S(2)}, u32[]{:S(2)}) collective-permute-start(bf16[256,128]{1,0:T(8,128)(2,1)S(1)} %get-tuple-element.19), channel_id=1, source_target_pairs={{0,16},{8,24},{16,0},{24,8},{1,17},{9,25},{17,1},{25,9},{2,18},{10... | collective-permute-start | bytes 196616 | tf_op jit(solution)/shard_map/ppermute | solution.py:305
  40.2 4.2 %collective-permute-start.11 = (bf16[256,128]{1,0:T(8,128)(2,1)S(1)}, bf16[256,128]{1,0:T(8,128)(2,1)S(1)}, u32[]{:S(2)}, u32[]{:S(2)}) collective-permute-start(bf16[256,128]{1,0:T(8,128)(2,1)S(1)} %get-tuple-element.20), channel_id=1, source_target_pairs={{0,24},{8,16},{16,8},{24,0},{1,25},{9,17},{17,9},{25,1},{2,26},{10... | collective-permute-start | bytes 196616 | tf_op jit(solution)/shard_map/ppermute | solution.py:305
  40.2 4.2 %copy-start.1 = (f32[512]{0:T(512)S(1)}, f32[512]{0:T(512)}, u32[]{:S(2)}) copy-start(f32[512]{0:T(512)} %param.8) | copy-start | bytes 6148
  40.2 4.2 %collective-permute-start.9 = (bf16[256,128]{1,0:T(8,128)(2,1)S(1)}, bf16[256,128]{1,0:T(8,128)(2,1)S(1)}, u32[]{:S(2)}, u32[]{:S(2)}) collective-permute-start(bf16[256,128]{1,0:T(8,128)(2,1)S(1)} %get-tuple-element.18), channel_id=1, source_target_pairs={{0,8},{8,0},{16,24},{24,16},{1,9},{9,1},{17,25},{25,17},{2,10},{10... | collective-permute-start | bytes 196616 | tf_op jit(solution)/shard_map/ppermute | solution.py:305

commit v7 on v6

--- a/solution.py
+++ b/solution.py
@@ -174,9 +174,9 @@
         for part in range(2):
             if more:
                 fill_part(g + 1, part, rounded, unroll)
+            if more and part:
+                put_scaled(g + 1)
             add_part(g, part, g == 0)
-        if more:
-            put_scaled(g + 1)
 
     @pl.when(jnp.max(total[:, LANES:]) >= 256.0)
     def _():

time: 46 us -> 46 us (level)
  no operation moved by 1% of the time
where the time goes in v7:
time: 46 us; the launch traced here: 45.8 us
  starting transfers between devices  18.7 us (41%)
  Pallas kernels  15.7 us (34%)
  waiting for transfers between devices  11.1 us (24%)
    pallas_call x3, Pallas kernels, add_blocks(): pl.pallas_call(functools.partial(sum_kernel, cols, shifts, groups, first,...  12.6 us
    ppermute x3, starting transfers between devices, body(): lax.ppermute(here, 'col', next_near)  5.9 us
    ppermute x3, starting transfers between devices, body(): lax.ppermute(there, 'col', near)  4.98 us
    all_to_all x1, waiting for transfers between devices, body(): lax.all_to_all(packed.reshape(rows * cols, depth, LANES), ('row', 'col'),...  4.43 us
    all_to_all x1, starting transfers between devices, body(): lax.all_to_all(packed.reshape(rows * cols, depth, LANES), ('row', 'col'),...  3.82 us
    ppermute x3, waiting for transfers between devices, body(): lax.ppermute(normed[shift], 'row', [(r, r ^ shift) for r in range(rows)])  3.53 us
    ppermute x3, waiting for transfers between devices, body(): lax.ppermute(there, 'col', near)  2.74 us
    ppermute x3, starting transfers between devices, body(): lax.ppermute(normed[shift], 'row', [(r, r ^ shift) for r in range(rows)])  2.21 us
  transfers between devices with their start and end apart: 13, of which 5 were waited for; matrix products, arithmetic and copies ran while one was open for 0% of the time, Pallas kernels for 27%

profile of v7, /device:TPU:0, one launch (start us, length us, event | category | flops | bytes accessed | tf_op | source)
XLA Modules:
  0.0 45.8 jit_solution(1309900388713234339)
XLA Ops:
  0.0 0.0 copy-start.2
  0.0 3.0 %collective-permute-start.1 = (bf16[1024,128]{1,0:T(8,128)(2,1)}, bf16[1024,128]{1,0:T(8,128)(2,1)S(1)}, u32[]{:S(2)}, u32[]{:S(2)}) collective-permute-start(bf16[1024,128]{1,0:T(8,128)(2,1)} %refs_3_.1), channel_id=1, source_target_pairs={{0,1},{2,4},{4,2},{6,7},{7,6},{5,3},{3,5},{1,0},{8,9},{10,12},{12,... | collective-permute-start | bytes 786440 | tf_op jit(solution)/shard_map/ppermute | solution.py:295
  3.0 1.6 %collective-permute-start.5 = (bf16[1024,128]{1,0:T(8,128)(2,1)}, bf16[1024,128]{1,0:T(8,128)(2,1)S(1)}, u32[]{:S(2)}, u32[]{:S(2)}) collective-permute-start(bf16[1024,128]{1,0:T(8,128)(2,1)} %refs_3_.1), channel_id=1, source_target_pairs={{0,2},{2,0},{4,6},{6,4},{7,5},{5,7},{3,1},{1,3},{8,10},{10,8},{12,... | collective-permute-start | bytes 786440 | tf_op jit(solution)/shard_map/ppermute | solution.py:295
  4.6 1.9 %shard_map.64 = s32[4,8,8,128]{3,2,1,0:T(8,128)} custom-call(s32[16,512]{1,0:T(8,128)} %src_ref.1, s32[16,512]{1,0:T(8,128)} %dst_ref.1, s32[16]{0:T(128)} %bitcast.15), custom_call_target="tpu_custom_call" | custom-call | tf_op jit(solution)/shard_map/pallas_call | solution.py:241
  6.5 3.8 %all-to-all-start = ((s32[32,8,128]{2,1,0:T(8,128)}), s32[32,8,128]{2,1,0:T(8,128)S(1)}, u32[]{:S(2)}, u32[]{:S(2)}) async-start(s32[32,8,128]{2,1,0:T(8,128)} %bitcast.14), calls=%async_computation | async-start | bytes 262144 | tf_op jit(solution)/shard_map/all_to_all | solution.py:247
  10.3 0.0 collective-permute-done.1.refs_5_
  10.3 1.8 %collective-permute-start.2 = (bf16[1024,128]{1,0:T(8,128)(2,1)S(1)}, bf16[1024,128]{1,0:T(8,128)(2,1)S(1)}, u32[]{:S(2)}, u32[]{:S(2)}) collective-permute-start(bf16[1024,128]{1,0:T(8,128)(2,1)S(1)} %collective-permute-done.1.refs_5_), channel_id=1, source_target_pairs={{0,2},{2,0},{4,6},{6,4},{7,5},{5,7},{3,1},{1,3},{8,10},{10,8},{12,... | collective-permute-start | bytes 786440 | tf_op jit(solution)/shard_map/ppermute | solution.py:295
  12.2 0.0 collective-permute-done.5.refs_4_
  12.2 1.5 %collective-permute-start.6 = (bf16[1024,128]{1,0:T(8,128)(2,1)S(1)}, bf16[1024,128]{1,0:T(8,128)(2,1)S(1)}, u32[]{:S(2)}, u32[]{:S(2)}) collective-permute-start(bf16[1024,128]{1,0:T(8,128)(2,1)S(1)} %collective-permute-done.5.refs_4_), channel_id=1, source_target_pairs={{0,1},{2,4},{4,2},{6,7},{7,6},{5,3},{3,5},{1,0},{8,9},{10,12},{12,... | collective-permute-start | bytes 786440 | tf_op jit(solution)/shard_map/ppermute | solution.py:295
  13.6 4.4 %all-to-all-done = s32[32,8,128]{2,1,0:T(8,128)S(1)} async-done(((s32[32,8,128]{2,1,0:T(8,128)}), s32[32,8,128]{2,1,0:T(8,128)S(1)}, u32[]{:S(2)}, u32[]{:S(2)}) %all-to-all-start) | async-done | bytes 131104 | tf_op jit(solution)/shard_map/all_to_all | solution.py:247
  18.1 0.1 collective-permute-start
  18.2 2.7 %collective-permute-done.2.refs_6_ = bf16[1024,128]{1,0:T(8,128)(2,1)S(1)} collective-permute-done((bf16[1024,128]{1,0:T(8,128)(2,1)S(1)}, bf16[1024,128]{1,0:T(8,128)(2,1)S(1)}, u32[]{:S(2)}, u32[]{:S(2)}) %collective-permute-start.2) | collective-permute-done | bytes 262176 | tf_op jit(solution)/shard_map/ppermute | solution.py:295
  20.9 1.5 %collective-permute-start.3 = (bf16[1024,128]{1,0:T(8,128)(2,1)S(1)}, bf16[1024,128]{1,0:T(8,128)(2,1)S(1)}, u32[]{:S(2)}, u32[]{:S(2)}) collective-permute-start(bf16[1024,128]{1,0:T(8,128)(2,1)S(1)} %collective-permute-done.2.refs_6_), channel_id=1, source_target_pairs={{0,1},{2,4},{4,2},{6,7},{7,6},{5,3},{3,5},{1,0},{8,9},{10,12},{12,... | collective-permute-start | bytes 786440 | tf_op jit(solution)/shard_map/ppermute | solution.py:295
  22.4 0.0 collective-permute-done.6.refs_7_
  22.4 1.5 %collective-permute-start.7 = (bf16[1024,128]{1,0:T(8,128)(2,1)S(1)}, bf16[1024,128]{1,0:T(8,128)(2,1)S(1)}, u32[]{:S(2)}, u32[]{:S(2)}) collective-permute-start(bf16[1024,128]{1,0:T(8,128)(2,1)S(1)} %collective-permute-done.6.refs_7_), channel_id=1, source_target_pairs={{0,2},{2,0},{4,6},{6,4},{7,5},{5,7},{3,1},{1,3},{8,10},{10,8},{12,... | collective-permute-start | bytes 786440 | tf_op jit(solution)/shard_map/ppermute | solution.py:295
  23.9 0.0 collective-permute-done
  23.9 0.0 copy-done.2
  23.9 7.1 %shard_map.65 = (f32[1024,128]{1,0:T(8,128)S(1)}, f32[8,128]{1,0:T(8,128)S(1)}) custom-call(s32[1]{0:T(128)} %bitcast.1.col_ref, s32[1]{0:T(128)} %bitcast.refs_0_.row_ref, s32[4,8,8,128]{3,2,1,0:T(8,128)S(1)} %bitcast.7, s32[4,8,8,128]{3,2,1,0:T(8,128)S(1)} %bitcast.11, bf16[1024,128]{1,0:T(8,128)(2,1)S(1)} %copy-done.2, ...), custom_call_target="tpu_custom_call" | custom-call | flops 16106127360 | bytes 4194304 | tf_op jit(solution)/shard_map/pallas_call | solution.py:281
  31.0 0.0 collective-permute-done.3.refs_4_
  31.0 0.6 %collective-permute-start.4 = (bf16[512,128]{1,0:T(8,128)(2,1)S(1)}, bf16[512,128]{1,0:T(8,128)(2,1)S(1)}, u32[]{:S(2)}, u32[]{:S(2)}) collective-permute-start(bf16[512,128]{1,0:T(8,128)(2,1)S(1)} %slice.8), channel_id=1, source_target_pairs={{0,2},{2,0},{4,6},{6,4},{7,5},{5,7},{3,1},{1,3},{8,10},{10,8},{12,... | collective-permute-start | bytes 393224 | tf_op jit(solution)/shard_map/ppermute | solution.py:300
  31.6 0.0 collective-permute-done.7.refs_3_
  31.6 1.1 %collective-permute-start.8 = (bf16[512,128]{1,0:T(8,128)(2,1)S(1)}, bf16[512,128]{1,0:T(8,128)(2,1)S(1)}, u32[]{:S(2)}, u32[]{:S(2)}) collective-permute-start(bf16[512,128]{1,0:T(8,128)(2,1)S(1)} %slice.9), channel_id=1, source_target_pairs={{0,1},{2,4},{4,2},{6,7},{7,6},{5,3},{3,5},{1,0},{8,9},{10,12},{12,... | collective-permute-start | bytes 393224 | tf_op jit(solution)/shard_map/ppermute | solution.py:301
  32.7 3.5 %shard_map.66 = (f32[1024,128]{1,0:T(8,128)S(1)}, f32[8,128]{1,0:T(8,128)S(1)}) custom-call(s32[1]{0:T(128)} %bitcast.1.col_ref, s32[1]{0:T(128)} %bitcast.refs_0_.row_ref, s32[4,8,8,128]{3,2,1,0:T(8,128)S(1)} %bitcast.8, s32[4,8,8,128]{3,2,1,0:T(8,128)S(1)} %bitcast.12, bf16[1024,128]{1,0:T(8,128)(2,1)S(1)} %collective-permute-done.7.refs_3_, ...), custom_call_target="tpu_custom_call" | custom-call | flops 6442450944 | bytes 4194304 | tf_op jit(solution)/shard_map/pallas_call | solution.py:281
  36.2 0.0 collective-permute-done.4.refs_3_
  36.3 0.4 collective-permute-done.8.refs_4_
  36.7 0.0 copy-start
  36.7 2.0 %shard_map.67 = (bf16[256,128]{1,0:T(8,128)(2,1)S(1)}, bf16[256,128]{1,0:T(8,128)(2,1)S(1)}, bf16[256,128]{1,0:T(8,128)(2,1)S(1)}, bf16[256,128]{1,0:T(8,128)(2,1)S(1)}) custom-call(s32[1]{0:T(128)} %bitcast.1.col_ref, s32[1]{0:T(128)} %bitcast.refs_0_.row_ref, s32[4,8,8,128]{3,2,1,0:T(8,128)S(1)} %bitcast.9, s32[4,8,8,128]{3,2,1,0:T(8,128)S(1)} %bitcast.13, ...), custom_call_target="tpu_custom_call" | custom-call | flops 1610612736 | bytes 4194304 | tf_op jit(solution)/shard_map/pallas_call | solution.py:281
  38.6 1.5 %collective-permute-start.10 = (bf16[256,128]{1,0:T(8,128)(2,1)S(1)}, bf16[256,128]{1,0:T(8,128)(2,1)S(1)}, u32[]{:S(2)}, u32[]{:S(2)}) collective-permute-start(bf16[256,128]{1,0:T(8,128)(2,1)S(1)} %get-tuple-element.19), channel_id=1, source_target_pairs={{0,16},{8,24},{16,0},{24,8},{1,17},{9,25},{17,1},{25,9},{2,18},{10... | collective-permute-start | bytes 196616 | tf_op jit(solution)/shard_map/ppermute | solution.py:305
  40.2 0.0 collective-permute-start.11
  40.2 0.0 copy-start.1
  40.2 0.7 %collective-permute-start.9 = (bf16[256,128]{1,0:T(8,128)(2,1)S(1)}, bf16[256,128]{1,0:T(8,128)(2,1)S(1)}, u32[]{:S(2)}, u32[]{:S(2)}) collective-permute-start(bf16[256,128]{1,0:T(8,128)(2,1)S(1)} %get-tuple-element.18), channel_id=1, source_target_pairs={{0,8},{8,0},{16,24},{24,16},{1,9},{9,1},{17,25},{25,17},{2,10},{10... | collective-permute-start | bytes 196616 | tf_op jit(solution)/shard_map/ppermute | solution.py:305
  40.9 2.1 %collective-permute-done.10.refs_2_ = bf16[256,128]{1,0:T(8,128)(2,1)S(1)} collective-permute-done((bf16[256,128]{1,0:T(8,128)(2,1)S(1)}, bf16[256,128]{1,0:T(8,128)(2,1)S(1)}, u32[]{:S(2)}, u32[]{:S(2)}) %collective-permute-start.10) | collective-permute-done | bytes 65568 | tf_op jit(solution)/shard_map/ppermute | solution.py:305
  43.0 1.4 %collective-permute-done.11.refs_3_ = bf16[256,128]{1,0:T(8,128)(2,1)S(1)} collective-permute-done((bf16[256,128]{1,0:T(8,128)(2,1)S(1)}, bf16[256,128]{1,0:T(8,128)(2,1)S(1)}, u32[]{:S(2)}, u32[]{:S(2)}) %collective-permute-start.11) | collective-permute-done | bytes 65568 | tf_op jit(solution)/shard_map/ppermute | solution.py:305
  44.4 0.0 collective-permute-done.9.refs_1_
  44.4 0.0 copy-done
  44.4 0.0 copy-done.1
  44.4 1.2 %shard_map.68 = bf16[256,512]{1,0:T(8,128)(2,1)} custom-call(s32[1]{0:T(128)} %bitcast.refs_0_.row_ref, bf16[256,128]{1,0:T(8,128)(2,1)S(1)} %get-tuple-element.17.refs_0_, bf16[256,128]{1,0:T(8,128)(2,1)S(1)} %collective-permute-done.9.refs_1_, bf16[256,128]{1,0:T(8,128)(2,1)S(1)} %collective-permute-done.10.refs_2_, ...), custom_call_target="tpu_custom_call" | custom-call | tf_op jit(solution)/shard_map/pallas_call | solution.py:309
  (2 shorter events, 0.0 us)
Async XLA Ops:
  0.0 23.9 %copy-start.2 = (bf16[1024,128]{1,0:T(8,128)(2,1)S(1)}, bf16[1024,128]{1,0:T(8,128)(2,1)}, u32[]{:S(2)}) copy-start(bf16[1024,128]{1,0:T(8,128)(2,1)} %refs_3_.1) | copy-start | bytes 786436
  0.0 10.3 %collective-permute-start.1 = (bf16[1024,128]{1,0:T(8,128)(2,1)}, bf16[1024,128]{1,0:T(8,128)(2,1)S(1)}, u32[]{:S(2)}, u32[]{:S(2)}) collective-permute-start(bf16[1024,128]{1,0:T(8,128)(2,1)} %refs_3_.1), channel_id=1, source_target_pairs={{0,1},{2,4},{4,2},{6,7},{7,6},{5,3},{3,5},{1,0},{8,9},{10,12},{12,... | collective-permute-start | bytes 786440 | tf_op jit(solution)/shard_map/ppermute | solution.py:295
  3.0 9.2 %collective-permute-start.5 = (bf16[1024,128]{1,0:T(8,128)(2,1)}, bf16[1024,128]{1,0:T(8,128)(2,1)S(1)}, u32[]{:S(2)}, u32[]{:S(2)}) collective-permute-start(bf16[1024,128]{1,0:T(8,128)(2,1)} %refs_3_.1), channel_id=1, source_target_pairs={{0,2},{2,0},{4,6},{6,4},{7,5},{5,7},{3,1},{1,3},{8,10},{10,8},{12,... | collective-permute-start | bytes 786440 | tf_op jit(solution)/shard_map/ppermute | solution.py:295
  6.5 11.6 %all-to-all-start = ((s32[32,8,128]{2,1,0:T(8,128)}), s32[32,8,128]{2,1,0:T(8,128)S(1)}, u32[]{:S(2)}, u32[]{:S(2)}) async-start(s32[32,8,128]{2,1,0:T(8,128)} %bitcast.14), calls=%async_computation | async-start | bytes 262144 | tf_op jit(solution)/shard_map/all_to_all | solution.py:247
  10.3 10.6 %collective-permute-start.2 = (bf16[1024,128]{1,0:T(8,128)(2,1)S(1)}, bf16[1024,128]{1,0:T(8,128)(2,1)S(1)}, u32[]{:S(2)}, u32[]{:S(2)}) collective-permute-start(bf16[1024,128]{1,0:T(8,128)(2,1)S(1)} %collective-permute-done.1.refs_5_), channel_id=1, source_target_pairs={{0,2},{2,0},{4,6},{6,4},{7,5},{5,7},{3,1},{1,3},{8,10},{10,8},{12,... | collective-permute-start | bytes 786440 | tf_op jit(solution)/shard_map/ppermute | solution.py:295
  12.2 10.2 %collective-permute-start.6 = (bf16[1024,128]{1,0:T(8,128)(2,1)S(1)}, bf16[1024,128]{1,0:T(8,128)(2,1)S(1)}, u32[]{:S(2)}, u32[]{:S(2)}) collective-permute-start(bf16[1024,128]{1,0:T(8,128)(2,1)S(1)} %collective-permute-done.5.refs_4_), channel_id=1, source_target_pairs={{0,1},{2,4},{4,2},{6,7},{7,6},{5,3},{3,5},{1,0},{8,9},{10,12},{12,... | collective-permute-start | bytes 786440 | tf_op jit(solution)/shard_map/ppermute | solution.py:295
  18.1 5.8 %collective-permute-start = (s32[32,8,128]{2,1,0:T(8,128)S(1)}, s32[32,8,128]{2,1,0:T(8,128)S(1)}, u32[]{:S(2)}, u32[]{:S(2)}) collective-permute-start(s32[32,8,128]{2,1,0:T(8,128)S(1)} %all-to-all-done), channel_id=1, source_target_pairs={{0,8},{8,0},{16,24},{24,16},{1,9},{9,1},{17,25},{25,17},{2,10},{10... | collective-permute-start | bytes 393224 | tf_op jit(solution)/shard_map/ppermute | solution.py:254
  20.9 10.1 %collective-permute-start.3 = (bf16[1024,128]{1,0:T(8,128)(2,1)S(1)}, bf16[1024,128]{1,0:T(8,128)(2,1)S(1)}, u32[]{:S(2)}, u32[]{:S(2)}) collective-permute-start(bf16[1024,128]{1,0:T(8,128)(2,1)S(1)} %collective-permute-done.2.refs_6_), channel_id=1, source_target_pairs={{0,1},{2,4},{4,2},{6,7},{7,6},{5,3},{3,5},{1,0},{8,9},{10,12},{12,... | collective-permute-start | bytes 786440 | tf_op jit(solution)/shard_map/ppermute | solution.py:295
  22.4 9.2 %collective-permute-start.7 = (bf16[1024,128]{1,0:T(8,128)(2,1)S(1)}, bf16[1024,128]{1,0:T(8,128)(2,1)S(1)}, u32[]{:S(2)}, u32[]{:S(2)}) collective-permute-start(bf16[1024,128]{1,0:T(8,128)(2,1)S(1)} %collective-permute-done.6.refs_7_), channel_id=1, source_target_pairs={{0,2},{2,0},{4,6},{6,4},{7,5},{5,7},{3,1},{1,3},{8,10},{10,8},{12,... | collective-permute-start | bytes 786440 | tf_op jit(solution)/shard_map/ppermute | solution.py:295
  31.0 5.2 %collective-permute-start.4 = (bf16[512,128]{1,0:T(8,128)(2,1)S(1)}, bf16[512,128]{1,0:T(8,128)(2,1)S(1)}, u32[]{:S(2)}, u32[]{:S(2)}) collective-permute-start(bf16[512,128]{1,0:T(8,128)(2,1)S(1)} %slice.8), channel_id=1, source_target_pairs={{0,2},{2,0},{4,6},{6,4},{7,5},{5,7},{3,1},{1,3},{8,10},{10,8},{12,... | collective-permute-start | bytes 393224 | tf_op jit(solution)/shard_map/ppermute | solution.py:300
  31.6 5.0 %collective-permute-start.8 = (bf16[512,128]{1,0:T(8,128)(2,1)S(1)}, bf16[512,128]{1,0:T(8,128)(2,1)S(1)}, u32[]{:S(2)}, u32[]{:S(2)}) collective-permute-start(bf16[512,128]{1,0:T(8,128)(2,1)S(1)} %slice.9), channel_id=1, source_target_pairs={{0,1},{2,4},{4,2},{6,7},{7,6},{5,3},{3,5},{1,0},{8,9},{10,12},{12,... | collective-permute-start | bytes 393224 | tf_op jit(solution)/shard_map/ppermute | solution.py:301
  36.7 7.7 %copy-start = (bf16[512,512]{1,0:T(8,128)(2,1)S(1)}, bf16[512,512]{1,0:T(8,128)(2,1)}, u32[]{:S(2)}) copy-start(bf16[512,512]{1,0:T(8,128)(2,1)} %refs_4_.1) | copy-start | bytes 1572868
  38.6 4.3 %collective-permute-start.10 = (bf16[256,128]{1,0:T(8,128)(2,1)S(1)}, bf16[256,128]{1,0:T(8,128)(2,1)S(1)}, u32[]{:S(2)}, u32[]{:S(2)}) collective-permute-start(bf16[256,128]{1,0:T(8,128)(2,1)S(1)} %get-tuple-element.19), channel_id=1, source_target_pairs={{0,16},{8,24},{16,0},{24,8},{1,17},{9,25},{17,1},{25,9},{2,18},{10... | collective-permute-start | bytes 196616 | tf_op jit(solution)/shard_map/ppermute | solution.py:305
  40.2 4.2 %collective-permute-start.11 = (bf16[256,128]{1,0:T(8,128)(2,1)S(1)}, bf16[256,128]{1,0:T(8,128)(2,1)S(1)}, u32[]{:S(2)}, u32[]{:S(2)}) collective-permute-start(bf16[256,128]{1,0:T(8,128)(2,1)S(1)} %get-tuple-element.20), channel_id=1, source_target_pairs={{0,24},{8,16},{16,8},{24,0},{1,25},{9,17},{17,9},{25,1},{2,26},{10... | collective-permute-start | bytes 196616 | tf_op jit(solution)/shard_map/ppermute | solution.py:305
  40.2 4.2 %copy-start.1 = (f32[512]{0:T(512)S(1)}, f32[512]{0:T(512)}, u32[]{:S(2)}) copy-start(f32[512]{0:T(512)} %param.8) | copy-start | bytes 6148
  40.2 4.2 %collective-permute-start.9 = (bf16[256,128]{1,0:T(8,128)(2,1)S(1)}, bf16[256,128]{1,0:T(8,128)(2,1)S(1)}, u32[]{:S(2)}, u32[]{:S(2)}) collective-permute-start(bf16[256,128]{1,0:T(8,128)(2,1)S(1)} %get-tuple-element.18), channel_id=1, source_target_pairs={{0,8},{8,0},{16,24},{24,16},{1,9},{9,1},{17,25},{25,17},{2,10},{10... | collective-permute-start | bytes 196616 | tf_op jit(solution)/shard_map/ppermute | solution.py:305
